TPU v7x, 512 devices: a whole 4x8x8 slice. The times are simulated.
512 devices in a mesh: dp: 64 (over z, x, y_hi), tensor: 8 (over y_lo, core).
Axes of the slice: x: 4, y: 8 (y_hi: 2, y_lo: 4; y = y_hi * 4 + y_lo), z: 8, core: 2. Of those that a mesh axis runs over, the one named last changes fastest.
Arguments:
- context: bfloat16 [32768, 2048], P('dp', 'tensor'), may hold values from -6 to 6
- residual: bfloat16 [32768, 4096], P('dp', 'tensor'), may hold values from -6 to 6
- out_weight: bfloat16 [2048, 4096], P(None, 'tensor'), may hold values from -0.125 to 0.125
- final_norm_weight: float32 [4096], P('tensor'), may hold values from 0.25 to 1.75
- query_lengths: int32 [1024], P('dp'), may hold values from 1 to 16, 8192 in all
- passage_lengths: int32 [1024], P('dp'), may hold values from 1 to 16, 8192 in all
- positive_index: int32 [1024], P('dp'), may hold values from 0 to 1023
- tile_mask: int32 [8, 8], replicated, may hold values 0 or 1
Outputs:
- query_loss: float32 [1024], P(('dp', 'tensor'))
- residual_gradient: bfloat16 [32768, 4096], P('dp', 'tensor')
- d_context: bfloat16 [32768, 2048], P('dp', 'tensor')
Inputs may be any that keep to these rules, and one draw needn't show every extreme that they name: `query_lengths`: tokens past a query's length are padding. `passage_lengths`: tokens past a passage's length are padding.
All inputs are finite; a program needn't handle non-finite values. No bound on the sum of `query_lengths` or of `passage_lengths` on one device may be relied on, other than what follows from the above.
Results may differ from a plain program's by a relative error of at most 0.023.
Values may be sent and summed in bfloat16 or wider, within the bound.
No kernel may reach another device: no remote copies, remote signals or barrier semaphores. Data moves between devices by JAX's collectives and lax.ppermute only.
A program may use at most 64 MiB of HBM per device.

v0:
```python
import jax
import jax.numpy as jnp
from jax import lax
from jax.sharding import PartitionSpec as P

Q_DEV = 16
P_DEV = 16
SEQ_LEN = 16
TILE = 128


EPS = 1e-06
LOGIT_SCALE = 20.0
LOSS_SCALE = 1024.0


def body(
    context,
    residual,
    out_weight,
    final_norm_weight,
    query_lengths,
    passage_lengths,
    positive_index,
    tile_mask,
):
    f32 = jnp.float32
    tok_rows = residual.shape[0]
    local_width = residual.shape[1]
    complete_width = local_width * lax.axis_size("tensor")
    seqs = Q_DEV + P_DEV
    rows = out_weight
    hidden_state = residual.astype(f32) + jnp.dot(
        lax.all_gather(context, "tensor", axis=1, tiled=True), rows, preferred_element_type=f32
    )
    square_sum = lax.psum(jnp.sum(hidden_state * hidden_state, axis=1), "tensor")
    inverse_deviation = lax.rsqrt(square_sum[:, None] / complete_width + EPS)
    standardized_state = hidden_state * inverse_deviation
    normalized_state = standardized_state * final_norm_weight
    lengths = jnp.concatenate([query_lengths, passage_lengths], axis=0)
    slots = jnp.arange(SEQ_LEN, dtype=jnp.int32)
    valid = (slots[None, :] < lengths[:, None]).astype(f32)
    weights = valid / lengths[:, None].astype(f32)
    pooled = jnp.einsum("st,std->sd", weights, normalized_state.reshape(seqs, SEQ_LEN, local_width))
    pooled_sq = lax.psum(jnp.sum(pooled * pooled, axis=1), "tensor")
    norms = jnp.sqrt(pooled_sq + EPS)[:, None]
    unit = pooled / norms
    q_emb = unit[:Q_DEV].astype(jnp.bfloat16)
    p_emb = unit[Q_DEV:].astype(jnp.bfloat16)
    p_all = lax.all_gather(p_emb, "dp", axis=0, tiled=True)
    partial_value = jnp.dot(q_emb, p_all.T, preferred_element_type=f32)
    logits = LOGIT_SCALE * lax.psum_scatter(
        partial_value, "tensor", scatter_dimension=0, tiled=True
    )
    share = logits.shape[0]
    passages = logits.shape[1]
    q_blocks = tile_mask.shape[0]
    p_blocks = tile_mask.shape[1]
    mask_f = tile_mask.astype(f32)
    first = lax.axis_index("tensor") * share
    own_pos = lax.dynamic_slice_in_dim(positive_index, first, share)
    query_ids = lax.axis_index("dp") * Q_DEV + first + jnp.arange(share, dtype=jnp.int32)
    q_onehot = (
        (query_ids // TILE)[:, None] == jnp.arange(q_blocks, dtype=jnp.int32)[None, :]
    ).astype(f32)
    row_mask = jnp.sum(q_onehot[:, :, None] * mask_f[None, :, :], axis=1)
    allowed = jnp.broadcast_to(row_mask[:, :, None], (share, p_blocks, TILE)).reshape(
        share, passages
    )
    columns = jnp.arange(passages, dtype=jnp.int32)
    is_pos = (columns[None, :] == own_pos[:, None]).astype(f32)
    keep = jnp.maximum(allowed, is_pos)
    expo = jnp.exp(logits) * keep
    denom = jnp.sum(expo, axis=1)
    pos_logit = jnp.sum(logits * is_pos, axis=1)
    query_loss = jnp.log(denom) - pos_logit
    dlogits = (LOSS_SCALE * (expo / denom[:, None] - is_pos)).astype(jnp.bfloat16)
    dlog_all = lax.all_gather(dlogits, "tensor", axis=0, tiled=True)
    d_q = LOGIT_SCALE * jnp.dot(dlog_all, p_all, preferred_element_type=f32)
    d_p = lax.psum_scatter(
        LOGIT_SCALE
        * lax.dot_general(dlog_all, q_emb, (((0,), (0,)), ((), ())), preferred_element_type=f32),
        "dp",
        scatter_dimension=0,
        tiled=True,
    )
    d_unit = jnp.concatenate([d_q, d_p], axis=0)
    inner = lax.psum(jnp.sum(unit * d_unit, axis=1), "tensor")
    d_pooled = (d_unit - unit * inner[:, None]) / norms
    normalized_output_gradient = (weights[:, :, None] * d_pooled[:, None, :]).reshape(
        tok_rows, local_width
    )
    standardized_gradient = normalized_output_gradient * final_norm_weight
    average_correction = (
        lax.psum(jnp.sum(standardized_gradient * standardized_state, axis=1), "tensor")
        / complete_width
    )
    residual_gradient = (
        inverse_deviation
        * (standardized_gradient - standardized_state * average_correction[:, None])
    ).astype(jnp.bfloat16)
    rows = out_weight
    summed = lax.psum_scatter(
        lax.dot_general(
            rows, residual_gradient, (((1,), (1,)), ((), ())), preferred_element_type=f32
        ).astype(jnp.bfloat16),
        "tensor",
        scatter_dimension=0,
        tiled=True,
    ).astype(jnp.float32)
    d_context = summed.T.astype(jnp.bfloat16)
    return (query_loss, residual_gradient, d_context)


def solution(mesh):
    in_specs = (
        P("dp", "tensor"),
        P("dp", "tensor"),
        P(None, "tensor"),
        P("tensor"),
        P("dp"),
        P("dp"),
        P("dp"),
        P(),
    )
    out_specs = (P(("dp", "tensor")), P("dp", "tensor"), P("dp", "tensor"))
    return jax.shard_map(body, mesh=mesh, in_specs=in_specs, out_specs=out_specs, check_vma=False)
```

profile of v0, /device:TPU:1, one launch (start us, length us, event | category | flops | bytes accessed | tf_op | source)
XLA Modules:
  0.0 825.0 jit_solution(8588975617585447296)
XLA Ops:
  7.2 0.7 all-gather.4.cloned.1.call-update
  8.0 0.7 fusion.16
  8.8 48.7 %all-gather.4.cloned.1.call-done = bf16[512,2048]{1,0:T(8,128)(2,1)} async-done(((bf16[512,256]{1,0:T(8,128)(2,1)}), bf16[512,2048]{1,0:T(8,128)(2,1)}) %all-gather.4.cloned.1.call-update) | async-done | bytes 2097168 | tf_op jit(solution)/shard_map/all_gather | solution.py:34
  57.5 3.0 multiply_reduce_fusion
  60.5 12.6 %psum.28 = f32[512]{0:T(512)S(1)} all-reduce(f32[512]{0:T(512)S(1)} %get-tuple-element.8), channel_id=1, replica_groups=mesh['dp'=64,'tensor'=8] {'tensor'}, use_global_device_ids=true, to_apply=%region_1.0 | all-reduce | flops 512 | bytes 4096 | tf_op jit(solution)/shard_map/psum | solution.py:36
  73.6 15.9 %psum.29 = f32[32]{0:T(128)S(1)} all-reduce(f32[32]{0:T(128)S(1)} %fusion.7), channel_id=1, replica_groups=mesh['dp'=64,'tensor'=8] {'tensor'}, use_global_device_ids=true, to_apply=%region_3.0 | all-reduce | flops 32 | bytes 256 | tf_op jit(solution)/shard_map/psum | solution.py:45
  89.6 0.6 slice.11
  90.5 120.7 %all-gather.6.cloned.1.call-done = bf16[1024,512]{1,0:T(8,128)(2,1)} async-done(((bf16[16,512]{1,0:T(8,128)(2,1)}), bf16[1024,512]{1,0:T(8,128)(2,1)}) %all-gather.6.cloned.1.call-update) | async-done | bytes 1048592 | tf_op jit(solution)/shard_map/all_gather | solution.py:50
  211.1 2.2 fusion.9
  213.5 1.3 dynamic-slice
  215.5 70.8 %all-reduce.3.cloned.1.call-done = f32[16,1024]{1,0:T(8,128)} async-done(((f32[16,1024]{1,0:T(8,128)}), f32[16,1024]{1,0:T(8,128)}) %all-reduce.3.cloned.1.call-update) | async-done | bytes 65552
  286.3 1.0 fusion.14
  287.4 16.4 %all-gather = bf16[8,2,1024]{2,1,0:T(2,128)(2,1)S(1)} all-gather(bf16[1,2,1024]{2,1,0:T(2,128)(2,1)S(1)} %fusion.12), channel_id=1, replica_groups=mesh['dp'=64,'tensor'=8] {'tensor'}, dimensions={0}, use_global_device_ids=true | all-gather | bytes 36864 | tf_op jit(solution)/shard_map/all_gather | solution.py:78
  303.8 1.8 convolution_multiply_fusion
  305.8 1.5 convolution_multiply_fusion.1
  307.3 393.1 %reduce-scatter.3.cloned.1.call-done = f32[16,512]{1,0:T(8,128)} async-done(((f32[1024,512]{1,0:T(8,128)}), f32[16,512]{1,0:T(8,128)}) %reduce-scatter.3.cloned.1.call-update) | async-done | bytes 32784 | tf_op jit(solution)/shard_map/reduce_scatter | solution.py:80
  700.4 0.9 multiply_reduce_fusion.1
  701.4 65.4 %psum.30 = f32[32]{0:T(128)S(1)} all-reduce(f32[32]{0:T(128)S(1)} %multiply_reduce_fusion.1), channel_id=1, replica_groups=mesh['dp'=64,'tensor'=8] {'tensor'}, use_global_device_ids=true, to_apply=%region_10.11 | all-reduce | flops 32 | bytes 256 | tf_op jit(solution)/shard_map/psum | solution.py:88
  766.8 0.8 subtract_divide_fusion
  768.0 13.6 %psum.31 = f32[512]{0:T(512)S(1)} all-reduce(f32[512]{0:T(512)S(1)} %fusion.4), channel_id=1, replica_groups=mesh['dp'=64,'tensor'=8] {'tensor'}, use_global_device_ids=true, to_apply=%region_12.13 | all-reduce | flops 512 | bytes 4096 | tf_op jit(solution)/shard_map/psum | solution.py:95
  781.9 0.8 copy-done.1
  782.7 2.6 fusion
  785.4 0.5 log_subtract_fusion
  785.9 32.6 %reduce-scatter.5.cloned.1.call-done = bf16[256,512]{0,1:T(8,128)(2,1)} async-done(((bf16[2048,512]{0,1:T(8,128)(2,1)}), bf16[256,512]{0,1:T(8,128)(2,1)}) %reduce-scatter.5.cloned.1.call-update) | async-done | bytes 262160 | tf_op jit(solution)/shard_map/reduce_scatter | solution.py:103
  (37 shorter events, 2.1 us)
Async XLA Ops:
  7.2 50.4 %copy-start = (bf16[2048,512]{1,0:T(8,128)(2,1)S(1)}, bf16[2048,512]{1,0:T(8,128)(2,1)}, u32[]{:S(2)}) copy-start(bf16[2048,512]{1,0:T(8,128)(2,1)} %param.10) | copy-start | bytes 6291460
  7.2 50.3 %all-gather.4.cloned.1.call-start = ((), (), s32[]{:S(2)}) async-start(), calls=%async_computation.2 | async-start | bytes 2359296 | tf_op jit(solution)/shard_map/all_gather | solution.py:34
  7.9 203.2 %all-gather.6.cloned.1.call-start = ((), (), s32[]{:S(2)}) async-start(), calls=%async_computation.3 | async-start | bytes 1064960 | tf_op jit(solution)/shard_map/all_gather | solution.py:50
  8.8 64.3 %copy-start.2 = (f32[512]{0:T(512)S(1)}, f32[512]{0:T(512)}, u32[]{:S(2)}) copy-start(f32[512]{0:T(512)} %param.11) | copy-start | bytes 6148
  60.5 29.7 %copy-start.3 = (s32[8,8]{1,0:T(8,128)S(1)}, s32[8,8]{1,0:T(8,128)}, u32[]{:S(2)}) copy-start(s32[8,8]{1,0:T(8,128)} %param.15) | copy-start | bytes 772
  60.5 154.9 %copy-start.4 = (s32[16]{0:T(128)S(1)}, s32[16]{0:T(128)}, u32[]{:S(2)}) copy-start(s32[16]{0:T(128)} %param.14) | copy-start | bytes 196
  90.2 196.1 %all-reduce.3.cloned.1.call-start = ((), (), s32[]{:S(2)}) async-start(), calls=%async_computation.6 | async-start | bytes 131072
  213.4 487.0 %reduce-scatter.3.cloned.1.call-start = ((), (), s32[]{:S(2)}) async-start(), calls=%async_computation.4 | async-start | bytes 2129920 | tf_op jit(solution)/shard_map/reduce_scatter | solution.py:80
  305.7 512.8 %reduce-scatter.5.cloned.1.call-start = ((), (), s32[]{:S(2)}) async-start(), calls=%async_computation.5 | async-start | bytes 2359296 | tf_op jit(solution)/shard_map/reduce_scatter | solution.py:103
  781.9 0.8 copy-start.1
Sparse Core Ops, SparseCore 0:
  10.0 47.4 all-gather.3
  90.3 120.7 all-gather.5
  214.6 71.6 all-reduce.2
  305.8 394.5 reduce-scatter.2
  785.5 32.9 reduce-scatter.4
where the time goes:
time: 827 us; the launch traced here: 825 us
  waiting for transfers between devices  667 us (81%)
  blocking collectives  124 us (15%)
  between operations  14.6 us (2%)
  matrix products  11.4 us (1%)
    reduce_scatter x1, waiting for transfers between devices, body(): lax.psum_scatter(LOGIT_SCALE * lax.dot_general(dlog_all, q_emb, (((0,), (...  393 us
    all_gather x1, waiting for transfers between devices, body(): p_all = lax.all_gather(p_emb, 'dp', axis=0, tiled=True)  121 us
    unnamed x6, waiting for transfers between devices  71.5 us
    psum x1, blocking collectives, body(): inner = lax.psum(jnp.sum(unit * d_unit, axis=1), 'tensor')  65.4 us
    all_gather x1, waiting for transfers between devices, body(): lax.all_gather(context, 'tensor', axis=1, tiled=True)  48.7 us
    reduce_scatter x1, waiting for transfers between devices, body(): lax.psum_scatter(lax.dot_general(rows, residual_gradient, (((1,), (1,)),...  32.6 us
  transfers between devices with their start and end apart: 5, of which 5 were waited for; matrix products, arithmetic and copies ran while one was open for 1% of the time, Pallas kernels for 0%

commit v1 on v0

v1 whole, which is shorter than its diff:
```python
import jax
import jax.numpy as jnp
from jax import lax
from jax.sharding import Mesh
from jax.sharding import PartitionSpec as P

Q_DEV = 16
P_DEV = 16
SEQ_LEN = 16
TILE = 128
SEQS = Q_DEV + P_DEV

EPS = 1e-06
LOGIT_SCALE = 20.0
LOSS_SCALE = 1024.0

NZ, NX, NYH, NYL, NC = 8, 4, 2, 4, 2
NT = NYL * NC
T = ("yl", "core")
ROW = ("x",)
COL = ("z", "yh")
N_ROW = NX
N_COL = NZ * NYH


def exchange(parts, axes):
    return lax.all_to_all(parts, axes, 0, 0)


def gather(value, axes, count):
    return exchange(jnp.broadcast_to(value, (count,) + value.shape), axes)


def body(
    context,
    residual,
    out_weight,
    final_norm_weight,
    query_lengths,
    passage_lengths,
    positive_index,
    tile_mask,
):
    f32 = jnp.float32
    bf16 = jnp.bfloat16
    tokens, width = residual.shape
    hw_dev = context.shape[1]
    hw = out_weight.shape[0]
    full_width = width * NT
    core = lax.axis_index("core")
    gain = final_norm_weight

    positives = gather(jnp.broadcast_to(positive_index[None, :], (8, Q_DEV)), ROW, N_ROW)[:, 0, :]
    positives = positives.reshape(N_ROW, NT, Q_DEV // NT)
    rows_pos = lax.dynamic_index_in_dim(positives, lax.axis_index(T), 1, keepdims=False).reshape(-1)

    weight_by_core = out_weight.reshape(NYL, NC, hw_dev, width)
    own_half = lax.dynamic_index_in_dim(weight_by_core, core, 1, keepdims=False).reshape(-1, width)
    other_half = lax.dynamic_index_in_dim(weight_by_core, 1 - core, 1, keepdims=False).reshape(
        -1, width
    )
    own_context = lax.all_gather(context, "yl", axis=1, tiled=True)
    other_context = lax.ppermute(own_context, "core", [(0, 1), (1, 0)])
    hidden = residual.astype(f32) + jnp.dot(own_context, own_half, preferred_element_type=f32)
    hidden = hidden + jnp.dot(other_context, other_half, preferred_element_type=f32)

    squares = jnp.sum(hidden * hidden, axis=1).reshape(tokens // 128, 128)
    squares = jnp.sum(gather(squares, T, NT), axis=0).reshape(tokens)
    inv = lax.rsqrt(squares / full_width + EPS)

    lengths = jnp.concatenate([query_lengths, passage_lengths], axis=0)
    slots = jnp.arange(SEQ_LEN, dtype=jnp.int32)
    valid = (slots[None, :] < lengths[:, None]).astype(f32)
    weights = valid / lengths[:, None].astype(f32)
    scale = weights * inv.reshape(SEQS, SEQ_LEN)
    by_seq = hidden.reshape(SEQS, SEQ_LEN, width)
    pooled = jnp.sum(by_seq * scale[:, :, None], axis=1) * gain
    pooled_low = pooled.astype(bf16)
    pooled_gain = pooled * gain

    lifted = jnp.concatenate([hidden.astype(bf16), pooled_gain.astype(bf16)], axis=0)
    lifted = lax.dot_general(
        out_weight, lifted, (((1,), (1,)), ((), ())), preferred_element_type=f32
    ).astype(bf16)
    lifted = lax.psum_scatter(lifted, T, scatter_dimension=0, tiled=True)

    q_rows = gather(pooled_low[:Q_DEV], ROW, N_ROW)
    q_rows = q_rows.reshape(N_ROW, NT, Q_DEV // NT, width).swapaxes(0, 1).reshape(-1, width)
    p_cols = gather(pooled_low[Q_DEV:], COL, N_COL).reshape(-1, width)
    n_rows, n_cols = q_rows.shape[0], p_cols.shape[0]
    share = n_rows // NT
    scores = lax.dot_general(
        q_rows, p_cols, (((1,), (1,)), ((), ())), preferred_element_type=f32
    ).reshape(NT, share, n_cols)
    q_wide, p_wide = q_rows.astype(f32), p_cols.astype(f32)
    q_sq = jnp.sum(q_wide * q_wide, axis=1).reshape(NT, share)
    p_sq = jnp.sum(p_wide * p_wide, axis=1)
    own_sq = jnp.sum(pooled * pooled, axis=1)
    cross = jnp.sum(by_seq * pooled_gain[:, None, :], axis=2).reshape(-1)
    common = jnp.concatenate([p_sq, own_sq, cross])
    side = jnp.concatenate([q_sq, jnp.broadcast_to(common, (NT,) + common.shape)], axis=1)
    side_width = -(-side.shape[1] // (share * 128)) * 128
    side = jnp.pad(side, ((0, 0), (0, share * side_width - side.shape[1])))
    payload = jnp.concatenate([scores, side.reshape(NT, share, side_width)], axis=2)
    summed = jnp.sum(exchange(payload, T), axis=0)
    scores = summed[:, :n_cols]
    side = summed[:, n_cols:].reshape(-1)
    q_sq = side[:share]
    p_sq = side[share : share + n_cols]
    own_sq = side[share + n_cols : share + n_cols + SEQS] + EPS
    cross = side[share + n_cols + SEQS : share + n_cols + SEQS + tokens]
    q_rn = lax.rsqrt(q_sq + EPS)[:, None]
    p_rn = lax.rsqrt(p_sq + EPS)[None, :]
    rn = q_rn * p_rn
    logits = LOGIT_SCALE * scores * rn

    z, x, yh = lax.axis_index("z"), lax.axis_index("x"), lax.axis_index("yh")
    col = jnp.arange(n_cols, dtype=jnp.int32)
    col_z, col_yh, col_in = col // (NYH * P_DEV), (col // P_DEV) % NYH, col % P_DEV
    passage = ((col_z * NX + x) * NYH + col_yh) * P_DEV + col_in
    row = jnp.arange(share, dtype=jnp.int32) // (Q_DEV // NT)
    query_tile = ((z * NX + row) * NYH + yh) * Q_DEV // TILE
    q_hot = (query_tile[:, None] == jnp.arange(tile_mask.shape[0])[None, :]).astype(f32)
    p_hot = ((passage // TILE)[None, :] == jnp.arange(tile_mask.shape[1])[:, None]).astype(f32)
    by_q = jnp.sum(q_hot[:, :, None] * tile_mask.astype(f32)[None, :, :], axis=1)
    allowed = jnp.sum(by_q[:, :, None] * p_hot[None, :, :], axis=1)
    is_pos = (passage[None, :] == rows_pos[:, None]).astype(f32)
    keep = jnp.maximum(allowed, is_pos)
    expo = jnp.exp(logits) * keep

    lane = jnp.arange(128, dtype=jnp.int32)[None, :]
    sums = jnp.where(
        lane == 0,
        jnp.sum(expo, axis=1)[:, None],
        jnp.where(lane == 1, jnp.sum(logits * is_pos, axis=1)[:, None], 0.0),
    )
    sums = jnp.sum(gather(sums, ROW, N_ROW), axis=0)
    denom = sums[:, :1]
    losses = (jnp.log(denom) - sums[:, 1:2]).reshape(N_ROW, Q_DEV // NT)
    query_loss = lax.dynamic_index_in_dim(losses, x, 0, keepdims=False)

    dlogits = (LOSS_SCALE * rn * (expo / denom - is_pos)).astype(bf16)
    dlogits = gather(dlogits, T, NT).reshape(n_rows, n_cols)
    d_q = jnp.dot(dlogits, p_cols, preferred_element_type=f32).astype(bf16)
    d_q = d_q.reshape(NT, N_ROW, Q_DEV // NT, width).swapaxes(0, 1).reshape(N_ROW, Q_DEV, width)
    d_p = lax.dot_general(
        dlogits, q_rows, (((0,), (0,)), ((), ())), preferred_element_type=f32
    ).astype(bf16)
    d_q = jnp.sum(exchange(d_q, ROW).astype(f32), axis=0)
    d_p = jnp.sum(exchange(d_p.reshape(N_COL, P_DEV, width), COL).astype(f32), axis=0)
    back = jnp.concatenate([d_q, d_p], axis=0)

    inner = jnp.sum(pooled * back, axis=1)
    back_gain = back * gain
    cross_back = jnp.sum(by_seq * back_gain[:, None, :], axis=2).reshape(-1)
    back_up = lax.dot_general(
        back_gain.astype(bf16), out_weight, (((1,), (1,)), ((), ())), preferred_element_type=f32
    )
    back_up = back_up.reshape(SEQS, NT, hw_dev).swapaxes(0, 1)
    side = jnp.concatenate([cross_back, inner])
    side_rows = -(-side.shape[0] // (8 * hw_dev)) * 8
    side = jnp.pad(side, (0, side_rows * hw_dev - side.shape[0])).reshape(1, side_rows, hw_dev)
    payload = jnp.concatenate([back_up, jnp.broadcast_to(side, (NT,) + side.shape[1:])], axis=1)
    summed = jnp.sum(exchange(payload, T), axis=0)
    back_up = summed[:SEQS]
    side = summed[SEQS:].reshape(-1)
    cross_back, inner = side[:tokens], side[tokens : tokens + SEQS]

    ratio = inner / own_sq
    lead = LOGIT_SCALE * scale
    mean = (
        lead
        * (cross_back.reshape(SEQS, SEQ_LEN) - ratio[:, None] * cross.reshape(SEQS, SEQ_LEN))
        / full_width
    )
    inv_seq = inv.reshape(SEQS, SEQ_LEN)
    trail = inv_seq * inv_seq * mean
    d_pooled = back_gain - ratio[:, None] * pooled_gain
    residual_gradient = (
        (lead[:, :, None] * d_pooled[:, None, :] - trail[:, :, None] * by_seq)
        .astype(bf16)
        .reshape(tokens, width)
    )
    lifted = lifted.T.astype(f32)
    seq_up = back_up - ratio[:, None] * lifted[tokens:]
    d_context = (
        (
            lead[:, :, None] * seq_up[:, None, :]
            - trail[:, :, None] * lifted[:tokens].reshape(SEQS, SEQ_LEN, hw_dev)
        )
        .astype(bf16)
        .reshape(tokens, hw_dev)
    )
    return (query_loss, residual_gradient, d_context)


def solution(mesh):
    fine = Mesh(
        mesh.devices.reshape(NZ, NX, NYH, NYL, NC), ("z", "x", "yh", "yl", "core")
    )
    dp = ("z", "x", "yh")
    in_specs = (
        P(dp, T),
        P(dp, T),
        P(None, T),
        P(T),
        P(dp),
        P(dp),
        P(dp),
        P(),
    )
    out_specs = (P(dp + T), P(dp, T), P(dp, T))
    return jax.shard_map(body, mesh=fine, in_specs=in_specs, out_specs=out_specs, check_vma=False)
```

time: 827 us -> 248 us (0.30)
  waiting for transfers between devices: 667 us -> 125 us
  blocking collectives: 124 us -> 7.23 us
  starting transfers between devices: 0.2 us -> 52.8 us
  other arithmetic: 5.4 us -> 22.2 us
  local copies, waits for them, and re-layouts: 2.94 us -> 14.6 us
    reduce_scatter x2 -> x1, waiting for transfers between devices: 426 us -> 32.3 us  [body(): lifted = lax.psum_scatter(lifted, T, scatter_dimension=0, tiled=True)]
    all_gather x2 -> x1, waiting for transfers between devices: 169 us -> 44.5 us  [body(): own_context = lax.all_gather(context, 'yl', axis=1, tiled=True)]
    psum x4 -> x0, blocking collectives: 107 us -> none  [the longest x1 65.4 us: body(): inner = lax.psum(jnp.sum(unit * d_unit, axis=1), 'tensor')]
    unnamed x6 -> x2, waiting for transfers between devices: 71.5 us -> 0.7 us
    all_to_all x0 -> x9, starting transfers between devices: none -> 49.2 us  [exchange(): return lax.all_to_all(parts, axes, 0, 0)]
    all_to_all x0 -> x9, waiting for transfers between devices: none -> 47.8 us  [exchange(): return lax.all_to_all(parts, axes, 0, 0)]
    all_gather x1 -> x0, blocking collectives: 16.4 us -> none  [body(): dlog_all = lax.all_gather(dlogits, 'tensor', axis=0, tiled=True)]
  transfers between devices with their start and end apart: 5 -> 12, of which waited for: 5 -> 11; matrix products, arithmetic and copies ran while one was open for 1% -> 8% of each run, Pallas kernels for 0% -> 0%
where the time goes in v1:
time: 248 us; the launch traced here: 245 us
  waiting for transfers between devices  125 us (50%)
  starting transfers between devices  52.8 us (21%)
  other arithmetic  22.2 us (9%)
  local copies, waits for them, and re-layouts  14.6 us (6%)
  between operations  14.4 us (6%)
  matrix products  8.76 us (4%)
  blocking collectives  7.23 us (3%)
    all_to_all x9, starting transfers between devices, exchange(): return lax.all_to_all(parts, axes, 0, 0)  49.2 us
    all_to_all x9, waiting for transfers between devices, exchange(): return lax.all_to_all(parts, axes, 0, 0)  47.8 us
    all_gather x1, waiting for transfers between devices, body(): own_context = lax.all_gather(context, 'yl', axis=1, tiled=True)  44.5 us
    reduce_scatter x1, waiting for transfers between devices, body(): lifted = lax.psum_scatter(lifted, T, scatter_dimension=0, tiled=True)  32.3 us
    all_to_all x1, blocking collectives, exchange(): return lax.all_to_all(parts, axes, 0, 0)  7.23 us
  transfers between devices with their start and end apart: 12, of which 11 were waited for; matrix products, arithmetic and copies ran while one was open for 8% of the time, Pallas kernels for 0%

profile of v1, /device:TPU:1, one launch (start us, length us, event | category | flops | bytes accessed | tf_op | source)
XLA Modules:
  0.0 245.2 jit_solution(12884732533182521448)
XLA Ops:
  7.9 44.5 %all-gather.2.cloned.1.call-done = bf16[512,1024]{1,0:T(8,128)(2,1)} async-done(((bf16[512,256]{1,0:T(8,128)(2,1)}), bf16[512,1024]{1,0:T(8,128)(2,1)}) %all-gather.2.cloned.1.call-update) | async-done | bytes 1048592 | tf_op jit(solution)/shard_map/all_gather | solution.py:62
  52.4 3.6 %collective-permute-start = (bf16[512,1024]{1,0:T(8,128)(2,1)}, bf16[512,1024]{1,0:T(8,128)(2,1)S(1)}, u32[]{:S(2)}, u32[]{:S(2)}) collective-permute-start(bf16[512,1024]{1,0:T(8,128)(2,1)} %all-gather.2.cloned.1.call-done), channel_id=1, source_target_pairs={{0,1},{1,0},{2,3},{3,2},{4,5},{5,4},{6,7},{7,6},{8,9},{9,8},{10,11... | collective-permute-start | bytes 3145736 | tf_op jit(solution)/shard_map/ppermute | solution.py:63
  56.8 1.9 constant_dynamic-slice_fusion.2
  61.0 4.5 %all-to-all-start = ((f32[8,4,128]{2,1,0:T(4,128)}), f32[8,4,128]{2,1,0:T(4,128)S(1)}, u32[]{:S(2)}, u32[]{:S(2)}) async-start(f32[8,4,128]{2,1,0:T(4,128)} %broadcast_in_dim.53), calls=%async_computation | async-start | bytes 32768 | tf_op jit(solution)/shard_map/all_to_all | solution.py:27
  65.6 4.8 %all-to-all-done = f32[8,4,128]{2,1,0:T(4,128)S(1)} async-done(((f32[8,4,128]{2,1,0:T(4,128)}), f32[8,4,128]{2,1,0:T(4,128)S(1)}, u32[]{:S(2)}, u32[]{:S(2)}) %all-to-all-start) | async-done | bytes 16416 | tf_op jit(solution)/shard_map/all_to_all | solution.py:27
  71.5 1.2 fusion.43
  73.4 3.3 %all-to-all-start.1 = ((bf16[4,16,512]{2,1,0:T(8,128)(2,1)}), bf16[4,16,512]{2,1,0:T(8,128)(2,1)S(1)}, u32[]{:S(2)}, u32[]{:S(2)}) async-start(bf16[4,16,512]{2,1,0:T(8,128)(2,1)} %broadcast_in_dim.54), calls=%async_computation.1 | async-start | bytes 131072 | tf_op jit(solution)/shard_map/all_to_all | solution.py:27
  76.7 4.4 %all-to-all-done.1 = bf16[4,16,512]{2,1,0:T(8,128)(2,1)S(1)} async-done(((bf16[4,16,512]{2,1,0:T(8,128)(2,1)}), bf16[4,16,512]{2,1,0:T(8,128)(2,1)S(1)}, u32[]{:S(2)}, u32[]{:S(2)}) %all-to-all-start.1) | async-done | bytes 65568 | tf_op jit(solution)/shard_map/all_to_all | solution.py:27
  81.9 9.5 %all-to-all-start.2 = ((bf16[16,16,512]{2,1,0:T(8,128)(2,1)}), bf16[16,16,512]{2,1,0:T(8,128)(2,1)S(1)}, u32[]{:S(2)}, u32[]{:S(2)}) async-start(bf16[16,16,512]{2,1,0:T(8,128)(2,1)} %broadcast_in_dim.55), calls=%async_computation.2 | async-start | bytes 524288 | tf_op jit(solution)/shard_map/all_to_all | solution.py:27
  95.1 8.7 %all-to-all-done.2 = bf16[16,16,512]{2,1,0:T(8,128)(2,1)S(1)} async-done(((bf16[16,16,512]{2,1,0:T(8,128)(2,1)}), bf16[16,16,512]{2,1,0:T(8,128)(2,1)S(1)}, u32[]{:S(2)}, u32[]{:S(2)}) %all-to-all-start.2) | async-done | bytes 262176 | tf_op jit(solution)/shard_map/all_to_all | solution.py:27
  103.8 3.2 %all-to-all-start.4 = ((s32[4,1,128]{2,1,0:T(1,128)}), s32[4,1,128]{2,1,0:T(1,128)S(1)}, u32[]{:S(2)}, u32[]{:S(2)}) async-start(s32[4,1,128]{2,1,0:T(1,128)} %reshape.530), calls=%async_computation.4 | async-start | bytes 4096 | tf_op jit(solution)/shard_map/all_to_all | solution.py:27
  110.9 8.8 %all-to-all-start.3 = ((f32[8,8,384]{2,1,0:T(8,128)}), f32[8,8,384]{2,1,0:T(8,128)}, u32[]{:S(2)}, u32[]{:S(2)}) async-start(f32[8,8,384]{2,1,0:T(8,128)} %pad_maximum_fusion.1), calls=%async_computation.3 | async-start | bytes 196608 | tf_op jit(solution)/shard_map/all_to_all | solution.py:27
  128.0 7.2 %all_to_all.50 = f32[4,8,128]{2,1,0:T(8,128)} all-to-all(f32[4,8,128]{2,1,0:T(8,128)S(1)} %broadcast_in_dim.61), channel_id=1, replica_groups=mesh['z'=8,'x'=4,'yh'=2,'yl'=4,'core'=2] {'x'}, dimensions={0} | all-to-all | bytes 32768 | tf_op jit(solution)/shard_map/all_to_all | solution.py:27
  138.1 5.9 %all-to-all-start.6 = ((bf16[8,8,256]{2,1,0:T(8,128)(2,1)}), bf16[8,8,256]{2,1,0:T(8,128)(2,1)}, u32[]{:S(2)}, u32[]{:S(2)}) async-start(bf16[8,8,256]{2,1,0:T(8,128)(2,1)} %broadcast_in_dim.62), calls=%async_computation.6 | async-start | bytes 65536 | tf_op jit(solution)/shard_map/all_to_all | solution.py:27
  144.6 4.4 %all-to-all-done.6 = bf16[8,8,256]{2,1,0:T(8,128)(2,1)} async-done(((bf16[8,8,256]{2,1,0:T(8,128)(2,1)}), bf16[8,8,256]{2,1,0:T(8,128)(2,1)}, u32[]{:S(2)}, u32[]{:S(2)}) %all-to-all-start.6) | async-done | bytes 32800 | tf_op jit(solution)/shard_map/all_to_all | solution.py:27
  150.7 3.3 %all-to-all-start.7 = ((bf16[4,16,512]{2,1,0:T(8,128)(2,1)}), bf16[4,16,512]{2,1,0:T(8,128)(2,1)S(1)}, u32[]{:S(2)}, u32[]{:S(2)}) async-start(bf16[4,16,512]{2,1,0:T(8,128)(2,1)} %copy.60), calls=%async_computation.7 | async-start | bytes 131072 | tf_op jit(solution)/shard_map/all_to_all | solution.py:27
  154.0 1.8 convolution_convert_fusion.1
  155.8 2.6 %all-to-all-done.7 = bf16[4,16,512]{2,1,0:T(8,128)(2,1)S(1)} async-done(((bf16[4,16,512]{2,1,0:T(8,128)(2,1)}), bf16[4,16,512]{2,1,0:T(8,128)(2,1)S(1)}, u32[]{:S(2)}, u32[]{:S(2)}) %all-to-all-start.7) | async-done | bytes 65568 | tf_op jit(solution)/shard_map/all_to_all | solution.py:27
  158.4 4.0 %all-to-all-start.8 = ((bf16[16,16,512]{2,1,0:T(8,128)(2,1)}), bf16[16,16,512]{2,1,0:T(8,128)(2,1)S(1)}, u32[]{:S(2)}, u32[]{:S(2)}) async-start(bf16[16,16,512]{2,1,0:T(8,128)(2,1)} %bitcast.21), calls=%async_computation.8 | async-start | bytes 524288 | tf_op jit(solution)/shard_map/all_to_all | solution.py:27
  163.0 11.8 %all-to-all-done.8 = bf16[16,16,512]{2,1,0:T(8,128)(2,1)S(1)} async-done(((bf16[16,16,512]{2,1,0:T(8,128)(2,1)}), bf16[16,16,512]{2,1,0:T(8,128)(2,1)S(1)}, u32[]{:S(2)}, u32[]{:S(2)}) %all-to-all-start.8) | async-done | bytes 262176 | tf_op jit(solution)/shard_map/all_to_all | solution.py:27
  177.5 6.9 %all-to-all-start.9 = ((f32[8,40,256]{2,1,0:T(8,128)}), f32[8,40,256]{2,1,0:T(8,128)S(1)}, u32[]{:S(2)}, u32[]{:S(2)}) async-start(f32[8,40,256]{2,1,0:T(8,128)} %pad_maximum_fusion), calls=%async_computation.9 | async-start | bytes 655360 | tf_op jit(solution)/shard_map/all_to_all | solution.py:27
  185.0 9.4 %all-to-all-done.9 = f32[8,40,256]{2,1,0:T(8,128)S(1)} async-done(((f32[8,40,256]{2,1,0:T(8,128)}), f32[8,40,256]{2,1,0:T(8,128)S(1)}, u32[]{:S(2)}, u32[]{:S(2)}) %all-to-all-start.9) | async-done | bytes 327712 | tf_op jit(solution)/shard_map/all_to_all | solution.py:27
  200.0 2.8 %fusion = bf16[2048,544]{0,1:T(8,128)(2,1)} fusion(bf16[2048,512]{1,0:T(8,128)(2,1)S(1)} %copy-done, bf16[32,512]{1,0:T(8,128)(2,1)S(1)} %copy-done.4, bf16[512,512]{1,0:T(8,128)(2,1)S(1)} %get-tuple-element.13), kind=kOutput, calls=%fused_computation.1 | convolution fusion | flops 1143078912 | bytes 4882432 | tf_op jit(solution)/shard_map/dot_general | solution.py:82
  204.1 32.3 %reduce-scatter.2.cloned.1.call-done = bf16[256,544]{0,1:T(8,128)(2,1)} async-done(((bf16[2048,544]{0,1:T(8,128)(2,1)}), bf16[256,544]{0,1:T(8,128)(2,1)}) %reduce-scatter.2.cloned.1.call-update) | async-done | bytes 278544 | tf_op jit(solution)/shard_map/reduce_scatter | solution.py:85
  (132 shorter events, 40.2 us)
Async XLA Ops:
  7.2 45.2 %all-gather.2.cloned.1.call-start = ((), (), s32[]{:S(2)}) async-start(), calls=%async_computation.11 | async-start | bytes 1310720 | tf_op jit(solution)/shard_map/all_gather | solution.py:62
  52.4 7.2 %collective-permute-start = (bf16[512,1024]{1,0:T(8,128)(2,1)}, bf16[512,1024]{1,0:T(8,128)(2,1)S(1)}, u32[]{:S(2)}, u32[]{:S(2)}) collective-permute-start(bf16[512,1024]{1,0:T(8,128)(2,1)} %all-gather.2.cloned.1.call-done), channel_id=1, source_target_pairs={{0,1},{1,0},{2,3},{3,2},{4,5},{5,4},{6,7},{7,6},{8,9},{9,8},{10,11... | collective-permute-start | bytes 3145736 | tf_op jit(solution)/shard_map/ppermute | solution.py:63
  56.8 2.0 copy-start.17
  59.5 6.0 %copy-start.14 = (s32[16]{0:T(128)S(1)}, s32[16]{0:T(128)}, u32[]{:S(2)}) copy-start(s32[16]{0:T(128)} %param.13) | copy-start | bytes 196
  59.5 6.0 %copy-start.15 = (s32[16]{0:T(128)S(1)}, s32[16]{0:T(128)}, u32[]{:S(2)}) copy-start(s32[16]{0:T(128)} %param.12) | copy-start | bytes 196
  59.5 11.9 %copy-start.8 = (f32[512]{0:T(512)S(1)}, f32[512]{0:T(512)}, u32[]{:S(2)}) copy-start(f32[512]{0:T(512)} %param.11) | copy-start | bytes 6148
  60.3 31.6 %copy-start.13 = (s32[16]{0:T(128)S(1)}, s32[16]{0:T(128)}, u32[]{:S(2)}) copy-start(s32[16]{0:T(128)} %param.14) | copy-start | bytes 196
  61.0 9.5 %all-to-all-start = ((f32[8,4,128]{2,1,0:T(4,128)}), f32[8,4,128]{2,1,0:T(4,128)S(1)}, u32[]{:S(2)}, u32[]{:S(2)}) async-start(f32[8,4,128]{2,1,0:T(4,128)} %broadcast_in_dim.53), calls=%async_computation | async-start | bytes 32768 | tf_op jit(solution)/shard_map/all_to_all | solution.py:27
  72.7 22.1 %copy-start.1 = (f32[32,512]{1,0:T(8,128)}, f32[32,512]{1,0:T(8,128)S(1)}, u32[]{:S(2)}) copy-start(f32[32,512]{1,0:T(8,128)S(1)} %get-tuple-element.8) | copy-start | bytes 196612
  73.4 7.7 %all-to-all-start.1 = ((bf16[4,16,512]{2,1,0:T(8,128)(2,1)}), bf16[4,16,512]{2,1,0:T(8,128)(2,1)S(1)}, u32[]{:S(2)}, u32[]{:S(2)}) async-start(bf16[4,16,512]{2,1,0:T(8,128)(2,1)} %broadcast_in_dim.54), calls=%async_computation.1 | async-start | bytes 131072 | tf_op jit(solution)/shard_map/all_to_all | solution.py:27
  81.9 21.9 %all-to-all-start.2 = ((bf16[16,16,512]{2,1,0:T(8,128)(2,1)}), bf16[16,16,512]{2,1,0:T(8,128)(2,1)S(1)}, u32[]{:S(2)}, u32[]{:S(2)}) async-start(bf16[16,16,512]{2,1,0:T(8,128)(2,1)} %broadcast_in_dim.55), calls=%async_computation.2 | async-start | bytes 524288 | tf_op jit(solution)/shard_map/all_to_all | solution.py:27
  94.9 80.8 %copy-start = (bf16[2048,512]{1,0:T(8,128)(2,1)S(1)}, bf16[2048,512]{1,0:T(8,128)(2,1)}, u32[]{:S(2)}) copy-start(bf16[2048,512]{1,0:T(8,128)(2,1)} %param.10) | copy-start | bytes 6291460
  103.8 7.1 %all-to-all-start.4 = ((s32[4,1,128]{2,1,0:T(1,128)}), s32[4,1,128]{2,1,0:T(1,128)S(1)}, u32[]{:S(2)}, u32[]{:S(2)}) async-start(s32[4,1,128]{2,1,0:T(1,128)} %reshape.530), calls=%async_computation.4 | async-start | bytes 4096 | tf_op jit(solution)/shard_map/all_to_all | solution.py:27
  110.9 14.4 %all-to-all-start.3 = ((f32[8,8,384]{2,1,0:T(8,128)}), f32[8,8,384]{2,1,0:T(8,128)}, u32[]{:S(2)}, u32[]{:S(2)}) async-start(f32[8,8,384]{2,1,0:T(8,128)} %pad_maximum_fusion.1), calls=%async_computation.3 | async-start | bytes 196608 | tf_op jit(solution)/shard_map/all_to_all | solution.py:27
  124.3 3.7 %copy-start.10 = (s32[8]{0:T(128)}, s32[8]{0:T(128)S(1)}, u32[]{:S(2)}) copy-start(s32[8]{0:T(128)S(1)} %eq.83) | copy-start | bytes 100
  136.6 38.2 %copy-start.9 = (f32[512]{0:T(512)S(1)}, f32[512]{0:T(512)}, u32[]{:S(2)}) copy-start(f32[512]{0:T(512)} %param.11) | copy-start | bytes 6148
  138.1 11.0 %all-to-all-start.6 = ((bf16[8,8,256]{2,1,0:T(8,128)(2,1)}), bf16[8,8,256]{2,1,0:T(8,128)(2,1)}, u32[]{:S(2)}, u32[]{:S(2)}) async-start(bf16[8,8,256]{2,1,0:T(8,128)(2,1)} %broadcast_in_dim.62), calls=%async_computation.6 | async-start | bytes 65536 | tf_op jit(solution)/shard_map/all_to_all | solution.py:27
  150.7 7.7 %all-to-all-start.7 = ((bf16[4,16,512]{2,1,0:T(8,128)(2,1)}), bf16[4,16,512]{2,1,0:T(8,128)(2,1)S(1)}, u32[]{:S(2)}, u32[]{:S(2)}) async-start(bf16[4,16,512]{2,1,0:T(8,128)(2,1)} %copy.60), calls=%async_computation.7 | async-start | bytes 131072 | tf_op jit(solution)/shard_map/all_to_all | solution.py:27
  158.4 16.4 %all-to-all-start.8 = ((bf16[16,16,512]{2,1,0:T(8,128)(2,1)}), bf16[16,16,512]{2,1,0:T(8,128)(2,1)S(1)}, u32[]{:S(2)}, u32[]{:S(2)}) async-start(bf16[16,16,512]{2,1,0:T(8,128)(2,1)} %bitcast.21), calls=%async_computation.8 | async-start | bytes 524288 | tf_op jit(solution)/shard_map/all_to_all | solution.py:27
  176.5 7.9 %copy-start.3 = (f32[32,16]{1,0:T(8,128)S(1)}, f32[32,16]{1,0:T(8,128)}, u32[]{:S(2)}) copy-start(f32[32,16]{1,0:T(8,128)} %get-tuple-element.23) | copy-start | bytes 6148
  177.5 16.9 %all-to-all-start.9 = ((f32[8,40,256]{2,1,0:T(8,128)}), f32[8,40,256]{2,1,0:T(8,128)S(1)}, u32[]{:S(2)}, u32[]{:S(2)}) async-start(f32[8,40,256]{2,1,0:T(8,128)} %pad_maximum_fusion), calls=%async_computation.9 | async-start | bytes 655360 | tf_op jit(solution)/shard_map/all_to_all | solution.py:27
  184.3 52.0 %reduce-scatter.2.cloned.1.call-start = ((), (), s32[]{:S(2)}) async-start(), calls=%async_computation.12 | async-start | bytes 2506752 | tf_op jit(solution)/shard_map/reduce_scatter | solution.py:85
  195.0 5.0 %copy-start.4 = (bf16[32,512]{1,0:T(8,128)(2,1)S(1)}, bf16[32,512]{1,0:T(8,128)(2,1)}, u32[]{:S(2)}) copy-start(bf16[32,512]{1,0:T(8,128)(2,1)} %get-tuple-element.7) | copy-start | bytes 98308
  202.8 34.5 %copy-start.2 = (f32[40,256]{1,0:T(8,128)S(1)}, f32[40,256]{1,0:T(8,128)}, u32[]{:S(2)}) copy-start(f32[40,256]{1,0:T(8,128)} %reduce_sum.182) | copy-start | bytes 122884
  (6 other events, 6.3 us)
Sparse Core Ops, SparseCore 0:
  10.1 42.2 all-gather.1
  203.0 33.3 reduce-scatter.1

commit v2 on v1

--- a/solution.py
+++ b/solution.py
@@ -50,19 +50,20 @@
     core = lax.axis_index("core")
     gain = final_norm_weight
 
-    positives = gather(jnp.broadcast_to(positive_index[None, :], (8, Q_DEV)), ROW, N_ROW)[:, 0, :]
-    positives = positives.reshape(N_ROW, NT, Q_DEV // NT)
-    rows_pos = lax.dynamic_index_in_dim(positives, lax.axis_index(T), 1, keepdims=False).reshape(-1)
-
     weight_by_core = out_weight.reshape(NYL, NC, hw_dev, width)
     own_half = lax.dynamic_index_in_dim(weight_by_core, core, 1, keepdims=False).reshape(-1, width)
     other_half = lax.dynamic_index_in_dim(weight_by_core, 1 - core, 1, keepdims=False).reshape(
         -1, width
     )
-    own_context = lax.all_gather(context, "yl", axis=1, tiled=True)
-    other_context = lax.ppermute(own_context, "core", [(0, 1), (1, 0)])
-    hidden = residual.astype(f32) + jnp.dot(own_context, own_half, preferred_element_type=f32)
-    hidden = hidden + jnp.dot(other_context, other_half, preferred_element_type=f32)
+    halves = []
+    step = tokens // 2
+    for first in (0, step):
+        part = lax.slice_in_dim(context, first, first + step, axis=0)
+        own_context = lax.all_gather(part, "yl", axis=1, tiled=True)
+        other_context = lax.ppermute(own_context, "core", [(0, 1), (1, 0)])
+        half = jnp.dot(own_context, own_half, preferred_element_type=f32)
+        halves.append(half + jnp.dot(other_context, other_half, preferred_element_type=f32))
+    hidden = residual.astype(f32) + jnp.concatenate(halves, axis=0)
 
     squares = jnp.sum(hidden * hidden, axis=1).reshape(tokens // 128, 128)
     squares = jnp.sum(gather(squares, T, NT), axis=0).reshape(tokens)
@@ -82,10 +83,16 @@
     lifted = lax.dot_general(
         out_weight, lifted, (((1,), (1,)), ((), ())), preferred_element_type=f32
     ).astype(bf16)
+    pooled_low, lifted = lax.optimization_barrier((pooled_low, lifted))
     lifted = lax.psum_scatter(lifted, T, scatter_dimension=0, tiled=True)
 
-    q_rows = gather(pooled_low[:Q_DEV], ROW, N_ROW)
-    q_rows = q_rows.reshape(N_ROW, NT, Q_DEV // NT, width).swapaxes(0, 1).reshape(-1, width)
+    position = jnp.stack([positive_index // 32, positive_index % 32], axis=1).astype(bf16)
+    position = jnp.pad(position, ((0, 0), (0, 126)))
+    q_rows = gather(jnp.concatenate([pooled_low[:Q_DEV], position], axis=1), ROW, N_ROW)
+    q_rows = q_rows.reshape(N_ROW, NT, Q_DEV // NT, -1).swapaxes(0, 1).reshape(N_ROW * Q_DEV, -1)
+    position = q_rows[:, width : width + 2].astype(jnp.int32)
+    position = position[:, 0] * 32 + position[:, 1]
+    q_rows = q_rows[:, :width]
     p_cols = gather(pooled_low[Q_DEV:], COL, N_COL).reshape(-1, width)
     n_rows, n_cols = q_rows.shape[0], p_cols.shape[0]
     share = n_rows // NT
@@ -124,29 +131,43 @@
     p_hot = ((passage // TILE)[None, :] == jnp.arange(tile_mask.shape[1])[:, None]).astype(f32)
     by_q = jnp.sum(q_hot[:, :, None] * tile_mask.astype(f32)[None, :, :], axis=1)
     allowed = jnp.sum(by_q[:, :, None] * p_hot[None, :, :], axis=1)
-    is_pos = (passage[None, :] == rows_pos[:, None]).astype(f32)
-    keep = jnp.maximum(allowed, is_pos)
-    expo = jnp.exp(logits) * keep
-
-    lane = jnp.arange(128, dtype=jnp.int32)[None, :]
-    sums = jnp.where(
-        lane == 0,
-        jnp.sum(expo, axis=1)[:, None],
-        jnp.where(lane == 1, jnp.sum(logits * is_pos, axis=1)[:, None], 0.0),
-    )
-    sums = jnp.sum(gather(sums, ROW, N_ROW), axis=0)
-    denom = sums[:, :1]
-    losses = (jnp.log(denom) - sums[:, 1:2]).reshape(N_ROW, Q_DEV // NT)
-    query_loss = lax.dynamic_index_in_dim(losses, x, 0, keepdims=False)
-
-    dlogits = (LOSS_SCALE * rn * (expo / denom - is_pos)).astype(bf16)
-    dlogits = gather(dlogits, T, NT).reshape(n_rows, n_cols)
+    me = lax.axis_index(T)
+    at_pos = (passage[None, :] == position[:, None]).astype(f32)
+    is_pos = lax.dynamic_slice_in_dim(at_pos, me * share, share, axis=0)
+    others = jnp.exp(logits) * allowed * (1.0 - is_pos)
+
+    sums = jnp.stack(
+        [
+            jnp.sum(others, axis=1),
+            jnp.sum(jnp.exp(logits) * is_pos, axis=1),
+            jnp.sum(logits * is_pos, axis=1),
+        ],
+        axis=1,
+    )
+    high = lax.reduce_precision(sums, 8, 7)
+    middle = lax.reduce_precision(sums - high, 8, 7)
+    low = sums - high - middle
+    sums = jnp.pad(jnp.concatenate([high, middle, low], axis=1), ((0, 0), (0, 128 - 9)))
+    terms = rn * (others + is_pos)
+    payload = jnp.concatenate([terms.astype(bf16), sums.astype(bf16)], axis=1)
+    payload = gather(payload, ROW + T, N_ROW * NT).reshape(N_ROW, NT * share, n_cols + 128)
+    sums = payload[:, :, n_cols : n_cols + 9].astype(f32)
+    sums = jnp.sum(sums.reshape(N_ROW, NT * share, 3, 3), axis=(0, 2))
+    denom = sums[:, 0] + sums[:, 1]
+    losses = (jnp.log(denom) - sums[:, 2]).reshape(NT, N_ROW, Q_DEV // NT)
+    query_loss = lax.dynamic_slice(losses, (me, x, 0), (1, 1, Q_DEV // NT)).reshape(-1)
+    terms = lax.dynamic_index_in_dim(payload, x, 0, keepdims=False)[:, :n_cols].astype(f32)
+    other_factor = LOSS_SCALE / denom
+    pos_factor = -other_factor * sums[:, 0]
+    factor = other_factor[:, None] + at_pos * (pos_factor - other_factor)[:, None]
+    dlogits = (terms * factor).astype(bf16)
     d_q = jnp.dot(dlogits, p_cols, preferred_element_type=f32).astype(bf16)
     d_q = d_q.reshape(NT, N_ROW, Q_DEV // NT, width).swapaxes(0, 1).reshape(N_ROW, Q_DEV, width)
     d_p = lax.dot_general(
         dlogits, q_rows, (((0,), (0,)), ((), ())), preferred_element_type=f32
     ).astype(bf16)
     d_q = jnp.sum(exchange(d_q, ROW).astype(f32), axis=0)
+    d_p, lifted = lax.optimization_barrier((d_p, lifted))
     d_p = jnp.sum(exchange(d_p.reshape(N_COL, P_DEV, width), COL).astype(f32), axis=0)
     back = jnp.concatenate([d_q, d_p], axis=0)
 
@@ -157,13 +178,15 @@
         back_gain.astype(bf16), out_weight, (((1,), (1,)), ((), ())), preferred_element_type=f32
     )
     back_up = back_up.reshape(SEQS, NT, hw_dev).swapaxes(0, 1)
-    side = jnp.concatenate([cross_back, inner])
-    side_rows = -(-side.shape[0] // (8 * hw_dev)) * 8
-    side = jnp.pad(side, (0, side_rows * hw_dev - side.shape[0])).reshape(1, side_rows, hw_dev)
-    payload = jnp.concatenate([back_up, jnp.broadcast_to(side, (NT,) + side.shape[1:])], axis=1)
-    summed = jnp.sum(exchange(payload, T), axis=0)
+    side = jnp.pad(jnp.concatenate([cross_back, inner]), (0, 8 * hw_dev - tokens - SEQS))
+    high = lax.reduce_precision(side, 8, 7)
+    side = jnp.concatenate([high, side - high]).astype(bf16).reshape(1, 16, hw_dev)
+    payload = jnp.concatenate(
+        [back_up.astype(bf16), jnp.broadcast_to(side, (NT,) + side.shape[1:])], axis=1
+    )
+    summed = jnp.sum(exchange(payload, T).astype(f32), axis=0)
     back_up = summed[:SEQS]
-    side = summed[SEQS:].reshape(-1)
+    side = (summed[SEQS : SEQS + 8] + summed[SEQS + 8 :]).reshape(-1)
     cross_back, inner = side[:tokens], side[tokens : tokens + SEQS]
 
     ratio = inner / own_sq

time: 248 us -> 219 us (0.88)
  waiting for transfers between devices: 125 us -> 47.1 us
  blocking collectives: 7.23 us -> 27.8 us
  local copies, waits for them, and re-layouts: 14.6 us -> 28.3 us
  starting transfers between devices: 52.8 us -> 62.5 us
  matrix products: 8.76 us -> 11.9 us
  other arithmetic: 22.2 us -> 24.8 us
    all_gather x1 -> x0, waiting for transfers between devices: 44.5 us -> none  [body(): own_context = lax.all_gather(context, 'yl', axis=1, tiled=True)]
    reduce_scatter x1, waiting for transfers between devices: 32.3 us -> 0.01 us  [body(): lifted = lax.psum_scatter(lifted, T, scatter_dimension=0, tiled=True)]
    all_gather x0 -> x2, blocking collectives: none -> 27.8 us  [body(): own_context = lax.all_gather(part, 'yl', axis=1, tiled=True)]
    ppermute x1 -> x2, starting transfers between devices: 3.56 us -> 14.7 us  [body(): other_context = lax.ppermute(own_context, 'core', [(0, 1), (1, 0)])]
    all_to_all x1 -> x0, blocking collectives: 7.23 us -> none  [exchange(): return lax.all_to_all(parts, axes, 0, 0)]
    another operation x1 -> x4, local copies, waits for them, and re-layouts: 0.01 us -> 4.01 us  [the longest x3 3.91 us: body(): jnp.stack([jnp.sum(others, axis=1), jnp.sum(jnp.exp(logits) * is_pos, axi...]
    reduce_sum x2 -> x5, other arithmetic: 1.65 us -> 4.9 us  [the longest x2 2.6 us: body(): sums = jnp.sum(sums.reshape(N_ROW, NT * share, 3, 3), axis=(0, 2))]
    all_to_all x9 -> x8, starting transfers between devices: 49.2 us -> 47.7 us  [exchange(): return lax.all_to_all(parts, axes, 0, 0)]
  transfers between devices with their start and end apart: 12 -> 11, of which waited for: 11 -> 8; matrix products, arithmetic and copies ran while one was open for 8% -> 21% of each run, Pallas kernels for 0% -> 0%
where the time goes in v2:
time: 219 us; the launch traced here: 217 us
  starting transfers between devices  62.5 us (29%)
  waiting for transfers between devices  47.1 us (22%)
  local copies, waits for them, and re-layouts  28.3 us (13%)
  blocking collectives  27.8 us (13%)
  other arithmetic  24.8 us (11%)
  between operations  14.5 us (7%)
  matrix products  11.9 us (5%)
    all_to_all x8, starting transfers between devices, exchange(): return lax.all_to_all(parts, axes, 0, 0)  47.7 us
    all_to_all x8, waiting for transfers between devices, exchange(): return lax.all_to_all(parts, axes, 0, 0)  47 us
    all_gather x2, blocking collectives, body(): own_context = lax.all_gather(part, 'yl', axis=1, tiled=True)  27.8 us
    ppermute x2, starting transfers between devices, body(): other_context = lax.ppermute(own_context, 'core', [(0, 1), (1, 0)])  14.7 us
    unnamed x42, local copies, waits for them, and re-layouts  4.6 us
  transfers between devices with their start and end apart: 11, of which 8 were waited for; matrix products, arithmetic and copies ran while one was open for 21% of the time, Pallas kernels for 0%

profile of v2, /device:TPU:1, one launch (start us, length us, event | category | flops | bytes accessed | tf_op | source)
XLA Modules:
  0.0 216.9 jit_solution(14269352977454399425)
XLA Ops:
  8.2 14.1 %all_gather.6 = bf16[256,1024]{1,0:T(8,128)(2,1)S(1)} all-gather(bf16[256,256]{1,0:T(8,128)(2,1)S(1)} %get-tuple-element.26), channel_id=1, replica_groups=mesh['z'=8,'x'=4,'yh'=2,'yl'=4,'core'=2] {'yl'}, dimensions={1}, use_global_device_ids=true | all-gather | bytes 655360 | tf_op jit(solution)/shard_map/all_gather | solution.py:62
  22.3 10.3 %collective-permute-start = (bf16[256,1024]{1,0:T(8,128)(2,1)S(1)}, bf16[256,1024]{1,0:T(8,128)(2,1)}, u32[]{:S(2)}, u32[]{:S(2)}) collective-permute-start(bf16[256,1024]{1,0:T(8,128)(2,1)S(1)} %all_gather.6), channel_id=1, source_target_pairs={{0,1},{1,0},{2,3},{3,2},{4,5},{5,4},{6,7},{7,6},{8,9},{9,8},{10,11... | collective-permute-start | bytes 1572872 | tf_op jit(solution)/shard_map/ppermute | solution.py:63
  32.6 13.7 %all_gather.7 = bf16[256,1024]{1,0:T(8,128)(2,1)S(1)} all-gather(bf16[256,256]{1,0:T(8,128)(2,1)S(1)} %get-tuple-element.27), channel_id=1, replica_groups=mesh['z'=8,'x'=4,'yh'=2,'yl'=4,'core'=2] {'yl'}, dimensions={1}, use_global_device_ids=true | all-gather | bytes 655360 | tf_op jit(solution)/shard_map/all_gather | solution.py:62
  46.3 4.4 %collective-permute-start.1 = (bf16[256,1024]{1,0:T(8,128)(2,1)S(1)}, bf16[256,1024]{1,0:T(8,128)(2,1)}, u32[]{:S(2)}, u32[]{:S(2)}) collective-permute-start(bf16[256,1024]{1,0:T(8,128)(2,1)S(1)} %all_gather.7), channel_id=1, source_target_pairs={{0,1},{1,0},{2,3},{3,2},{4,5},{5,4},{6,7},{7,6},{8,9},{9,8},{10,11... | collective-permute-start | bytes 1572872 | tf_op jit(solution)/shard_map/ppermute | solution.py:63
  50.7 1.7 constant_dynamic-slice_fusion.2
  58.6 3.3 %all-to-all-start = ((f32[8,4,128]{2,1,0:T(4,128)}), f32[8,4,128]{2,1,0:T(4,128)S(1)}, u32[]{:S(2)}, u32[]{:S(2)}) async-start(f32[8,4,128]{2,1,0:T(4,128)} %broadcast_in_dim.12), calls=%async_computation | async-start | bytes 32768 | tf_op jit(solution)/shard_map/all_to_all | solution.py:27
  62.0 4.8 %all-to-all-done = f32[8,4,128]{2,1,0:T(4,128)S(1)} async-done(((f32[8,4,128]{2,1,0:T(4,128)}), f32[8,4,128]{2,1,0:T(4,128)S(1)}, u32[]{:S(2)}, u32[]{:S(2)}) %all-to-all-start) | async-done | bytes 16416 | tf_op jit(solution)/shard_map/all_to_all | solution.py:27
  69.7 3.8 %fusion = bf16[2048,544]{0,1:T(8,128)(2,1)} fusion(bf16[2048,512]{1,0:T(8,128)(2,1)S(1)} %copy-done, bf16[32,512]{1,0:T(8,128)(2,1)S(1)} %get-tuple-element.20, bf16[512,512]{1,0:T(8,128)(2,1)} %get-tuple-element.18), kind=kOutput, calls=%fused_computation.1 | convolution fusion | flops 1143078912 | bytes 4882432 | tf_op jit(solution)/shard_map/dot_general | solution.py:83
  74.1 3.3 %all-to-all-start.1 = ((bf16[4,16,640]{2,1,0:T(8,128)(2,1)}), bf16[4,16,640]{2,1,0:T(8,128)(2,1)S(1)}, u32[]{:S(2)}, u32[]{:S(2)}) async-start(bf16[4,16,640]{2,1,0:T(8,128)(2,1)} %broadcast_in_dim.13), calls=%async_computation.1 | async-start | bytes 163840 | tf_op jit(solution)/shard_map/all_to_all | solution.py:27
  78.2 3.8 %all-to-all-done.1 = bf16[4,16,640]{2,1,0:T(8,128)(2,1)S(1)} async-done(((bf16[4,16,640]{2,1,0:T(8,128)(2,1)}), bf16[4,16,640]{2,1,0:T(8,128)(2,1)S(1)}, u32[]{:S(2)}, u32[]{:S(2)}) %all-to-all-start.1) | async-done | bytes 81952 | tf_op jit(solution)/shard_map/all_to_all | solution.py:27
  82.7 11.0 %all-to-all-start.2 = ((bf16[16,16,512]{2,1,0:T(8,128)(2,1)}), bf16[16,16,512]{2,1,0:T(8,128)(2,1)S(1)}, u32[]{:S(2)}, u32[]{:S(2)}) async-start(bf16[16,16,512]{2,1,0:T(8,128)(2,1)} %broadcast_in_dim.14), calls=%async_computation.2 | async-start | bytes 524288 | tf_op jit(solution)/shard_map/all_to_all | solution.py:27
  99.3 6.8 %all-to-all-done.2 = bf16[16,16,512]{2,1,0:T(8,128)(2,1)S(1)} async-done(((bf16[16,16,512]{2,1,0:T(8,128)(2,1)}), bf16[16,16,512]{2,1,0:T(8,128)(2,1)S(1)}, u32[]{:S(2)}, u32[]{:S(2)}) %all-to-all-start.2) | async-done | bytes 262176 | tf_op jit(solution)/shard_map/all_to_all | solution.py:27
  110.6 8.3 %all-to-all-start.3 = ((f32[8,8,384]{2,1,0:T(8,128)}), f32[8,8,384]{2,1,0:T(8,128)}, u32[]{:S(2)}, u32[]{:S(2)}) async-start(f32[8,8,384]{2,1,0:T(8,128)} %pad_maximum_fusion.1), calls=%async_computation.3 | async-start | bytes 196608 | tf_op jit(solution)/shard_map/all_to_all | solution.py:27
  120.2 4.9 %all-to-all-done.3 = f32[8,8,384]{2,1,0:T(8,128)} async-done(((f32[8,8,384]{2,1,0:T(8,128)}), f32[8,8,384]{2,1,0:T(8,128)}, u32[]{:S(2)}, u32[]{:S(2)}) %all-to-all-start.3) | async-done | bytes 98336 | tf_op jit(solution)/shard_map/all_to_all | solution.py:27
  127.9 2.1 fusion.55
  136.2 5.5 %all-to-all-start.4 = ((bf16[32,8,384]{2,1,0:T(8,128)(2,1)}), bf16[32,8,384]{2,1,0:T(8,128)(2,1)}, u32[]{:S(2)}, u32[]{:S(2)}) async-start(bf16[32,8,384]{2,1,0:T(8,128)(2,1)} %broadcast_in_dim.16), calls=%async_computation.4 | async-start | bytes 393216 | tf_op jit(solution)/shard_map/all_to_all | solution.py:27
  141.8 10.1 %all-to-all-done.4 = bf16[32,8,384]{2,1,0:T(8,128)(2,1)} async-done(((bf16[32,8,384]{2,1,0:T(8,128)(2,1)}), bf16[32,8,384]{2,1,0:T(8,128)(2,1)}, u32[]{:S(2)}, u32[]{:S(2)}) %all-to-all-start.4) | async-done | bytes 196640 | tf_op jit(solution)/shard_map/all_to_all | solution.py:27
  164.5 3.3 %all-to-all-start.5 = ((bf16[4,16,512]{2,1,0:T(8,128)(2,1)}), bf16[4,16,512]{2,1,0:T(8,128)(2,1)S(1)}, u32[]{:S(2)}, u32[]{:S(2)}) async-start(bf16[4,16,512]{2,1,0:T(8,128)(2,1)} %copy.73), calls=%async_computation.5 | async-start | bytes 131072 | tf_op jit(solution)/shard_map/all_to_all | solution.py:27
  167.8 1.8 convolution_convert_fusion.2
  169.6 2.6 %all-to-all-done.5 = bf16[4,16,512]{2,1,0:T(8,128)(2,1)S(1)} async-done(((bf16[4,16,512]{2,1,0:T(8,128)(2,1)}), bf16[4,16,512]{2,1,0:T(8,128)(2,1)S(1)}, u32[]{:S(2)}, u32[]{:S(2)}) %all-to-all-start.5) | async-done | bytes 65568 | tf_op jit(solution)/shard_map/all_to_all | solution.py:27
  172.9 6.3 %all-to-all-start.6 = ((bf16[16,16,512]{2,1,0:T(8,128)(2,1)}), bf16[16,16,512]{2,1,0:T(8,128)(2,1)S(1)}, u32[]{:S(2)}, u32[]{:S(2)}) async-start(bf16[16,16,512]{2,1,0:T(8,128)(2,1)} %bitcast.28), calls=%async_computation.7 | async-start | bytes 524288 | tf_op jit(solution)/shard_map/all_to_all | solution.py:27
  182.8 8.9 %all-to-all-done.6 = bf16[16,16,512]{2,1,0:T(8,128)(2,1)S(1)} async-done(((bf16[16,16,512]{2,1,0:T(8,128)(2,1)}), bf16[16,16,512]{2,1,0:T(8,128)(2,1)S(1)}, u32[]{:S(2)}, u32[]{:S(2)}) %all-to-all-start.6) | async-done | bytes 262176 | tf_op jit(solution)/shard_map/all_to_all | solution.py:27
  194.4 6.7 %all-to-all-start.7 = ((bf16[8,48,256]{2,1,0:T(8,128)(2,1)}), bf16[8,48,256]{2,1,0:T(8,128)(2,1)S(1)}, u32[]{:S(2)}, u32[]{:S(2)}) async-start(bf16[8,48,256]{2,1,0:T(8,128)(2,1)} %pad_maximum_fusion), calls=%async_computation.8 | async-start | bytes 393216 | tf_op jit(solution)/shard_map/all_to_all | solution.py:27
  202.3 5.2 %all-to-all-done.7 = bf16[8,48,256]{2,1,0:T(8,128)(2,1)S(1)} async-done(((bf16[8,48,256]{2,1,0:T(8,128)(2,1)}), bf16[8,48,256]{2,1,0:T(8,128)(2,1)S(1)}, u32[]{:S(2)}, u32[]{:S(2)}) %all-to-all-start.7) | async-done | bytes 196640 | tf_op jit(solution)/shard_map/all_to_all | solution.py:27
  (141 shorter events, 55.6 us)
Async XLA Ops:
  22.3 31.5 %collective-permute-start = (bf16[256,1024]{1,0:T(8,128)(2,1)S(1)}, bf16[256,1024]{1,0:T(8,128)(2,1)}, u32[]{:S(2)}, u32[]{:S(2)}) collective-permute-start(bf16[256,1024]{1,0:T(8,128)(2,1)S(1)} %all_gather.6), channel_id=1, source_target_pairs={{0,1},{1,0},{2,3},{3,2},{4,5},{5,4},{6,7},{7,6},{8,9},{9,8},{10,11... | collective-permute-start | bytes 1572872 | tf_op jit(solution)/shard_map/ppermute | solution.py:63
  46.3 9.0 %collective-permute-start.1 = (bf16[256,1024]{1,0:T(8,128)(2,1)S(1)}, bf16[256,1024]{1,0:T(8,128)(2,1)}, u32[]{:S(2)}, u32[]{:S(2)}) collective-permute-start(bf16[256,1024]{1,0:T(8,128)(2,1)S(1)} %all_gather.7), channel_id=1, source_target_pairs={{0,1},{1,0},{2,3},{3,2},{4,5},{5,4},{6,7},{7,6},{8,9},{9,8},{10,11... | collective-permute-start | bytes 1572872 | tf_op jit(solution)/shard_map/ppermute | solution.py:63
  52.5 1.0 copy-start.12
  52.5 1.1 copy-start.17
  52.5 1.1 copy-start.15
  52.5 1.1 copy-start.16
  53.7 3.0 %copy-start.2 = (bf16[512,512]{1,0:T(8,128)(2,1)S(1)}, bf16[512,512]{1,0:T(8,128)(2,1)}, u32[]{:S(2)}) copy-start(bf16[512,512]{1,0:T(8,128)(2,1)} %param.9) | copy-start | bytes 1572868
  56.8 12.3 %copy-start.10 = (f32[512]{0:T(512)S(1)}, f32[512]{0:T(512)}, u32[]{:S(2)}) copy-start(f32[512]{0:T(512)} %param.11) | copy-start | bytes 6148
  56.8 12.9 %copy-start = (bf16[2048,512]{1,0:T(8,128)(2,1)S(1)}, bf16[2048,512]{1,0:T(8,128)(2,1)}, u32[]{:S(2)}) copy-start(bf16[2048,512]{1,0:T(8,128)(2,1)} %param.10) | copy-start | bytes 6291460
  58.6 8.2 %all-to-all-start = ((f32[8,4,128]{2,1,0:T(4,128)}), f32[8,4,128]{2,1,0:T(4,128)S(1)}, u32[]{:S(2)}, u32[]{:S(2)}) async-start(f32[8,4,128]{2,1,0:T(4,128)} %broadcast_in_dim.12), calls=%async_computation | async-start | bytes 32768 | tf_op jit(solution)/shard_map/all_to_all | solution.py:27
  74.1 7.8 %all-to-all-start.1 = ((bf16[4,16,640]{2,1,0:T(8,128)(2,1)}), bf16[4,16,640]{2,1,0:T(8,128)(2,1)S(1)}, u32[]{:S(2)}, u32[]{:S(2)}) async-start(bf16[4,16,640]{2,1,0:T(8,128)(2,1)} %broadcast_in_dim.13), calls=%async_computation.1 | async-start | bytes 163840 | tf_op jit(solution)/shard_map/all_to_all | solution.py:27
  77.4 92.2 %reduce-scatter.2.cloned.1.call-start = ((), (), s32[]{:S(2)}) async-start(), calls=%async_computation.9 | async-start | bytes 2506752 | tf_op jit(solution)/shard_map/reduce_scatter | solution.py:87
  82.7 23.5 %all-to-all-start.2 = ((bf16[16,16,512]{2,1,0:T(8,128)(2,1)}), bf16[16,16,512]{2,1,0:T(8,128)(2,1)S(1)}, u32[]{:S(2)}, u32[]{:S(2)}) async-start(bf16[16,16,512]{2,1,0:T(8,128)(2,1)} %broadcast_in_dim.14), calls=%async_computation.2 | async-start | bytes 524288 | tf_op jit(solution)/shard_map/all_to_all | solution.py:27
  110.6 14.5 %all-to-all-start.3 = ((f32[8,8,384]{2,1,0:T(8,128)}), f32[8,8,384]{2,1,0:T(8,128)}, u32[]{:S(2)}, u32[]{:S(2)}) async-start(f32[8,8,384]{2,1,0:T(8,128)} %pad_maximum_fusion.1), calls=%async_computation.3 | async-start | bytes 196608 | tf_op jit(solution)/shard_map/all_to_all | solution.py:27
  136.2 15.6 %all-to-all-start.4 = ((bf16[32,8,384]{2,1,0:T(8,128)(2,1)}), bf16[32,8,384]{2,1,0:T(8,128)(2,1)}, u32[]{:S(2)}, u32[]{:S(2)}) async-start(bf16[32,8,384]{2,1,0:T(8,128)(2,1)} %broadcast_in_dim.16), calls=%async_computation.4 | async-start | bytes 393216 | tf_op jit(solution)/shard_map/all_to_all | solution.py:27
  159.5 1.3 copy-start.5
  164.5 7.7 %all-to-all-start.5 = ((bf16[4,16,512]{2,1,0:T(8,128)(2,1)}), bf16[4,16,512]{2,1,0:T(8,128)(2,1)S(1)}, u32[]{:S(2)}, u32[]{:S(2)}) async-start(bf16[4,16,512]{2,1,0:T(8,128)(2,1)} %copy.73), calls=%async_computation.5 | async-start | bytes 131072 | tf_op jit(solution)/shard_map/all_to_all | solution.py:27
  172.2 0.6 copy-start.4
  172.9 18.8 %all-to-all-start.6 = ((bf16[16,16,512]{2,1,0:T(8,128)(2,1)}), bf16[16,16,512]{2,1,0:T(8,128)(2,1)S(1)}, u32[]{:S(2)}, u32[]{:S(2)}) async-start(bf16[16,16,512]{2,1,0:T(8,128)(2,1)} %bitcast.28), calls=%async_computation.7 | async-start | bytes 524288 | tf_op jit(solution)/shard_map/all_to_all | solution.py:27
  192.7 9.6 %copy-start.3 = (bf16[256,544]{0,1:T(8,128)(2,1)S(1)}, bf16[256,544]{0,1:T(8,128)(2,1)}, u32[]{:S(2)}) copy-start(bf16[256,544]{0,1:T(8,128)(2,1)} %reduce-scatter.2.cloned.1.call-done) | copy-start | bytes 835588
  193.4 14.2 %copy-start.9 = (f32[1024]{0:T(1024)S(1)}, f32[1024]{0:T(1024)}, u32[]{:S(2)}) copy-start(f32[1024]{0:T(1024)} %copy-done.8) | copy-start | bytes 12292
  193.4 14.6 %copy-start.7 = (f32[4,128]{1,0:T(4,128)S(1)}, f32[4,128]{1,0:T(4,128)}, u32[]{:S(2)}) copy-start(f32[4,128]{1,0:T(4,128)} %copy-done.6) | copy-start | bytes 6148
  193.4 14.6 %copy-start.11 = (f32[512]{0:T(512)S(1)}, f32[512]{0:T(512)}, u32[]{:S(2)}) copy-start(f32[512]{0:T(512)} %div.114) | copy-start | bytes 6148
  194.4 13.1 %all-to-all-start.7 = ((bf16[8,48,256]{2,1,0:T(8,128)(2,1)}), bf16[8,48,256]{2,1,0:T(8,128)(2,1)S(1)}, u32[]{:S(2)}, u32[]{:S(2)}) async-start(bf16[8,48,256]{2,1,0:T(8,128)(2,1)} %pad_maximum_fusion), calls=%async_computation.8 | async-start | bytes 393216 | tf_op jit(solution)/shard_map/all_to_all | solution.py:27
  (5 other events, 2.9 us)
Sparse Core Ops, SparseCore 0:
  81.1 46.9 reduce-scatter.1

commit v3 on v0

v3 whole, which is shorter than its diff:
```python
import functools

import jax
import jax.numpy as jnp
from jax import lax
from jax.experimental import pallas as pl
from jax.experimental.pallas import tpu as pltpu
from jax.sharding import Mesh
from jax.sharding import PartitionSpec as P

Q_DEV = 16
P_DEV = 16
SEQ_LEN = 16
SEQS = Q_DEV + P_DEV
TOKENS = SEQS * SEQ_LEN
HALF = TOKENS // 2

EPS = 1e-06
LOGIT_SCALE = 20.0
LOSS_SCALE = 1024.0

NZ, NX, NYH, NYL, NC = 8, 4, 2, 4, 2
NT = NYL * NC
T = ("yl", "core")
ROW = ("x",)
COL = ("z", "yh")
N_ROW = NX
N_COL = NZ * NYH
ROWS = N_ROW * Q_DEV
COLS = N_COL * P_DEV
SHARE = ROWS // NT
PAIR = Q_DEV // NT
HW_DEV = 256
WIDTH = 512
FULL = WIDTH * NT

f32 = jnp.float32
bf16 = jnp.bfloat16
i32 = jnp.int32


def dot(a, b, dims=((1,), (0,)), exact=False):
    return lax.dot_general(
        a,
        b,
        (dims, ((), ())),
        preferred_element_type=f32,
        precision=lax.Precision.HIGHEST if exact else None,
    )


def iota(shape, dim):
    return lax.broadcasted_iota(i32, shape, dim)


def to_col(row, n):
    eye = iota((n, n), 0) == iota((n, n), 1)
    return jnp.sum(jnp.where(eye, row, 0.0), axis=1, keepdims=True)


def to_row(col, n):
    eye = iota((n, n), 0) == iota((n, n), 1)
    return jnp.sum(jnp.where(eye, col, 0.0), axis=0, keepdims=True)


def seg_mask():
    return iota((SEQS, TOKENS), 1) // SEQ_LEN == iota((SEQS, TOKENS), 0)


def split(value):
    high = value.astype(bf16).astype(f32)
    return high, value - high


def row_order():
    shape = (ROWS, ROWS)
    here, there = iota(shape, 0), iota(shape, 1)
    k, x, j = here // SHARE, (here % SHARE) // PAIR, here % PAIR
    return (there == x * Q_DEV + k * PAIR + j).astype(f32).astype(bf16)


def hidden_kernel(last, ids, own, other, weight, residual, *refs):
    if last:
        before, hidden, low, payload = refs
    else:
        hidden, low, payload = refs
    core = ids[0]
    total = residual[...].astype(f32)
    for y in range(NYL):
        part = slice(y * HW_DEV, (y + 1) * HW_DEV)
        for ref, c in ((own, core), (other, 1 - core)):
            first = pl.multiple_of((y * NC + c) * HW_DEV, HW_DEV)
            total = total + dot(ref[:, part], weight[pl.ds(first, HW_DEV), :])
    hidden[...] = total
    low[...] = total.astype(bf16)
    square = jnp.sum(total * total, axis=1, keepdims=True)
    rows = [to_row(square[b * 128 : (b + 1) * 128], 128) for b in range(HALF // 128)]
    if last:
        rows = [before[0:1], before[1:2]] + rows + [jnp.zeros((4, 128), f32)]
        payload[...] = jnp.broadcast_to(jnp.concatenate(rows, axis=0)[None], (NT, 8, 128))
    else:
        payload[...] = jnp.concatenate(rows + [jnp.zeros((6, 128), f32)], axis=0)


def pool_kernel(
    squares, q_len, p_len, position, gain, hidden_a, hidden_b, wi, inv, pooled, lift, q_pay, p_pay
):
    total = jnp.sum(squares[...], axis=0)
    total = jnp.concatenate([total[b : b + 1] for b in range(TOKENS // 128)], axis=1)
    inverse = lax.rsqrt(total / FULL + EPS)
    inv[...] = inverse
    lengths = jnp.concatenate(
        [to_col(q_len[...].astype(f32), Q_DEV), to_col(p_len[...].astype(f32), P_DEV)], axis=0
    )
    slot = (iota((SEQS, TOKENS), 1) % SEQ_LEN).astype(f32)
    weight = jnp.where(seg_mask() & (slot < lengths), 1.0 / lengths, 0.0) * inverse
    wi[...] = weight
    value = dot(weight[:, :HALF], hidden_a[...], exact=True)
    value = value + dot(weight[:, HALF:], hidden_b[...], exact=True)
    value = value * gain[...]
    pooled[...] = value
    lift[...] = (value * gain[...]).astype(bf16)
    low = value.astype(bf16)
    where = to_col(position[...].astype(f32), Q_DEV)
    high = jnp.floor(where * (1.0 / 32.0))
    lane = iota((Q_DEV, 128), 1)
    where = jnp.where(lane == 0, high, jnp.where(lane == 1, where - 32.0 * high, 0.0))
    q_pay[:, :, :WIDTH] = jnp.broadcast_to(low[None, :Q_DEV], (N_ROW, Q_DEV, WIDTH))
    q_pay[:, :, WIDTH:] = jnp.broadcast_to(where.astype(bf16)[None], (N_ROW, Q_DEV, 128))
    p_pay[...] = jnp.broadcast_to(low[None, Q_DEV:], (N_COL, P_DEV, WIDTH))


def lift_kernel(low_a, low_b, pooled, weight, out):
    for n in range(NT):
        part = slice(n * HW_DEV, (n + 1) * HW_DEV)
        w = weight[part, :]
        out[:HALF, part] = dot(low_a[...], w, ((1,), (1,))).astype(bf16)
        out[HALF:TOKENS, part] = dot(low_b[...], w, ((1,), (1,))).astype(bf16)
        out[TOKENS:, part] = dot(pooled[...], w, ((1,), (1,))).astype(bf16)


def score_kernel(q_all, p_all, pooled, lift, low_a, low_b, payload, position):
    order = row_order()
    q_rows = dot(order, q_all[...].reshape(ROWS, WIDTH + 128))
    position[...] = q_rows[:, WIDTH:]
    q_rows = q_rows[:, :WIDTH]
    p_cols = p_all[...].reshape(COLS, WIDTH)
    scores = dot(q_rows.astype(bf16), p_cols, ((1,), (1,)))
    payload[:, :, :COLS] = scores.reshape(NT, SHARE, COLS)
    q_sq = to_row(jnp.sum(q_rows * q_rows, axis=1, keepdims=True), ROWS)
    p_wide = p_cols.astype(f32)
    p_sq = jnp.sum(p_wide * p_wide, axis=1, keepdims=True)
    own = pooled[...]
    own_sq = to_row(jnp.sum(own * own, axis=1, keepdims=True), SEQS)
    cross = [dot(lift[...], low[...], ((1,), (1,))) for low in (low_a, low_b)]
    cross = jnp.sum(jnp.where(seg_mask(), jnp.concatenate(cross, axis=1), 0.0), axis=0, keepdims=True)
    rows = [to_row(p_sq[b * 128 : (b + 1) * 128], 128) for b in range(COLS // 128)]
    rows += [cross[:, b * 128 : (b + 1) * 128] for b in range(TOKENS // 128)]
    rows.append(jnp.concatenate([own_sq, jnp.zeros((1, 128 - SEQS), f32)], axis=1))
    rows.append(jnp.concatenate([q_sq, jnp.zeros((1, 128 - ROWS), f32)], axis=1))
    payload[:, :, COLS:] = jnp.broadcast_to(jnp.concatenate(rows, axis=0)[None], (NT, 8, 128))


def at_positive(position, x):
    where = position[:, 0:1] * 32.0 + position[:, 1:2]
    col = iota((position.shape[0], COLS), 1)
    passage = (col // 32) * 128 + x * 32 + col % 32
    return passage.astype(f32) == where


def softmax_kernel(ids, tile_mask, parts, position, payload, side):
    me, z, x = ids[1], ids[2], ids[3]
    total = jnp.sum(parts[...], axis=0)
    side[...] = total[:, COLS:]
    block = total[:, COLS:]
    scores = total[:, :COLS]
    p_sq = jnp.concatenate([block[0:1], block[1:2]], axis=1)
    own = iota((SHARE, 128), 1) == me * SHARE + iota((SHARE, 128), 0)
    q_sq = jnp.sum(jnp.where(own, block[7:8], 0.0), axis=1, keepdims=True)
    rn = lax.rsqrt(q_sq + EPS) * lax.rsqrt(p_sq + EPS)
    logits = LOGIT_SCALE * scores * rn
    block_of = iota((SHARE, COLS), 1) // 32
    allowed = jnp.zeros((SHARE, COLS), f32)
    for j in range(NZ):
        allowed = jnp.where(block_of == j, tile_mask[z, j].astype(f32), allowed)
    first = pl.multiple_of(me * SHARE, SHARE)
    is_pos = at_positive(position[pl.ds(first, SHARE), :], x)
    expo = jnp.exp(logits)
    others = jnp.where(is_pos, 0.0, expo * allowed)
    sums = [
        jnp.sum(others, axis=1, keepdims=True),
        jnp.sum(jnp.where(is_pos, expo, 0.0), axis=1, keepdims=True),
        jnp.sum(jnp.where(is_pos, logits, 0.0), axis=1, keepdims=True),
    ]
    lane = iota((SHARE, COLS), 1)
    row = jnp.zeros((SHARE, COLS), f32)
    for i, value in enumerate(sums):
        high, rest = split(value)
        middle, low = split(rest)
        for j, piece in enumerate((high, middle, low)):
            row = jnp.where(lane == 3 * i + j, piece, row)
    terms = rn * jnp.where(is_pos, 1.0, others)
    payload[...] = jnp.broadcast_to(
        jnp.concatenate([terms, row], axis=0).astype(bf16)[None], payload.shape
    )


def back_kernel(ids, parts, position, q_all, p_all, loss, q_pay, p_pay):
    me, x = ids[1], ids[3]
    total = jnp.zeros((NT, SHARE, 128), f32)
    for k in range(N_ROW):
        total = total + parts[k * NT : (k + 1) * NT, :, :128].astype(f32)[:, SHARE:, :]
    total = total.reshape(ROWS, 128)
    lane = iota((ROWS, 128), 1)
    others, positive, logit = (
        jnp.sum(jnp.where(lane // 3 == i, total, 0.0), axis=1, keepdims=True) for i in range(3)
    )
    denom = others + positive
    losses = jnp.log(denom) - logit
    row = me * SHARE + x * PAIR + iota((ROWS, 128), 1)
    mine = (iota((ROWS, 128), 0) == row) & (lane < PAIR)
    loss[...] = jnp.broadcast_to(
        jnp.sum(jnp.where(mine, losses, 0.0), axis=0, keepdims=True), loss.shape
    )
    first = pl.multiple_of(x * NT, NT)
    terms = parts[pl.ds(first, NT)].astype(f32)[:, :SHARE, :].reshape(ROWS, COLS)
    factor = LOSS_SCALE / denom
    terms = terms * jnp.where(at_positive(position[...], x), -factor * others, factor)
    terms = dot(row_order(), terms.astype(bf16), ((0,), (0,))).astype(bf16)
    d_q = dot(terms, p_all[...].reshape(COLS, WIDTH))
    q_pay[...] = d_q.astype(bf16).reshape(N_ROW, Q_DEV, WIDTH)
    d_p = dot(terms, q_all[...].reshape(ROWS, WIDTH + 128)[:, :WIDTH], ((0,), (0,)))
    p_pay[...] = d_p.astype(bf16).reshape(N_COL, P_DEV, WIDTH)


def up_kernel(q_parts, p_parts, pooled, gain, low_a, low_b, weight, back_gain, payload):
    back = jnp.concatenate(
        [jnp.sum(q_parts[...].astype(f32), axis=0), jnp.sum(p_parts[...].astype(f32), axis=0)],
        axis=0,
    )
    inner = to_row(jnp.sum(pooled[...] * back, axis=1, keepdims=True), SEQS)
    scaled = back * gain[...]
    back_gain[...] = scaled
    scaled = scaled.astype(bf16)
    cross = [dot(scaled, low[...], ((1,), (1,))) for low in (low_a, low_b)]
    cross = jnp.sum(jnp.where(seg_mask(), jnp.concatenate(cross, axis=1), 0.0), axis=0, keepdims=True)
    inner = jnp.concatenate([inner, jnp.zeros((1, HW_DEV - SEQS), f32)], axis=1)
    rows = jnp.concatenate([cross[:, :HW_DEV], cross[:, HW_DEV:], inner, jnp.zeros((5, HW_DEV), f32)], axis=0)
    high, low = split(rows)
    side = jnp.concatenate([high, low], axis=0).astype(bf16)
    for n in range(NT):
        w = weight[n * HW_DEV : (n + 1) * HW_DEV, :]
        payload[n, :SEQS, :] = dot(scaled, w, ((1,), (1,))).astype(bf16)
        payload[n, SEQS:, :] = side


def final_kernel(parts, side, wi, inv, pooled, gain, back_gain, hidden_a, hidden_b, lifted, d_res, d_ctx):
    total = jnp.sum(parts[...].astype(f32), axis=0)
    rows = total[SEQS : SEQS + 8] + total[SEQS + 8 :]
    cross_back = jnp.concatenate([rows[0:1], rows[1:2]], axis=1)
    inner = rows[2:3, :SEQS]
    block = side[...]
    cross = jnp.concatenate([block[b : b + 1] for b in range(2, 6)], axis=1)
    ratio = to_col(inner / (block[6:7, :SEQS] + EPS), SEQS)
    lead = LOGIT_SCALE * wi[...]
    inverse = inv[...]
    by_token = jnp.sum(lead * (cross_back - ratio * cross), axis=0, keepdims=True)
    trail = inverse * inverse * by_token / FULL
    d_pooled = back_gain[...] - ratio * (pooled[...] * gain[...])
    seq_up = total[:SEQS] - ratio * lifted[TOKENS:, :].astype(f32)
    both = jnp.concatenate([d_pooled, seq_up], axis=1)
    for b in range(TOKENS // 128):
        part = slice(b * 128, (b + 1) * 128)
        hidden = (hidden_a, hidden_b)[b * 128 // HALF]
        inner_part = slice(b * 128 % HALF, b * 128 % HALF + 128)
        spread = dot(lead[:, part], both, ((0,), (0,)), exact=True)
        column = to_col(trail[:, part], 128)
        d_res[part, :] = (spread[:, :WIDTH] - column * hidden[inner_part, :]).astype(bf16)
        d_ctx[part, :] = (spread[:, WIDTH:] - column * lifted[part, :].astype(f32)).astype(bf16)


VMEM = pl.BlockSpec(memory_space=pltpu.VMEM)
SMEM = pl.BlockSpec(memory_space=pltpu.SMEM)


def call(kernel, name, outs, args, scalars=0, flops=1 << 20):
    out = [jax.ShapeDtypeStruct(shape, dtype) for shape, dtype in outs]
    size = sum(a.size * a.dtype.itemsize for a in (*args, *out))
    return pl.pallas_call(
        kernel,
        out_shape=out,
        in_specs=[SMEM] * scalars + [VMEM] * (len(args) - scalars),
        out_specs=[VMEM] * len(out),
        compiler_params=pltpu.CompilerParams(vmem_limit_bytes=40 << 20),
        cost_estimate=pl.CostEstimate(flops=flops, bytes_accessed=size, transcendentals=0),
        name=name,
    )(*args)


def exchange(parts, axes):
    return lax.all_to_all(parts, axes, 0, 0)


def body(
    context,
    residual,
    out_weight,
    final_norm_weight,
    query_lengths,
    passage_lengths,
    positive_index,
    tile_mask,
):
    me = lax.axis_index(T)
    ids = jnp.stack(
        [lax.axis_index("core"), me, lax.axis_index("z"), lax.axis_index("x")]
    ).astype(i32)
    gain = final_norm_weight.reshape(1, WIDTH)

    parts = []
    for first in (0, HALF):
        own = lax.all_gather(context[first : first + HALF], "yl", axis=1, tiled=True)
        parts.append((own, lax.ppermute(own, "core", [(0, 1), (1, 0)])))
    hidden_outs = [((HALF, WIDTH), f32), ((HALF, WIDTH), bf16)]
    hidden_a, low_a, squares = call(
        functools.partial(hidden_kernel, False),
        "hidden_a",
        hidden_outs + [((8, 128), f32)],
        (ids, *parts[0], out_weight, residual[:HALF]),
        1,
        flops=2 * HALF * 2048 * WIDTH,
    )
    hidden_b, low_b, squares = call(
        functools.partial(hidden_kernel, True),
        "hidden_b",
        hidden_outs + [((NT, 8, 128), f32)],
        (ids, *parts[1], out_weight, residual[HALF:], squares),
        1,
        flops=2 * HALF * 2048 * WIDTH,
    )
    squares = exchange(squares, T)

    wi, inv, pooled, lift, q_pay, p_pay = call(
        pool_kernel,
        "pool",
        [
            ((SEQS, TOKENS), f32),
            ((1, TOKENS), f32),
            ((SEQS, WIDTH), f32),
            ((SEQS, WIDTH), bf16),
            ((N_ROW, Q_DEV, WIDTH + 128), bf16),
            ((N_COL, P_DEV, WIDTH), bf16),
        ],
        (
            squares,
            query_lengths.reshape(1, Q_DEV),
            passage_lengths.reshape(1, P_DEV),
            positive_index.reshape(1, Q_DEV),
            gain,
            hidden_a,
            hidden_b,
        ),
    )
    q_all = exchange(q_pay, ROW)
    (lifted,) = call(
        lift_kernel,
        "lift",
        [((TOKENS + SEQS, NT * HW_DEV), bf16)],
        (low_a, low_b, lift, out_weight),
        flops=2 * TOKENS * 2048 * WIDTH,
    )
    p_pay, lifted = lax.optimization_barrier((p_pay, lifted))
    lifted = lax.psum_scatter(lifted, T, scatter_dimension=1, tiled=True)
    p_all = exchange(p_pay, COL)

    payload, position = call(
        score_kernel,
        "score",
        [((NT, SHARE, COLS + 128), f32), ((ROWS, 128), f32)],
        (q_all, p_all, pooled, lift, low_a, low_b),
    )
    payload, side = call(
        softmax_kernel,
        "softmax",
        [((N_ROW * NT, 2 * SHARE, COLS), bf16), ((SHARE, 128), f32)],
        (ids, tile_mask, exchange(payload, T), position),
        2,
    )
    loss, q_pay, p_pay = call(
        back_kernel,
        "back",
        [((8, 128), f32), ((N_ROW, Q_DEV, WIDTH), bf16), ((N_COL, P_DEV, WIDTH), bf16)],
        (ids, exchange(payload, ROW + T), position, q_all, p_all),
        1,
    )
    query_loss = loss[0, :PAIR]
    q_back = exchange(q_pay, ROW)
    p_pay, lifted = lax.optimization_barrier((p_pay, lifted))
    p_back = exchange(p_pay, COL)
    back_gain, payload = call(
        up_kernel,
        "up",
        [((SEQS, WIDTH), f32), ((NT, SEQS + 16, HW_DEV), bf16)],
        (q_back, p_back, pooled, gain, low_a, low_b, out_weight),
    )
    residual_gradient, d_context = call(
        final_kernel,
        "final",
        [((TOKENS, WIDTH), bf16), ((TOKENS, HW_DEV), bf16)],
        (exchange(payload, T), side, wi, inv, pooled, gain, back_gain, hidden_a, hidden_b, lifted),
    )
    return (query_loss, residual_gradient, d_context)


def solution(mesh):
    fine = Mesh(
        mesh.devices.reshape(NZ, NX, NYH, NYL, NC), ("z", "x", "yh", "yl", "core")
    )
    dp = ("z", "x", "yh")
    in_specs = (
        P(dp, T),
        P(dp, T),
        P(None, T),
        P(T),
        P(dp),
        P(dp),
        P(dp),
        P(),
    )
    out_specs = (P(dp + T), P(dp, T), P(dp, T))
    return jax.shard_map(body, mesh=fine, in_specs=in_specs, out_specs=out_specs, check_vma=False)
```

time: 827 us -> 194 us (0.23)
  waiting for transfers between devices: 667 us -> 9.7 us
  starting transfers between devices: 0.2 us -> 24.1 us
  local copies, waits for them, and re-layouts: 2.94 us -> 17 us
  Pallas kernels: 0 us -> 12 us
  matrix products: 11.4 us -> 0 us
    reduce_scatter x2 -> x1, waiting for transfers between devices: 426 us -> 0.02 us  [body(): lifted = lax.psum_scatter(lifted, T, scatter_dimension=1, tiled=True)]
    all_gather x2 -> x0, waiting for transfers between devices: 169 us -> none  [the longest x1 121 us: body(): p_all = lax.all_gather(p_emb, 'dp', axis=0, tiled=True)]
    psum x4 -> x0, blocking collectives: 107 us -> none  [the longest x1 65.4 us: body(): inner = lax.psum(jnp.sum(unit * d_unit, axis=1), 'tensor')]
    all_to_all x0 -> x6, blocking collectives: none -> 86.8 us  [exchange(): return lax.all_to_all(parts, axes, 0, 0)]
    unnamed x6 -> x1, waiting for transfers between devices: 71.5 us -> 0.02 us
    ppermute x0 -> x2, starting transfers between devices: none -> 14.5 us  [body(): parts.append((own, lax.ppermute(own, 'core', [(0, 1), (1, 0)])))]
    all_gather x1 -> x2, blocking collectives: 16.4 us -> 28.8 us  [body(): own = lax.all_gather(context[first:first + HALF], 'yl', axis=1, tiled=True)]
    pallas_call x0 -> x9, Pallas kernels: none -> 12 us  [call(): pl.pallas_call(kernel, out_shape=out, in_specs=[SMEM] * scalars + [VMEM]...]
  transfers between devices with their start and end apart: 5 -> 5, of which waited for: 5 -> 2; matrix products, arithmetic and copies ran while one was open for 1% -> 1% of each run, Pallas kernels for 0% -> 2%
where the time goes in v3:
time: 194 us; the launch traced here: 193 us
  blocking collectives  116 us (60%)
  starting transfers between devices  24.1 us (12%)
  local copies, waits for them, and re-layouts  17 us (9%)
  between operations  14.3 us (7%)
  Pallas kernels  12 us (6%)
  waiting for transfers between devices  9.7 us (5%)
    all_to_all x6, blocking collectives, exchange(): return lax.all_to_all(parts, axes, 0, 0)  86.8 us
    all_gather x2, blocking collectives, body(): own = lax.all_gather(context[first:first + HALF], 'yl', axis=1, tiled=True)  28.8 us
    ppermute x2, starting transfers between devices, body(): parts.append((own, lax.ppermute(own, 'core', [(0, 1), (1, 0)])))  14.5 us
    unnamed x56, local copies, waits for them, and re-layouts  13.6 us
    pallas_call x9, Pallas kernels, call(): pl.pallas_call(kernel, out_shape=out, in_specs=[SMEM] * scalars + [VMEM]...  12 us
    all_to_all x2, waiting for transfers between devices, exchange(): return lax.all_to_all(parts, axes, 0, 0)  9.66 us
    all_to_all x2, starting transfers between devices, exchange(): return lax.all_to_all(parts, axes, 0, 0)  9.58 us
  transfers between devices with their start and end apart: 5, of which 2 were waited for; matrix products, arithmetic and copies ran while one was open for 1% of the time, Pallas kernels for 2%

profile of v3, /device:TPU:1, one launch (start us, length us, event | category | flops | bytes accessed | tf_op | source)
XLA Modules:
  0.0 192.6 jit_solution(5179521953274066012)
XLA Ops:
  7.2 1.1 fusion.1
  8.3 14.1 %all_gather.7.own = bf16[256,1024]{1,0:T(8,128)(2,1)S(1)} all-gather(bf16[256,256]{1,0:T(8,128)(2,1)S(1)} %get-tuple-element.59), channel_id=1, replica_groups=mesh['z'=8,'x'=4,'yh'=2,'yl'=4,'core'=2] {'yl'}, dimensions={1}, use_global_device_ids=true | all-gather | bytes 655360 | tf_op jit(solution)/shard_map/all_gather | solution.py:322
  22.5 10.3 %collective-permute-start.1 = (bf16[256,1024]{1,0:T(8,128)(2,1)S(1)}, bf16[256,1024]{1,0:T(8,128)(2,1)S(1)}, u32[]{:S(2)}, u32[]{:S(2)}) collective-permute-start(bf16[256,1024]{1,0:T(8,128)(2,1)S(1)} %all_gather.7.own), channel_id=1, source_target_pairs={{0,1},{1,0},{2,3},{3,2},{4,5},{5,4},{6,7},{7,6},{8,9},{9,8},{10,11... | collective-permute-start | bytes 1572872 | tf_op jit(solution)/shard_map/ppermute | solution.py:323
  32.8 14.7 %all_gather.6.own = bf16[256,1024]{1,0:T(8,128)(2,1)} all-gather(bf16[256,256]{1,0:T(8,128)(2,1)S(1)} %get-tuple-element.60), channel_id=1, replica_groups=mesh['z'=8,'x'=4,'yh'=2,'yl'=4,'core'=2] {'yl'}, dimensions={1}, use_global_device_ids=true | all-gather | bytes 655360 | tf_op jit(solution)/shard_map/all_gather | solution.py:322
  47.5 4.1 %collective-permute-start = (bf16[256,1024]{1,0:T(8,128)(2,1)}, bf16[256,1024]{1,0:T(8,128)(2,1)}, u32[]{:S(2)}, u32[]{:S(2)}) collective-permute-start(bf16[256,1024]{1,0:T(8,128)(2,1)} %all_gather.6.own), channel_id=1, source_target_pairs={{0,1},{1,0},{2,3},{3,2},{4,5},{5,4},{6,7},{7,6},{8,9},{9,8},{10,11... | collective-permute-start | bytes 1572872 | tf_op jit(solution)/shard_map/ppermute | solution.py:323
  51.7 1.1 fusion
  55.7 1.3 hidden_a.1
  57.1 2.0 %hidden_b.1 = (f32[256,512]{1,0:T(8,128)S(1)}, bf16[256,512]{1,0:T(8,128)(2,1)S(1)}, f32[8,8,128]{2,1,0:T(8,128)S(1)}) custom-call(s32[4]{0:T(128)S(1)} %pad_add_fusion.ids, bf16[256,1024]{1,0:T(8,128)(2,1)} %all_gather.6.own, bf16[256,1024]{1,0:T(8,128)(2,1)} %collective-permute-done.other, bf16[2048,512]{1,0:T(8,128)(2,1)S(1)} %copy-done, ...), custom_call_target="tpu_custom_call" | custom-call | flops 536870912 | bytes 4231184 | tf_op jit(solution)/shard_map/hidden_b/pallas_call | solution.py:289
  59.1 7.3 %all_to_all.40.squares = f32[8,8,128]{2,1,0:T(8,128)S(1)} all-to-all(f32[8,8,128]{2,1,0:T(8,128)S(1)} %get-tuple-element.31), channel_id=1, replica_groups=mesh['z'=8,'x'=4,'yh'=2,'yl'=4,'core'=2] {'yl','core'}, dimensions={0} | all-to-all | bytes 65536 | tf_op jit(solution)/shard_map/all_to_all | solution.py:301
  69.1 1.8 lift.1
  71.0 1.4 copy-done.1
  72.4 7.8 %all_to_all.41.q_all = bf16[4,16,640]{2,1,0:T(8,128)(2,1)S(1)} all-to-all(bf16[4,16,640]{2,1,0:T(8,128)(2,1)} %copy-done.11), channel_id=1, replica_groups=mesh['z'=8,'x'=4,'yh'=2,'yl'=4,'core'=2] {'x'}, dimensions={0} | all-to-all | bytes 163840 | tf_op jit(solution)/shard_map/all_to_all | solution.py:301
  80.2 24.6 %all_to_all.42.p_all = bf16[16,16,512]{2,1,0:T(8,128)(2,1)S(1)} all-to-all(bf16[16,16,512]{2,1,0:T(8,128)(2,1)S(1)} %get-tuple-element.39), channel_id=1, replica_groups=mesh['z'=8,'x'=4,'yh'=2,'yl'=4,'core'=2] {'z','yh'}, dimensions={0} | all-to-all | bytes 524288 | tf_op jit(solution)/shard_map/all_to_all | solution.py:301
  105.3 14.0 %all_to_all.43.parts = f32[8,8,384]{2,1,0:T(8,128)S(1)} all-to-all(f32[8,8,384]{2,1,0:T(8,128)S(1)} %get-tuple-element.41), channel_id=1, replica_groups=mesh['z'=8,'x'=4,'yh'=2,'yl'=4,'core'=2] {'yl','core'}, dimensions={0} | all-to-all | bytes 196608 | tf_op jit(solution)/shard_map/all_to_all | solution.py:301
  120.1 15.8 %all_to_all.44.parts = bf16[32,16,256]{2,1,0:T(8,128)(2,1)S(1)} all-to-all(bf16[32,16,256]{2,1,0:T(8,128)(2,1)S(1)} %get-tuple-element.43), channel_id=1, replica_groups=mesh['z'=8,'x'=4,'yh'=2,'yl'=4,'core'=2] {'x','yl','core'}, dimensions={0} | all-to-all | bytes 524288 | tf_op jit(solution)/shard_map/all_to_all | solution.py:301
  135.9 1.6 back.1
  138.2 3.3 %all-to-all-start.5 = ((bf16[4,16,512]{2,1,0:T(8,128)(2,1)}), bf16[4,16,512]{2,1,0:T(8,128)(2,1)S(1)}, u32[]{:S(2)}, u32[]{:S(2)}) async-start(bf16[4,16,512]{2,1,0:T(8,128)(2,1)} %get-tuple-element.45), calls=%async_computation.5 | async-start | bytes 131072 | tf_op jit(solution)/shard_map/all_to_all | solution.py:301
  141.5 4.4 %all-to-all-done.5.q_parts = bf16[4,16,512]{2,1,0:T(8,128)(2,1)S(1)} async-done(((bf16[4,16,512]{2,1,0:T(8,128)(2,1)}), bf16[4,16,512]{2,1,0:T(8,128)(2,1)S(1)}, u32[]{:S(2)}, u32[]{:S(2)}) %all-to-all-start.5) | async-done | bytes 65568 | tf_op jit(solution)/shard_map/all_to_all | solution.py:301
  145.9 17.1 %all_to_all.45.p_parts = bf16[16,16,512]{2,1,0:T(8,128)(2,1)S(1)} all-to-all(bf16[16,16,512]{2,1,0:T(8,128)(2,1)} %copy-done.9), channel_id=1, replica_groups=mesh['z'=8,'x'=4,'yh'=2,'yl'=4,'core'=2] {'z','yh'}, dimensions={0} | all-to-all | bytes 524288 | tf_op jit(solution)/shard_map/all_to_all | solution.py:301
  165.9 6.3 %all-to-all-start.7 = ((bf16[8,48,256]{2,1,0:T(8,128)(2,1)}), bf16[8,48,256]{2,1,0:T(8,128)(2,1)S(1)}, u32[]{:S(2)}, u32[]{:S(2)}) async-start(bf16[8,48,256]{2,1,0:T(8,128)(2,1)} %copy-done.10), calls=%async_computation.8 | async-start | bytes 393216 | tf_op jit(solution)/shard_map/all_to_all | solution.py:301
  172.2 1.2 slice_bitcast_fusion
  173.4 5.3 %all-to-all-done.7.parts = bf16[8,48,256]{2,1,0:T(8,128)(2,1)S(1)} async-done(((bf16[8,48,256]{2,1,0:T(8,128)(2,1)}), bf16[8,48,256]{2,1,0:T(8,128)(2,1)S(1)}, u32[]{:S(2)}, u32[]{:S(2)}) %all-to-all-start.7) | async-done | bytes 196640 | tf_op jit(solution)/shard_map/all_to_all | solution.py:301
  178.7 1.0 copy-done.3
  183.5 2.3 %final.1 = (bf16[512,512]{1,0:T(8,128)(2,1)}, bf16[512,256]{1,0:T(8,128)(2,1)}) custom-call(bf16[8,48,256]{2,1,0:T(8,128)(2,1)S(1)} %all-to-all-done.7.parts, f32[8,128]{1,0:T(8,128)S(1)} %copy-done.20, f32[32,512]{1,0:T(8,128)S(1)} %copy-done.13, f32[1,512]{1,0:T(1,128)S(1)} %copy-done.23, f32[32,512]{1,0:T(8,128)S(1)} %get-tuple-element.40.pooled, ...), custom_call_target="tpu_custom_call" | custom-call | flops 1048576 | bytes 2514944 | tf_op jit(solution)/shard_map/final/pallas_call | solution.py:289
  (64 shorter events, 14.2 us)
Async XLA Ops:
  7.2 46.5 %copy-start = (bf16[2048,512]{1,0:T(8,128)(2,1)S(1)}, bf16[2048,512]{1,0:T(8,128)(2,1)}, u32[]{:S(2)}) copy-start(bf16[2048,512]{1,0:T(8,128)(2,1)} %weight.7) | copy-start | bytes 6291460
  7.2 134.3 %reduce-scatter.2.cloned.1.call-start = ((), (), s32[]{:S(2)}) async-start(), calls=%async_computation.9 | async-start | bytes 2506752 | tf_op jit(solution)/shard_map/reduce_scatter | solution.py:373
  22.5 30.3 %copy-start.4 = (bf16[256,1024]{1,0:T(8,128)(2,1)}, bf16[256,1024]{1,0:T(8,128)(2,1)S(1)}, u32[]{:S(2)}) copy-start(bf16[256,1024]{1,0:T(8,128)(2,1)S(1)} %all_gather.7.own) | copy-start | bytes 1572868
  22.5 30.3 %collective-permute-start.1 = (bf16[256,1024]{1,0:T(8,128)(2,1)S(1)}, bf16[256,1024]{1,0:T(8,128)(2,1)S(1)}, u32[]{:S(2)}, u32[]{:S(2)}) collective-permute-start(bf16[256,1024]{1,0:T(8,128)(2,1)S(1)} %all_gather.7.own), channel_id=1, source_target_pairs={{0,1},{1,0},{2,3},{3,2},{4,5},{5,4},{6,7},{7,6},{8,9},{9,8},{10,11... | collective-permute-start | bytes 1572872 | tf_op jit(solution)/shard_map/ppermute | solution.py:323
  47.5 9.6 %collective-permute-start = (bf16[256,1024]{1,0:T(8,128)(2,1)}, bf16[256,1024]{1,0:T(8,128)(2,1)}, u32[]{:S(2)}, u32[]{:S(2)}) collective-permute-start(bf16[256,1024]{1,0:T(8,128)(2,1)} %all_gather.6.own), channel_id=1, source_target_pairs={{0,1},{1,0},{2,3},{3,2},{4,5},{5,4},{6,7},{7,6},{8,9},{9,8},{10,11... | collective-permute-start | bytes 1572872 | tf_op jit(solution)/shard_map/ppermute | solution.py:323
  52.8 0.8 copy-start.6
  53.6 1.0 copy-start.5
  54.7 1.0 copy-start.7
  57.1 9.4 %copy-start.16 = (f32[512]{0:T(512)S(1)}, f32[512]{0:T(512)}, u32[]{:S(2)}) copy-start(f32[512]{0:T(512)} %param.11) | copy-start | bytes 6148
  57.1 9.4 %copy-start.24 = (s32[16]{0:T(128)S(1)}, s32[16]{0:T(128)}, u32[]{:S(2)}) copy-start(s32[16]{0:T(128)} %param.12) | copy-start | bytes 196
  57.1 9.4 %copy-start.25 = (s32[16]{0:T(128)S(1)}, s32[16]{0:T(128)}, u32[]{:S(2)}) copy-start(s32[16]{0:T(128)} %param.13) | copy-start | bytes 196
  57.1 9.4 %copy-start.26 = (s32[16]{0:T(128)S(1)}, s32[16]{0:T(128)}, u32[]{:S(2)}) copy-start(s32[16]{0:T(128)} %param.14) | copy-start | bytes 196
  59.1 9.4 %copy-start.2 = (f32[256,512]{1,0:T(8,128)}, f32[256,512]{1,0:T(8,128)S(1)}, u32[]{:S(2)}) copy-start(f32[256,512]{1,0:T(8,128)S(1)} %get-tuple-element.33.hidden_b) | copy-start | bytes 1572868
  71.0 1.4 copy-start.1
  72.3 46.9 %copy-start.21 = (s32[8,8]{1,0:T(8,128)S(1)}, s32[8,8]{1,0:T(8,128)}, u32[]{:S(2)}) copy-start(s32[8,8]{1,0:T(8,128)} %tile_mask.1) | copy-start | bytes 772
  120.1 21.4 %copy-start.19 = (f32[8,128]{1,0:T(8,128)}, f32[8,128]{1,0:T(8,128)S(1)}, u32[]{:S(2)}) copy-start(f32[8,128]{1,0:T(8,128)S(1)} %get-tuple-element.50.side) | copy-start | bytes 12292
  137.5 0.7 copy-start.9
  138.2 3.3 %copy-start.27 = (f32[8,128]{1,0:T(8,128)}, f32[8,128]{1,0:T(8,128)S(1)}, u32[]{:S(2)}) copy-start(f32[8,128]{1,0:T(8,128)S(1)} %get-tuple-element.44) | copy-start | bytes 12292
  138.2 7.7 %all-to-all-start.5 = ((bf16[4,16,512]{2,1,0:T(8,128)(2,1)}), bf16[4,16,512]{2,1,0:T(8,128)(2,1)S(1)}, u32[]{:S(2)}, u32[]{:S(2)}) async-start(bf16[4,16,512]{2,1,0:T(8,128)(2,1)} %get-tuple-element.45), calls=%async_computation.5 | async-start | bytes 131072 | tf_op jit(solution)/shard_map/all_to_all | solution.py:301
  141.5 37.2 %copy-start.8 = (bf16[544,256]{1,0:T(8,128)(2,1)S(1)}, bf16[544,256]{1,0:T(8,128)(2,1)}, u32[]{:S(2)}) copy-start(bf16[544,256]{1,0:T(8,128)(2,1)} %reduce-scatter.2.cloned.1.call-done.lifted) | copy-start | bytes 835588
  165.9 12.8 %all-to-all-start.7 = ((bf16[8,48,256]{2,1,0:T(8,128)(2,1)}), bf16[8,48,256]{2,1,0:T(8,128)(2,1)S(1)}, u32[]{:S(2)}, u32[]{:S(2)}) async-start(bf16[8,48,256]{2,1,0:T(8,128)(2,1)} %copy-done.10), calls=%async_computation.8 | async-start | bytes 393216 | tf_op jit(solution)/shard_map/all_to_all | solution.py:301
  178.7 1.0 copy-start.3
  179.7 0.8 copy-start.13
  180.6 0.8 copy-start.15
  (9 other events, 5.9 us)
Sparse Core Ops, SparseCore 0:
  72.5 45.8 reduce-scatter.1

commit v4 on v3

--- a/solution.py
+++ b/solution.py
@@ -33,6 +33,8 @@
 HW_DEV = 256
 WIDTH = 512
 FULL = WIDTH * NT
+CAP = 352
+CAP_PAD = 384
 
 f32 = jnp.float32
 bf16 = jnp.bfloat16
@@ -85,7 +87,7 @@
     else:
         hidden, low, payload = refs
     core = ids[0]
-    total = residual[...].astype(f32)
+    total = residual[HALF * last : HALF * (last + 1), :].astype(f32)
     for y in range(NYL):
         part = slice(y * HW_DEV, (y + 1) * HW_DEV)
         for ref, c in ((own, core), (other, 1 - core)):
@@ -102,23 +104,63 @@
         payload[...] = jnp.concatenate(rows + [jnp.zeros((6, 128), f32)], axis=0)
 
 
+def compact_kernel(q_len, p_len, context, out, dest):
+    lengths = jnp.concatenate(
+        [to_col(q_len[...].astype(f32), Q_DEV), to_col(p_len[...].astype(f32), P_DEV)], axis=0
+    )
+    by_lane = to_row(lengths, SEQS)
+    before = iota((SEQS, SEQS), 1) < iota((SEQS, SEQS), 0)
+    first = jnp.sum(jnp.where(before, by_lane, 0.0), axis=1, keepdims=True)
+    slot = (iota((SEQS, TOKENS), 1) % SEQ_LEN).astype(f32)
+    row = jnp.where(seg_mask() & (slot < lengths), first + slot + 1.0, 0.0)
+    row = jnp.sum(row, axis=0, keepdims=True) - 1.0
+    dest[...] = jnp.broadcast_to(row, (8, TOKENS))
+    chosen = (iota((CAP, TOKENS), 0).astype(f32) == row).astype(f32).astype(bf16)
+    out[...] = dot(chosen, context[...]).astype(bf16)
+
+
+def few_kernel(ids, own, other, weight, residual, dest, hidden_a, hidden_b, low_a, low_b, payload):
+    core = ids[0]
+    total = jnp.zeros((CAP, WIDTH), f32)
+    for y in range(NYL):
+        part = slice(y * HW_DEV, (y + 1) * HW_DEV)
+        for ref, c in ((own, core), (other, 1 - core)):
+            first = pl.multiple_of((y * NC + c) * HW_DEV, HW_DEV)
+            total = total + dot(ref[:, part], weight[pl.ds(first, HW_DEV), :])
+    total = jnp.concatenate([total, jnp.zeros((CAP_PAD - CAP, WIDTH), f32)], axis=0)
+    high, rest = split(total)
+    high, rest = high.astype(bf16), rest.astype(bf16)
+    rows = []
+    for b in range(TOKENS // 128):
+        part = slice(b * 128, (b + 1) * 128)
+        inner = slice(b * 128 % HALF, b * 128 % HALF + 128)
+        column = to_col(dest[0:1, part], 128)
+        chosen = (iota((128, CAP_PAD), 1).astype(f32) == column).astype(f32).astype(bf16)
+        block = dot(chosen, high) + dot(chosen, rest) + residual[part, :].astype(f32)
+        (hidden_a, hidden_b)[b * 128 // HALF][inner, :] = block
+        (low_a, low_b)[b * 128 // HALF][inner, :] = block.astype(bf16)
+        rows.append(to_row(jnp.sum(block * block, axis=1, keepdims=True), 128))
+    rows = jnp.concatenate(rows + [jnp.zeros((4, 128), f32)], axis=0)
+    payload[...] = jnp.broadcast_to(rows[None], (NT, 8, 128))
+
+
 def pool_kernel(
-    squares, q_len, p_len, position, gain, hidden_a, hidden_b, wi, inv, pooled, lift, q_pay, p_pay
+    squares, q_len, p_len, position, gain, hidden_a, hidden_b, state, lift, q_pay, p_pay
 ):
     total = jnp.sum(squares[...], axis=0)
     total = jnp.concatenate([total[b : b + 1] for b in range(TOKENS // 128)], axis=1)
     inverse = lax.rsqrt(total / FULL + EPS)
-    inv[...] = inverse
     lengths = jnp.concatenate(
         [to_col(q_len[...].astype(f32), Q_DEV), to_col(p_len[...].astype(f32), P_DEV)], axis=0
     )
     slot = (iota((SEQS, TOKENS), 1) % SEQ_LEN).astype(f32)
     weight = jnp.where(seg_mask() & (slot < lengths), 1.0 / lengths, 0.0) * inverse
-    wi[...] = weight
     value = dot(weight[:, :HALF], hidden_a[...], exact=True)
     value = value + dot(weight[:, HALF:], hidden_b[...], exact=True)
     value = value * gain[...]
-    pooled[...] = value
+    state[:SEQS, :] = weight
+    state[SEQS : 2 * SEQS, :] = value
+    state[2 * SEQS :, :] = jnp.concatenate([inverse, gain[...], jnp.zeros((6, WIDTH), f32)], axis=0)
     lift[...] = (value * gain[...]).astype(bf16)
     low = value.astype(bf16)
     where = to_col(position[...].astype(f32), Q_DEV)
@@ -139,7 +181,7 @@
         out[TOKENS:, part] = dot(pooled[...], w, ((1,), (1,))).astype(bf16)
 
 
-def score_kernel(q_all, p_all, pooled, lift, low_a, low_b, payload, position):
+def score_kernel(q_all, p_all, state, lift, low_a, low_b, payload, position):
     order = row_order()
     q_rows = dot(order, q_all[...].reshape(ROWS, WIDTH + 128))
     position[...] = q_rows[:, WIDTH:]
@@ -150,7 +192,7 @@
     q_sq = to_row(jnp.sum(q_rows * q_rows, axis=1, keepdims=True), ROWS)
     p_wide = p_cols.astype(f32)
     p_sq = jnp.sum(p_wide * p_wide, axis=1, keepdims=True)
-    own = pooled[...]
+    own = state[SEQS : 2 * SEQS, :]
     own_sq = to_row(jnp.sum(own * own, axis=1, keepdims=True), SEQS)
     cross = [dot(lift[...], low[...], ((1,), (1,))) for low in (low_a, low_b)]
     cross = jnp.sum(jnp.where(seg_mask(), jnp.concatenate(cross, axis=1), 0.0), axis=0, keepdims=True)
@@ -233,13 +275,13 @@
     p_pay[...] = d_p.astype(bf16).reshape(N_COL, P_DEV, WIDTH)
 
 
-def up_kernel(q_parts, p_parts, pooled, gain, low_a, low_b, weight, back_gain, payload):
+def up_kernel(q_parts, p_parts, state, low_a, low_b, weight, back_gain, payload):
     back = jnp.concatenate(
         [jnp.sum(q_parts[...].astype(f32), axis=0), jnp.sum(p_parts[...].astype(f32), axis=0)],
         axis=0,
     )
-    inner = to_row(jnp.sum(pooled[...] * back, axis=1, keepdims=True), SEQS)
-    scaled = back * gain[...]
+    inner = to_row(jnp.sum(state[SEQS : 2 * SEQS, :] * back, axis=1, keepdims=True), SEQS)
+    scaled = back * state[2 * SEQS + 1 : 2 * SEQS + 2, :]
     back_gain[...] = scaled
     scaled = scaled.astype(bf16)
     cross = [dot(scaled, low[...], ((1,), (1,))) for low in (low_a, low_b)]
@@ -254,7 +296,7 @@
         payload[n, SEQS:, :] = side
 
 
-def final_kernel(parts, side, wi, inv, pooled, gain, back_gain, hidden_a, hidden_b, lifted, d_res, d_ctx):
+def final_kernel(parts, side, state, back_gain, hidden_a, hidden_b, lifted, d_res, d_ctx):
     total = jnp.sum(parts[...].astype(f32), axis=0)
     rows = total[SEQS : SEQS + 8] + total[SEQS + 8 :]
     cross_back = jnp.concatenate([rows[0:1], rows[1:2]], axis=1)
@@ -262,11 +304,12 @@
     block = side[...]
     cross = jnp.concatenate([block[b : b + 1] for b in range(2, 6)], axis=1)
     ratio = to_col(inner / (block[6:7, :SEQS] + EPS), SEQS)
-    lead = LOGIT_SCALE * wi[...]
-    inverse = inv[...]
+    lead = LOGIT_SCALE * state[:SEQS, :]
+    inverse = state[2 * SEQS : 2 * SEQS + 1, :]
+    gain = state[2 * SEQS + 1 : 2 * SEQS + 2, :]
     by_token = jnp.sum(lead * (cross_back - ratio * cross), axis=0, keepdims=True)
     trail = inverse * inverse * by_token / FULL
-    d_pooled = back_gain[...] - ratio * (pooled[...] * gain[...])
+    d_pooled = back_gain[...] - ratio * (state[SEQS : 2 * SEQS, :] * gain)
     seq_up = total[:SEQS] - ratio * lifted[TOKENS:, :].astype(f32)
     both = jnp.concatenate([d_pooled, seq_up], axis=1)
     for b in range(TOKENS // 128):
@@ -279,7 +322,7 @@
         d_ctx[part, :] = (spread[:, WIDTH:] - column * lifted[part, :].astype(f32)).astype(bf16)
 
 
-VMEM = pl.BlockSpec(memory_space=pltpu.VMEM)
+VMEM = pl.BlockSpec()
 SMEM = pl.BlockSpec(memory_space=pltpu.SMEM)
 
 
@@ -291,7 +334,7 @@
         out_shape=out,
         in_specs=[SMEM] * scalars + [VMEM] * (len(args) - scalars),
         out_specs=[VMEM] * len(out),
-        compiler_params=pltpu.CompilerParams(vmem_limit_bytes=40 << 20),
+        compiler_params=pltpu.CompilerParams(vmem_limit_bytes=16 << 20),
         cost_estimate=pl.CostEstimate(flops=flops, bytes_accessed=size, transcendentals=0),
         name=name,
     )(*args)
@@ -299,6 +342,46 @@
 
 def exchange(parts, axes):
     return lax.all_to_all(parts, axes, 0, 0)
+
+
+def hidden_all(ids, out_weight, residual, context):
+    parts = []
+    for first in (0, HALF):
+        own = lax.all_gather(context[first : first + HALF], "yl", axis=1, tiled=True)
+        parts.append((own, lax.ppermute(own, "core", [(0, 1), (1, 0)])))
+    hidden_outs = [((HALF, WIDTH), f32), ((HALF, WIDTH), bf16)]
+    hidden_a, low_a, squares = call(
+        functools.partial(hidden_kernel, 0),
+        "hidden_a",
+        hidden_outs + [((8, 128), f32)],
+        (ids, *parts[0], out_weight, residual),
+        1,
+        flops=2 * HALF * 2048 * WIDTH,
+    )
+    hidden_b, low_b, squares = call(
+        functools.partial(hidden_kernel, 1),
+        "hidden_b",
+        hidden_outs + [((NT, 8, 128), f32)],
+        (ids, *parts[1], out_weight, residual, squares),
+        1,
+        flops=2 * HALF * 2048 * WIDTH,
+    )
+    return hidden_a, hidden_b, low_a, low_b, squares
+
+
+def hidden_few(ids, out_weight, residual, compacted, dest):
+    own = lax.all_gather(compacted, "yl", axis=1, tiled=True)
+    other = lax.ppermute(own, "core", [(0, 1), (1, 0)])
+    return tuple(
+        call(
+            few_kernel,
+            "hidden",
+            [((HALF, WIDTH), f32)] * 2 + [((HALF, WIDTH), bf16)] * 2 + [((NT, 8, 128), f32)],
+            (ids, own, other, out_weight, residual, dest),
+            1,
+            flops=2 * CAP * 2048 * WIDTH,
+        )
+    )
 
 
 def body(
@@ -317,36 +400,26 @@
     ).astype(i32)
     gain = final_norm_weight.reshape(1, WIDTH)
 
-    parts = []
-    for first in (0, HALF):
-        own = lax.all_gather(context[first : first + HALF], "yl", axis=1, tiled=True)
-        parts.append((own, lax.ppermute(own, "core", [(0, 1), (1, 0)])))
-    hidden_outs = [((HALF, WIDTH), f32), ((HALF, WIDTH), bf16)]
-    hidden_a, low_a, squares = call(
-        functools.partial(hidden_kernel, False),
-        "hidden_a",
-        hidden_outs + [((8, 128), f32)],
-        (ids, *parts[0], out_weight, residual[:HALF]),
-        1,
-        flops=2 * HALF * 2048 * WIDTH,
-    )
-    hidden_b, low_b, squares = call(
-        functools.partial(hidden_kernel, True),
-        "hidden_b",
-        hidden_outs + [((NT, 8, 128), f32)],
-        (ids, *parts[1], out_weight, residual[HALF:], squares),
-        1,
-        flops=2 * HALF * 2048 * WIDTH,
+    compacted, dest = call(
+        compact_kernel,
+        "compact",
+        [((CAP, HW_DEV), bf16), ((8, TOKENS), f32)],
+        (query_lengths.reshape(1, Q_DEV), passage_lengths.reshape(1, P_DEV), context),
+        flops=2 * CAP * TOKENS * HW_DEV,
+    )
+    used = jnp.sum(jnp.concatenate([query_lengths, passage_lengths]))
+    hidden_a, hidden_b, low_a, low_b, squares = lax.cond(
+        used <= CAP,
+        functools.partial(hidden_few, ids, out_weight, residual, compacted, dest),
+        functools.partial(hidden_all, ids, out_weight, residual, context),
     )
     squares = exchange(squares, T)
 
-    wi, inv, pooled, lift, q_pay, p_pay = call(
+    state, lift, q_pay, p_pay = call(
         pool_kernel,
         "pool",
         [
-            ((SEQS, TOKENS), f32),
-            ((1, TOKENS), f32),
-            ((SEQS, WIDTH), f32),
+            ((2 * SEQS + 8, WIDTH), f32),
             ((SEQS, WIDTH), bf16),
             ((N_ROW, Q_DEV, WIDTH + 128), bf16),
             ((N_COL, P_DEV, WIDTH), bf16),
@@ -369,16 +442,16 @@
         (low_a, low_b, lift, out_weight),
         flops=2 * TOKENS * 2048 * WIDTH,
     )
-    p_pay, lifted = lax.optimization_barrier((p_pay, lifted))
-    lifted = lax.psum_scatter(lifted, T, scatter_dimension=1, tiled=True)
     p_all = exchange(p_pay, COL)
 
     payload, position = call(
         score_kernel,
         "score",
         [((NT, SHARE, COLS + 128), f32), ((ROWS, 128), f32)],
-        (q_all, p_all, pooled, lift, low_a, low_b),
-    )
+        (q_all, p_all, state, lift, low_a, low_b),
+    )
+    payload, lifted = lax.optimization_barrier((payload, lifted))
+    lifted = lax.psum_scatter(lifted, T, scatter_dimension=1, tiled=True)
     payload, side = call(
         softmax_kernel,
         "softmax",
@@ -395,19 +468,19 @@
     )
     query_loss = loss[0, :PAIR]
     q_back = exchange(q_pay, ROW)
-    p_pay, lifted = lax.optimization_barrier((p_pay, lifted))
     p_back = exchange(p_pay, COL)
     back_gain, payload = call(
         up_kernel,
         "up",
         [((SEQS, WIDTH), f32), ((NT, SEQS + 16, HW_DEV), bf16)],
-        (q_back, p_back, pooled, gain, low_a, low_b, out_weight),
-    )
+        (q_back, p_back, state, low_a, low_b, out_weight),
+    )
+    payload, lifted = lax.optimization_barrier((payload, lifted))
     residual_gradient, d_context = call(
         final_kernel,
         "final",
         [((TOKENS, WIDTH), bf16), ((TOKENS, HW_DEV), bf16)],
-        (exchange(payload, T), side, wi, inv, pooled, gain, back_gain, hidden_a, hidden_b, lifted),
+        (exchange(payload, T), side, state, back_gain, hidden_a, hidden_b, lifted),
     )
     return (query_loss, residual_gradient, d_context)
 

time: 194 us -> 169 us (0.87)
  blocking collectives: 116 us -> 86.2 us
  local copies, waits for them, and re-layouts: 17 us -> 2.81 us
  Pallas kernels: 12 us -> 18.5 us
  waiting for transfers between devices: 9.7 us -> 15.3 us
  starting transfers between devices: 24.1 us -> 27.2 us
  other arithmetic: 0.08 us -> 2.77 us
    all_to_all x6, blocking collectives: 86.8 us -> 70 us  [exchange(): return lax.all_to_all(parts, axes, 0, 0)]
    all_gather x2 -> x1, blocking collectives: 28.8 us -> 16.2 us  [hidden_few(): own = lax.all_gather(compacted, 'yl', axis=1, tiled=True)]
    unnamed x56 -> x22, local copies, waits for them, and re-layouts: 13.6 us -> 2.29 us
    all_to_all x2, starting transfers between devices: 9.58 us -> 17.4 us  [exchange(): return lax.all_to_all(parts, axes, 0, 0)]
    pallas_call x9, Pallas kernels: 12 us -> 18.5 us  [call(): pl.pallas_call(kernel, out_shape=out, in_specs=[SMEM] * scalars + [VMEM]...]
    ppermute x2 -> x1, starting transfers between devices: 14.5 us -> 9.79 us  [hidden_few(): other = lax.ppermute(own, 'core', [(0, 1), (1, 0)])]
    all_to_all x2, waiting for transfers between devices: 9.66 us -> 13.5 us  [exchange(): return lax.all_to_all(parts, axes, 0, 0)]
    reduce_sum x0 -> x2, other arithmetic: none -> 2.69 us  [body(): used = jnp.sum(jnp.concatenate([query_lengths, passage_lengths]))]
  transfers between devices with their start and end apart: 5 -> 4, of which waited for: 2 -> 3; matrix products, arithmetic and copies ran while one was open for 1% -> 0% of each run, Pallas kernels for 2% -> 5%
where the time goes in v4:
time: 169 us; the launch traced here: 168 us
  blocking collectives  86.2 us (51%)
  starting transfers between devices  27.2 us (16%)
  Pallas kernels  18.5 us (11%)
  between operations  15.5 us (9%)
  waiting for transfers between devices  15.3 us (9%)
  local copies, waits for them, and re-layouts  2.81 us (2%)
  other arithmetic  2.77 us (2%)
    all_to_all x6, blocking collectives, exchange(): return lax.all_to_all(parts, axes, 0, 0)  70 us
    pallas_call x9, Pallas kernels, call(): pl.pallas_call(kernel, out_shape=out, in_specs=[SMEM] * scalars + [VMEM]...  18.5 us
    all_to_all x2, starting transfers between devices, exchange(): return lax.all_to_all(parts, axes, 0, 0)  17.4 us
    all_gather x1, blocking collectives, hidden_few(): own = lax.all_gather(compacted, 'yl', axis=1, tiled=True)  16.2 us
    all_to_all x2, waiting for transfers between devices, exchange(): return lax.all_to_all(parts, axes, 0, 0)  13.5 us
    ppermute x1, starting transfers between devices, hidden_few(): other = lax.ppermute(own, 'core', [(0, 1), (1, 0)])  9.79 us
  transfers between devices with their start and end apart: 4, of which 3 were waited for; matrix products, arithmetic and copies ran while one was open for 0% of the time, Pallas kernels for 5%

profile of v4, /device:TPU:1, one launch (start us, length us, event | category | flops | bytes accessed | tf_op | source)
XLA Modules:
  0.0 168.3 jit_solution(7572800327225134374)
XLA Ops:
  7.2 1.3 reduce_sum.18
  8.5 1.4 reduce_sum.14
  12.5 1.4 compact.1
  14.0 31.2 %conditional.1 = ((f32[256,512]{1,0:T(8,128)S(1)}, f32[256,512]{1,0:T(8,128)S(1)}, bf16[256,512]{1,0:T(8,128)(2,1)S(1)}, bf16[256,512]{1,0:T(8,128)(2,1)S(1)}, f32[8,8,128]{2,1,0:T(8,128)S(1)})) conditional(s32[]{:T(128)} %convert_element_type.3, (bf16[512,256]{1,0:T(8,128)(2,1)}, s32[4]{0:T(128)S(1)}, bf16[2048,512]{1,0:T(8,128)(2,1)}, ...), branch_computations={%region_2.0_spmd, %region_3.0_spmd} | conditional | flops 1073741824 | bytes 25469144 | solution.py:411
  14.1 16.2 %all_gather.8.own = bf16[352,1024]{1,0:T(8,128)(2,1)S(1)} all-gather(bf16[352,256]{1,0:T(8,128)(2,1)S(1)} %get-tuple-element.29), channel_id=1, replica_groups=mesh['z'=8,'x'=4,'yh'=2,'yl'=4,'core'=2] {'yl'}, dimensions={1}, use_global_device_ids=true | all-gather | bytes 901120 | tf_op jit(solution)/shard_map/cond/branch_1_fun/all_gather | solution.py:373
  30.3 9.8 %collective-permute-start = (bf16[352,1024]{1,0:T(8,128)(2,1)S(1)}, bf16[352,1024]{1,0:T(8,128)(2,1)S(1)}, u32[]{:S(2)}, u32[]{:S(2)}) collective-permute-start(bf16[352,1024]{1,0:T(8,128)(2,1)S(1)} %all_gather.8.own), channel_id=1, source_target_pairs={{0,1},{1,0},{2,3},{3,2},{4,5},{5,4},{6,7},{7,6},{8,9},{9,8},{10,11... | collective-permute-start | bytes 2162696 | tf_op jit(solution)/shard_map/cond/branch_1_fun/ppermute | solution.py:374
  40.1 1.8 %collective-permute-done.other = bf16[352,1024]{1,0:T(8,128)(2,1)S(1)} collective-permute-done((bf16[352,1024]{1,0:T(8,128)(2,1)S(1)}, bf16[352,1024]{1,0:T(8,128)(2,1)S(1)}, u32[]{:S(2)}, u32[]{:S(2)}) %collective-permute-start) | collective-permute-done | bytes 720928 | tf_op jit(solution)/shard_map/cond/branch_1_fun/ppermute | solution.py:374
  41.9 3.4 %hidden.1 = (f32[256,512]{1,0:T(8,128)S(1)}, f32[256,512]{1,0:T(8,128)S(1)}, bf16[256,512]{1,0:T(8,128)(2,1)S(1)}, bf16[256,512]{1,0:T(8,128)(2,1)S(1)}, f32[8,8,128]{2,1,0:T(8,128)S(1)}) custom-call(s32[4]{0:T(128)S(1)} %get-tuple-element.28.ids, bf16[352,1024]{1,0:T(8,128)(2,1)S(1)} %all_gather.8.own, bf16[352,1024]{1,0:T(8,128)(2,1)S(1)} %collective-permute-done.other, ...), custom_call_target="tpu_custom_call" | custom-call | flops 738197504 | bytes 5685264 | tf_op jit(solution)/shard_map/cond/branch_1_fun/hidden/pallas_call | solution.py:332
  45.2 7.7 %all_to_all.40.squares = f32[8,8,128]{2,1,0:T(8,128)S(1)} all-to-all(f32[8,8,128]{2,1,0:T(8,128)S(1)} %get-tuple-element.64), channel_id=1, replica_groups=mesh['z'=8,'x'=4,'yh'=2,'yl'=4,'core'=2] {'yl','core'}, dimensions={0} | all-to-all | bytes 65536 | tf_op jit(solution)/shard_map/all_to_all | solution.py:344
  53.0 1.5 pool.1
  54.5 6.9 %all_to_all.41.q_all = bf16[4,16,640]{2,1,0:T(8,128)(2,1)S(1)} all-to-all(bf16[4,16,640]{2,1,0:T(8,128)(2,1)S(1)} %get-tuple-element.67), channel_id=1, replica_groups=mesh['z'=8,'x'=4,'yh'=2,'yl'=4,'core'=2] {'x'}, dimensions={0} | all-to-all | bytes 163840 | tf_op jit(solution)/shard_map/all_to_all | solution.py:344
  61.4 12.2 %all-to-all-start.2 = ((bf16[16,16,512]{2,1,0:T(8,128)(2,1)}), bf16[16,16,512]{2,1,0:T(8,128)(2,1)S(1)}, u32[]{:S(2)}, u32[]{:S(2)}) async-start(bf16[16,16,512]{2,1,0:T(8,128)(2,1)} %get-tuple-element.68), calls=%async_computation.2 | async-start | bytes 524288 | tf_op jit(solution)/shard_map/all_to_all | solution.py:344
  73.6 4.8 %lift.1 = bf16[544,2048]{1,0:T(8,128)(2,1)} custom-call(bf16[256,512]{1,0:T(8,128)(2,1)S(1)} %get-tuple-element.71.low_a, bf16[256,512]{1,0:T(8,128)(2,1)S(1)} %get-tuple-element.72.low_b, bf16[32,512]{1,0:T(8,128)(2,1)S(1)} %get-tuple-element.70.lift.pooled, bf16[2048,512]{1,0:T(8,128)(2,1)} %weight.3), custom_call_target="tpu_custom_call" | custom-call | flops 1073741824 | bytes 4882432 | tf_op jit(solution)/shard_map/lift/pallas_call | solution.py:332
  78.4 7.6 %all-to-all-done.2.p_all = bf16[16,16,512]{2,1,0:T(8,128)(2,1)S(1)} async-done(((bf16[16,16,512]{2,1,0:T(8,128)(2,1)}), bf16[16,16,512]{2,1,0:T(8,128)(2,1)S(1)}, u32[]{:S(2)}, u32[]{:S(2)}) %all-to-all-start.2) | async-done | bytes 262176 | tf_op jit(solution)/shard_map/all_to_all | solution.py:344
  86.5 12.3 %all_to_all.42.parts = f32[8,8,384]{2,1,0:T(8,128)S(1)} all-to-all(f32[8,8,384]{2,1,0:T(8,128)S(1)} %get-tuple-element.74), channel_id=1, replica_groups=mesh['z'=8,'x'=4,'yh'=2,'yl'=4,'core'=2] {'yl','core'}, dimensions={0} | all-to-all | bytes 196608 | tf_op jit(solution)/shard_map/all_to_all | solution.py:344
  99.6 19.2 %all_to_all.43.parts = bf16[32,16,256]{2,1,0:T(8,128)(2,1)S(1)} all-to-all(bf16[32,16,256]{2,1,0:T(8,128)(2,1)S(1)} %get-tuple-element.76), channel_id=1, replica_groups=mesh['z'=8,'x'=4,'yh'=2,'yl'=4,'core'=2] {'x','yl','core'}, dimensions={0} | all-to-all | bytes 524288 | tf_op jit(solution)/shard_map/all_to_all | solution.py:344
  118.8 1.1 back.1
  119.9 7.8 %all_to_all.44.q_parts = bf16[4,16,512]{2,1,0:T(8,128)(2,1)S(1)} all-to-all(bf16[4,16,512]{2,1,0:T(8,128)(2,1)S(1)} %get-tuple-element.78), channel_id=1, replica_groups=mesh['z'=8,'x'=4,'yh'=2,'yl'=4,'core'=2] {'x'}, dimensions={0} | all-to-all | bytes 131072 | tf_op jit(solution)/shard_map/all_to_all | solution.py:344
  127.7 16.1 %all_to_all.45.p_parts = bf16[16,16,512]{2,1,0:T(8,128)(2,1)S(1)} all-to-all(bf16[16,16,512]{2,1,0:T(8,128)(2,1)S(1)} %get-tuple-element.79), channel_id=1, replica_groups=mesh['z'=8,'x'=4,'yh'=2,'yl'=4,'core'=2] {'z','yh'}, dimensions={0} | all-to-all | bytes 524288 | tf_op jit(solution)/shard_map/all_to_all | solution.py:344
  143.8 1.6 up.1
  145.3 5.2 %all-to-all-start.7 = ((bf16[8,48,256]{2,1,0:T(8,128)(2,1)}), bf16[8,48,256]{2,1,0:T(8,128)(2,1)S(1)}, u32[]{:S(2)}, u32[]{:S(2)}) async-start(bf16[8,48,256]{2,1,0:T(8,128)(2,1)} %get-tuple-element.82), calls=%async_computation.8 | async-start | bytes 393216 | tf_op jit(solution)/shard_map/all_to_all | solution.py:344
  151.0 6.0 %all-to-all-done.7.parts = bf16[8,48,256]{2,1,0:T(8,128)(2,1)S(1)} async-done(((bf16[8,48,256]{2,1,0:T(8,128)(2,1)}), bf16[8,48,256]{2,1,0:T(8,128)(2,1)S(1)}, u32[]{:S(2)}, u32[]{:S(2)}) %all-to-all-start.7) | async-done | bytes 196640 | tf_op jit(solution)/shard_map/all_to_all | solution.py:344
  157.0 1.0 copy-done
  157.9 3.5 %final.1 = (bf16[512,512]{1,0:T(8,128)(2,1)}, bf16[512,256]{1,0:T(8,128)(2,1)}) custom-call(bf16[8,48,256]{2,1,0:T(8,128)(2,1)S(1)} %all-to-all-done.7.parts, f32[8,128]{1,0:T(8,128)S(1)} %get-tuple-element.83.side, f32[72,512]{1,0:T(8,128)S(1)} %get-tuple-element.69.state, f32[32,512]{1,0:T(8,128)S(1)} %get-tuple-element.84.back_gain, ...), custom_call_target="tpu_custom_call" | custom-call | flops 1048576 | bytes 2527232 | tf_op jit(solution)/shard_map/final/pallas_call | solution.py:332
  (28 shorter events, 3.2 us)
Async XLA Ops:
  11.2 0.7 copy-start.3
  11.8 0.7 copy-start.5
  14.0 38.9 %copy-start.2 = (f32[512]{0:T(512)S(1)}, f32[512]{0:T(512)}, u32[]{:S(2)}) copy-start(f32[512]{0:T(512)} %param.13) | copy-start | bytes 6148
  14.0 38.9 %copy-start.4 = (s32[16]{0:T(128)S(1)}, s32[16]{0:T(128)}, u32[]{:S(2)}) copy-start(s32[16]{0:T(128)} %param.14) | copy-start | bytes 196
  14.0 38.9 %copy-start.6 = (s32[16]{0:T(128)S(1)}, s32[16]{0:T(128)}, u32[]{:S(2)}) copy-start(s32[16]{0:T(128)} %param.15) | copy-start | bytes 196
  14.0 38.9 %copy-start.7 = (s32[16]{0:T(128)S(1)}, s32[16]{0:T(128)}, u32[]{:S(2)}) copy-start(s32[16]{0:T(128)} %param.16) | copy-start | bytes 196
  30.3 11.6 %collective-permute-start = (bf16[352,1024]{1,0:T(8,128)(2,1)S(1)}, bf16[352,1024]{1,0:T(8,128)(2,1)S(1)}, u32[]{:S(2)}, u32[]{:S(2)}) collective-permute-start(bf16[352,1024]{1,0:T(8,128)(2,1)S(1)} %all_gather.8.own), channel_id=1, source_target_pairs={{0,1},{1,0},{2,3},{3,2},{4,5},{5,4},{6,7},{7,6},{8,9},{9,8},{10,11... | collective-permute-start | bytes 2162696 | tf_op jit(solution)/shard_map/cond/branch_1_fun/ppermute | solution.py:374
  45.2 33.2 %copy-start.11 = (f32[256,512]{1,0:T(8,128)}, f32[256,512]{1,0:T(8,128)S(1)}, u32[]{:S(2)}) copy-start(f32[256,512]{1,0:T(8,128)S(1)} %get-tuple-element.65.hidden_a) | copy-start | bytes 1572868
  45.2 40.8 %copy-start.12 = (f32[256,512]{1,0:T(8,128)}, f32[256,512]{1,0:T(8,128)S(1)}, u32[]{:S(2)}) copy-start(f32[256,512]{1,0:T(8,128)S(1)} %get-tuple-element.66.hidden_b) | copy-start | bytes 1572868
  61.4 24.6 %all-to-all-start.2 = ((bf16[16,16,512]{2,1,0:T(8,128)(2,1)}), bf16[16,16,512]{2,1,0:T(8,128)(2,1)S(1)}, u32[]{:S(2)}, u32[]{:S(2)}) async-start(bf16[16,16,512]{2,1,0:T(8,128)(2,1)} %get-tuple-element.68), calls=%async_computation.2 | async-start | bytes 524288 | tf_op jit(solution)/shard_map/all_to_all | solution.py:344
  73.6 71.8 %reduce-scatter.2.cloned.1.call-start = ((), (), s32[]{:S(2)}) async-start(), calls=%async_computation.9 | async-start | bytes 2506752 | tf_op jit(solution)/shard_map/reduce_scatter | solution.py:454
  78.4 20.3 %copy-start.1 = (s32[8,8]{1,0:T(8,128)S(1)}, s32[8,8]{1,0:T(8,128)}, u32[]{:S(2)}) copy-start(s32[8,8]{1,0:T(8,128)} %tile_mask.1) | copy-start | bytes 772
  86.4 57.3 %copy-start.8 = (bf16[2048,512]{1,0:T(8,128)(2,1)S(1)}, bf16[2048,512]{1,0:T(8,128)(2,1)}, u32[]{:S(2)}) copy-start(bf16[2048,512]{1,0:T(8,128)(2,1)} %weight.3) | copy-start | bytes 6291460
  145.3 11.6 %all-to-all-start.7 = ((bf16[8,48,256]{2,1,0:T(8,128)(2,1)}), bf16[8,48,256]{2,1,0:T(8,128)(2,1)S(1)}, u32[]{:S(2)}, u32[]{:S(2)}) async-start(bf16[8,48,256]{2,1,0:T(8,128)(2,1)} %get-tuple-element.82), calls=%async_computation.8 | async-start | bytes 393216 | tf_op jit(solution)/shard_map/all_to_all | solution.py:344
  157.0 1.0 copy-start
Sparse Core Ops, SparseCore 0:
  86.6 40.2 reduce-scatter.1

commit v5 on v4

--- a/solution.py
+++ b/solution.py
@@ -104,11 +104,12 @@
         payload[...] = jnp.concatenate(rows + [jnp.zeros((6, 128), f32)], axis=0)
 
 
-def compact_kernel(q_len, p_len, context, out, dest):
+def compact_kernel(q_len, p_len, context, out, dest, fits):
     lengths = jnp.concatenate(
         [to_col(q_len[...].astype(f32), Q_DEV), to_col(p_len[...].astype(f32), P_DEV)], axis=0
     )
     by_lane = to_row(lengths, SEQS)
+    fits[0, 0] = (jnp.sum(by_lane) <= CAP).astype(i32)
     before = iota((SEQS, SEQS), 1) < iota((SEQS, SEQS), 0)
     first = jnp.sum(jnp.where(before, by_lane, 0.0), axis=1, keepdims=True)
     slot = (iota((SEQS, TOKENS), 1) % SEQ_LEN).astype(f32)
@@ -119,7 +120,7 @@
     out[...] = dot(chosen, context[...]).astype(bf16)
 
 
-def few_kernel(ids, own, other, weight, residual, dest, hidden_a, hidden_b, low_a, low_b, payload):
+def few_kernel(ids, own, other, weight, residual, dest, hidden, low, payload):
     core = ids[0]
     total = jnp.zeros((CAP, WIDTH), f32)
     for y in range(NYL):
@@ -133,19 +134,18 @@
     rows = []
     for b in range(TOKENS // 128):
         part = slice(b * 128, (b + 1) * 128)
-        inner = slice(b * 128 % HALF, b * 128 % HALF + 128)
         column = to_col(dest[0:1, part], 128)
         chosen = (iota((128, CAP_PAD), 1).astype(f32) == column).astype(f32).astype(bf16)
         block = dot(chosen, high) + dot(chosen, rest) + residual[part, :].astype(f32)
-        (hidden_a, hidden_b)[b * 128 // HALF][inner, :] = block
-        (low_a, low_b)[b * 128 // HALF][inner, :] = block.astype(bf16)
+        hidden[part, :] = block
+        low[part, :] = block.astype(bf16)
         rows.append(to_row(jnp.sum(block * block, axis=1, keepdims=True), 128))
     rows = jnp.concatenate(rows + [jnp.zeros((4, 128), f32)], axis=0)
     payload[...] = jnp.broadcast_to(rows[None], (NT, 8, 128))
 
 
 def pool_kernel(
-    squares, q_len, p_len, position, gain, hidden_a, hidden_b, state, lift, q_pay, p_pay
+    squares, q_len, p_len, position, gain, hidden, state, lift, q_pay, p_pay
 ):
     total = jnp.sum(squares[...], axis=0)
     total = jnp.concatenate([total[b : b + 1] for b in range(TOKENS // 128)], axis=1)
@@ -155,9 +155,7 @@
     )
     slot = (iota((SEQS, TOKENS), 1) % SEQ_LEN).astype(f32)
     weight = jnp.where(seg_mask() & (slot < lengths), 1.0 / lengths, 0.0) * inverse
-    value = dot(weight[:, :HALF], hidden_a[...], exact=True)
-    value = value + dot(weight[:, HALF:], hidden_b[...], exact=True)
-    value = value * gain[...]
+    value = dot(weight, hidden[...], exact=True) * gain[...]
     state[:SEQS, :] = weight
     state[SEQS : 2 * SEQS, :] = value
     state[2 * SEQS :, :] = jnp.concatenate([inverse, gain[...], jnp.zeros((6, WIDTH), f32)], axis=0)
@@ -172,16 +170,12 @@
     p_pay[...] = jnp.broadcast_to(low[None, Q_DEV:], (N_COL, P_DEV, WIDTH))
 
 
-def lift_kernel(low_a, low_b, pooled, weight, out):
-    for n in range(NT):
-        part = slice(n * HW_DEV, (n + 1) * HW_DEV)
-        w = weight[part, :]
-        out[:HALF, part] = dot(low_a[...], w, ((1,), (1,))).astype(bf16)
-        out[HALF:TOKENS, part] = dot(low_b[...], w, ((1,), (1,))).astype(bf16)
-        out[TOKENS:, part] = dot(pooled[...], w, ((1,), (1,))).astype(bf16)
-
-
-def score_kernel(q_all, p_all, state, lift, low_a, low_b, payload, position):
+def lift_kernel(low, pooled, weight, out):
+    out[:TOKENS, :] = dot(low[...], weight[...], ((1,), (1,))).astype(bf16)
+    out[TOKENS:, :] = dot(pooled[...], weight[...], ((1,), (1,))).astype(bf16)
+
+
+def score_kernel(q_all, p_all, state, lift, low, payload, position):
     order = row_order()
     q_rows = dot(order, q_all[...].reshape(ROWS, WIDTH + 128))
     position[...] = q_rows[:, WIDTH:]
@@ -194,8 +188,8 @@
     p_sq = jnp.sum(p_wide * p_wide, axis=1, keepdims=True)
     own = state[SEQS : 2 * SEQS, :]
     own_sq = to_row(jnp.sum(own * own, axis=1, keepdims=True), SEQS)
-    cross = [dot(lift[...], low[...], ((1,), (1,))) for low in (low_a, low_b)]
-    cross = jnp.sum(jnp.where(seg_mask(), jnp.concatenate(cross, axis=1), 0.0), axis=0, keepdims=True)
+    cross = dot(lift[...], low[...], ((1,), (1,)))
+    cross = jnp.sum(jnp.where(seg_mask(), cross, 0.0), axis=0, keepdims=True)
     rows = [to_row(p_sq[b * 128 : (b + 1) * 128], 128) for b in range(COLS // 128)]
     rows += [cross[:, b * 128 : (b + 1) * 128] for b in range(TOKENS // 128)]
     rows.append(jnp.concatenate([own_sq, jnp.zeros((1, 128 - SEQS), f32)], axis=1))
@@ -247,56 +241,74 @@
     )
 
 
-def back_kernel(ids, parts, position, q_all, p_all, loss, q_pay, p_pay):
+def query_kernel(ids, parts, q_all, p_all, payload, terms_out):
+    x = ids[3]
+    value = parts[...].astype(f32)
+    order = row_order()
+    terms = value[:, :SHARE, :].reshape(ROWS, COLS).astype(bf16)
+    terms = dot(order, terms, ((0,), (0,)))
+    sums = value[:, SHARE:, :128].reshape(ROWS, 128).astype(bf16)
+    sums = dot(order, sums, ((0,), (0,)))
+    low = terms.astype(bf16)
+    terms_out[...] = low
+    at_pos = at_positive(q_all[...].reshape(ROWS, WIDTH + 128)[:, WIDTH:].astype(f32), x)
+    p_cols = p_all[...].reshape(COLS, WIDTH)
+    others = dot(jnp.where(at_pos, 0.0, terms).astype(bf16), p_cols)
+    positive = dot(jnp.where(at_pos, terms, 0.0).astype(bf16), p_cols)
+    payload[:, :Q_DEV, :] = others.astype(bf16).reshape(N_ROW, Q_DEV, WIDTH)
+    payload[:, Q_DEV : 2 * Q_DEV, :] = positive.astype(bf16).reshape(N_ROW, Q_DEV, WIDTH)
+    sums = jnp.concatenate([sums[k * Q_DEV : (k + 1) * Q_DEV] for k in range(N_ROW)], axis=1)
+    payload[:, 2 * Q_DEV :, :] = jnp.broadcast_to(sums.astype(bf16)[None], (N_ROW, Q_DEV, WIDTH))
+
+
+def passage_kernel(ids, parts, terms, q_all, loss, back_q, payload):
     me, x = ids[1], ids[3]
-    total = jnp.zeros((NT, SHARE, 128), f32)
-    for k in range(N_ROW):
-        total = total + parts[k * NT : (k + 1) * NT, :, :128].astype(f32)[:, SHARE:, :]
-    total = total.reshape(ROWS, 128)
+    total = jnp.sum(parts[...].astype(f32), axis=0)
+    sums = total[2 * Q_DEV :]
+    sums = jnp.concatenate([sums[:, k * 128 : (k + 1) * 128] for k in range(N_ROW)], axis=0)
     lane = iota((ROWS, 128), 1)
     others, positive, logit = (
-        jnp.sum(jnp.where(lane // 3 == i, total, 0.0), axis=1, keepdims=True) for i in range(3)
+        jnp.sum(jnp.where(lane // 3 == i, sums, 0.0), axis=1, keepdims=True) for i in range(3)
     )
     denom = others + positive
     losses = jnp.log(denom) - logit
-    row = me * SHARE + x * PAIR + iota((ROWS, 128), 1)
-    mine = (iota((ROWS, 128), 0) == row) & (lane < PAIR)
+    mine = (iota((ROWS, 128), 0) == x * Q_DEV + me * PAIR + lane) & (lane < PAIR)
     loss[...] = jnp.broadcast_to(
         jnp.sum(jnp.where(mine, losses, 0.0), axis=0, keepdims=True), loss.shape
     )
-    first = pl.multiple_of(x * NT, NT)
-    terms = parts[pl.ds(first, NT)].astype(f32)[:, :SHARE, :].reshape(ROWS, COLS)
     factor = LOSS_SCALE / denom
-    terms = terms * jnp.where(at_positive(position[...], x), -factor * others, factor)
-    terms = dot(row_order(), terms.astype(bf16), ((0,), (0,))).astype(bf16)
-    d_q = dot(terms, p_all[...].reshape(COLS, WIDTH))
-    q_pay[...] = d_q.astype(bf16).reshape(N_ROW, Q_DEV, WIDTH)
-    d_p = dot(terms, q_all[...].reshape(ROWS, WIDTH + 128)[:, :WIDTH], ((0,), (0,)))
-    p_pay[...] = d_p.astype(bf16).reshape(N_COL, P_DEV, WIDTH)
-
-
-def up_kernel(q_parts, p_parts, state, low_a, low_b, weight, back_gain, payload):
-    back = jnp.concatenate(
-        [jnp.sum(q_parts[...].astype(f32), axis=0), jnp.sum(p_parts[...].astype(f32), axis=0)],
-        axis=0,
-    )
+    own_factor = jnp.zeros((Q_DEV, 1), f32)
+    own_others = jnp.zeros((Q_DEV, 1), f32)
+    for k in range(N_ROW):
+        rows = slice(k * Q_DEV, (k + 1) * Q_DEV)
+        own_factor = jnp.where(x == k, factor[rows], own_factor)
+        own_others = jnp.where(x == k, others[rows], own_others)
+    back_q[...] = own_factor * (total[:Q_DEV] - own_others * total[Q_DEV : 2 * Q_DEV])
+    q_wide = q_all[...].reshape(ROWS, WIDTH + 128)
+    at_pos = at_positive(q_wide[:, WIDTH:].astype(f32), x)
+    value = terms[...].astype(f32) * jnp.where(at_pos, -factor * others, factor)
+    d_p = dot(value.astype(bf16), q_wide[:, :WIDTH], ((0,), (0,)))
+    payload[...] = d_p.astype(bf16).reshape(N_COL, P_DEV, WIDTH)
+
+
+def up_kernel(back_q, p_parts, state, low, weight, back_gain, payload):
+    back = jnp.concatenate([back_q[...], jnp.sum(p_parts[...].astype(f32), axis=0)], axis=0)
     inner = to_row(jnp.sum(state[SEQS : 2 * SEQS, :] * back, axis=1, keepdims=True), SEQS)
     scaled = back * state[2 * SEQS + 1 : 2 * SEQS + 2, :]
     back_gain[...] = scaled
     scaled = scaled.astype(bf16)
-    cross = [dot(scaled, low[...], ((1,), (1,))) for low in (low_a, low_b)]
-    cross = jnp.sum(jnp.where(seg_mask(), jnp.concatenate(cross, axis=1), 0.0), axis=0, keepdims=True)
+    cross = dot(scaled, low[...], ((1,), (1,)))
+    cross = jnp.sum(jnp.where(seg_mask(), cross, 0.0), axis=0, keepdims=True)
     inner = jnp.concatenate([inner, jnp.zeros((1, HW_DEV - SEQS), f32)], axis=1)
-    rows = jnp.concatenate([cross[:, :HW_DEV], cross[:, HW_DEV:], inner, jnp.zeros((5, HW_DEV), f32)], axis=0)
-    high, low = split(rows)
-    side = jnp.concatenate([high, low], axis=0).astype(bf16)
+    rows = [cross[:, :HW_DEV], cross[:, HW_DEV:], inner, jnp.zeros((5, HW_DEV), f32)]
+    side = jnp.concatenate(split(jnp.concatenate(rows, axis=0)), axis=0).astype(bf16)
     for n in range(NT):
         w = weight[n * HW_DEV : (n + 1) * HW_DEV, :]
         payload[n, :SEQS, :] = dot(scaled, w, ((1,), (1,))).astype(bf16)
         payload[n, SEQS:, :] = side
 
 
-def final_kernel(parts, side, state, back_gain, hidden_a, hidden_b, lifted, d_res, d_ctx):
+def final_kernel(parts, side, state, back_gain, hidden, lifted, d_res, d_ctx):
     total = jnp.sum(parts[...].astype(f32), axis=0)
     rows = total[SEQS : SEQS + 8] + total[SEQS + 8 :]
     cross_back = jnp.concatenate([rows[0:1], rows[1:2]], axis=1)
@@ -314,26 +326,34 @@
     both = jnp.concatenate([d_pooled, seq_up], axis=1)
     for b in range(TOKENS // 128):
         part = slice(b * 128, (b + 1) * 128)
-        hidden = (hidden_a, hidden_b)[b * 128 // HALF]
-        inner_part = slice(b * 128 % HALF, b * 128 % HALF + 128)
         spread = dot(lead[:, part], both, ((0,), (0,)), exact=True)
         column = to_col(trail[:, part], 128)
-        d_res[part, :] = (spread[:, :WIDTH] - column * hidden[inner_part, :]).astype(bf16)
+        d_res[part, :] = (spread[:, :WIDTH] - column * hidden[part, :]).astype(bf16)
         d_ctx[part, :] = (spread[:, WIDTH:] - column * lifted[part, :].astype(f32)).astype(bf16)
 
 
 VMEM = pl.BlockSpec()
+PINNED = pl.BlockSpec(memory_space=pltpu.VMEM)
 SMEM = pl.BlockSpec(memory_space=pltpu.SMEM)
 
 
-def call(kernel, name, outs, args, scalars=0, flops=1 << 20):
+def whole(*shape):
+    return pl.BlockSpec(shape, lambda i: (0,) * len(shape))
+
+
+def call(kernel, name, outs, args, scalars=0, flops=1 << 20, flags=0, pinned=(), **grid):
     out = [jax.ShapeDtypeStruct(shape, dtype) for shape, dtype in outs]
+    if not grid:
+        grid = dict(
+            in_specs=[SMEM] * scalars
+            + [PINNED if i in pinned else VMEM for i in range(scalars, len(args))],
+            out_specs=[VMEM] * (len(out) - flags) + [SMEM] * flags,
+        )
     size = sum(a.size * a.dtype.itemsize for a in (*args, *out))
     return pl.pallas_call(
         kernel,
         out_shape=out,
-        in_specs=[SMEM] * scalars + [VMEM] * (len(args) - scalars),
-        out_specs=[VMEM] * len(out),
+        **grid,
         compiler_params=pltpu.CompilerParams(vmem_limit_bytes=16 << 20),
         cost_estimate=pl.CostEstimate(flops=flops, bytes_accessed=size, transcendentals=0),
         name=name,
@@ -366,7 +386,9 @@
         1,
         flops=2 * HALF * 2048 * WIDTH,
     )
-    return hidden_a, hidden_b, low_a, low_b, squares
+    hidden = jnp.concatenate([hidden_a, hidden_b], axis=0)
+    low = jnp.concatenate([low_a, low_b], axis=0)
+    return hidden, low, squares
 
 
 def hidden_few(ids, out_weight, residual, compacted, dest):
@@ -376,7 +398,7 @@
         call(
             few_kernel,
             "hidden",
-            [((HALF, WIDTH), f32)] * 2 + [((HALF, WIDTH), bf16)] * 2 + [((NT, 8, 128), f32)],
+            [((TOKENS, WIDTH), f32), ((TOKENS, WIDTH), bf16), ((NT, 8, 128), f32)],
             (ids, own, other, out_weight, residual, dest),
             1,
             flops=2 * CAP * 2048 * WIDTH,
@@ -400,16 +422,16 @@
     ).astype(i32)
     gain = final_norm_weight.reshape(1, WIDTH)
 
-    compacted, dest = call(
+    compacted, dest, fits = call(
         compact_kernel,
         "compact",
-        [((CAP, HW_DEV), bf16), ((8, TOKENS), f32)],
+        [((CAP, HW_DEV), bf16), ((8, TOKENS), f32), ((1, 1), i32)],
         (query_lengths.reshape(1, Q_DEV), passage_lengths.reshape(1, P_DEV), context),
         flops=2 * CAP * TOKENS * HW_DEV,
-    )
-    used = jnp.sum(jnp.concatenate([query_lengths, passage_lengths]))
-    hidden_a, hidden_b, low_a, low_b, squares = lax.cond(
-        used <= CAP,
+        flags=1,
+    )
+    hidden, low, squares = lax.cond(
+        fits[0, 0] == 1,
         functools.partial(hidden_few, ids, out_weight, residual, compacted, dest),
         functools.partial(hidden_all, ids, out_weight, residual, context),
     )
@@ -430,8 +452,7 @@
             passage_lengths.reshape(1, P_DEV),
             positive_index.reshape(1, Q_DEV),
             gain,
-            hidden_a,
-            hidden_b,
+            hidden,
         ),
     )
     q_all = exchange(q_pay, ROW)
@@ -439,8 +460,15 @@
         lift_kernel,
         "lift",
         [((TOKENS + SEQS, NT * HW_DEV), bf16)],
-        (low_a, low_b, lift, out_weight),
+        (low, lift, out_weight),
         flops=2 * TOKENS * 2048 * WIDTH,
+        grid=(NT // 2,),
+        in_specs=[
+            whole(TOKENS, WIDTH),
+            whole(SEQS, WIDTH),
+            pl.BlockSpec((2 * HW_DEV, WIDTH), lambda i: (i, 0)),
+        ],
+        out_specs=[pl.BlockSpec((TOKENS + SEQS, 2 * HW_DEV), lambda i: (0, i))],
     )
     p_all = exchange(p_pay, COL)
 
@@ -448,39 +476,44 @@
         score_kernel,
         "score",
         [((NT, SHARE, COLS + 128), f32), ((ROWS, 128), f32)],
-        (q_all, p_all, state, lift, low_a, low_b),
+        (q_all, p_all, state, lift, low),
     )
     payload, lifted = lax.optimization_barrier((payload, lifted))
     lifted = lax.psum_scatter(lifted, T, scatter_dimension=1, tiled=True)
     payload, side = call(
         softmax_kernel,
         "softmax",
-        [((N_ROW * NT, 2 * SHARE, COLS), bf16), ((SHARE, 128), f32)],
+        [((NT, 2 * SHARE, COLS), bf16), ((SHARE, 128), f32)],
         (ids, tile_mask, exchange(payload, T), position),
         2,
     )
-    loss, q_pay, p_pay = call(
-        back_kernel,
-        "back",
-        [((8, 128), f32), ((N_ROW, Q_DEV, WIDTH), bf16), ((N_COL, P_DEV, WIDTH), bf16)],
-        (ids, exchange(payload, ROW + T), position, q_all, p_all),
+    payload, terms = call(
+        query_kernel,
+        "query",
+        [((N_ROW, 3 * Q_DEV, WIDTH), bf16), ((ROWS, COLS), bf16)],
+        (ids, exchange(payload, T), q_all, p_all),
         1,
     )
+    loss, back_q, payload = call(
+        passage_kernel,
+        "passage",
+        [((8, 128), f32), ((Q_DEV, WIDTH), f32), ((N_COL, P_DEV, WIDTH), bf16)],
+        (ids, exchange(payload, ROW), terms, q_all),
+        1,
+    )
     query_loss = loss[0, :PAIR]
-    q_back = exchange(q_pay, ROW)
-    p_back = exchange(p_pay, COL)
     back_gain, payload = call(
         up_kernel,
         "up",
         [((SEQS, WIDTH), f32), ((NT, SEQS + 16, HW_DEV), bf16)],
-        (q_back, p_back, state, low_a, low_b, out_weight),
+        (back_q, exchange(payload, COL), state, low, out_weight),
     )
     payload, lifted = lax.optimization_barrier((payload, lifted))
     residual_gradient, d_context = call(
         final_kernel,
         "final",
         [((TOKENS, WIDTH), bf16), ((TOKENS, HW_DEV), bf16)],
-        (exchange(payload, T), side, state, back_gain, hidden_a, hidden_b, lifted),
+        (exchange(payload, T), side, state, back_gain, hidden, lifted),
     )
     return (query_loss, residual_gradient, d_context)
 

time: 169 us -> 158 us (0.935)
  blocking collectives: 86.2 us -> 75.9 us
  other arithmetic: 2.77 us -> 0.08 us
    all_to_all x6, blocking collectives: 70 us -> 59.7 us  [exchange(): return lax.all_to_all(parts, axes, 0, 0)]
    reduce_sum x2 -> x0, other arithmetic: 2.69 us -> none  [body(): used = jnp.sum(jnp.concatenate([query_lengths, passage_lengths]))]
    pallas_call x9 -> x10, Pallas kernels: 18.5 us -> 19.8 us  [call(): pl.pallas_call(kernel, out_shape=out, **grid, compiler_params=pltpu.Compi...]
  transfers between devices with their start and end apart: 4 -> 4, of which waited for: 3 -> 3; matrix products, arithmetic and copies ran while one was open for 0% -> 0% of each run, Pallas kernels for 5% -> 6%
where the time goes in v5:
time: 158 us; the launch traced here: 157 us
  blocking collectives  75.9 us (48%)
  starting transfers between devices  28.7 us (18%)
  Pallas kernels  19.8 us (13%)
  waiting for transfers between devices  15.2 us (10%)
  between operations  14.8 us (9%)
  local copies, waits for them, and re-layouts  2.8 us (2%)
    all_to_all x6, blocking collectives, exchange(): return lax.all_to_all(parts, axes, 0, 0)  59.7 us
    pallas_call x10, Pallas kernels, call(): pl.pallas_call(kernel, out_shape=out, **grid, compiler_params=pltpu.Compi...  19.8 us
    all_to_all x2, starting transfers between devices, exchange(): return lax.all_to_all(parts, axes, 0, 0)  18.8 us
    all_gather x1, blocking collectives, hidden_few(): own = lax.all_gather(compacted, 'yl', axis=1, tiled=True)  16.2 us
    all_to_all x2, waiting for transfers between devices, exchange(): return lax.all_to_all(parts, axes, 0, 0)  13.4 us
    ppermute x1, starting transfers between devices, hidden_few(): other = lax.ppermute(own, 'core', [(0, 1), (1, 0)])  9.8 us
  transfers between devices with their start and end apart: 4, of which 3 were waited for; matrix products, arithmetic and copies ran while one was open for 0% of the time, Pallas kernels for 6%

profile of v5, /device:TPU:1, one launch (start us, length us, event | category | flops | bytes accessed | tf_op | source)
XLA Modules:
  0.0 157.3 jit_solution(11373257768077295085)
XLA Ops:
  8.5 1.8 %compact.1 = (bf16[352,256]{1,0:T(8,128)(2,1)S(1)}, f32[8,512]{1,0:T(8,128)S(1)}, s32[1,1]{1,0:T(1,128)}) custom-call(s32[1,16]{1,0:T(1,128)S(1)} %bitcast.12, s32[1,16]{1,0:T(1,128)S(1)} %bitcast.14, bf16[512,256]{1,0:T(8,128)(2,1)} %context.1), custom_call_target="tpu_custom_call" | custom-call | flops 92274688 | bytes 458884 | tf_op jit(solution)/shard_map/compact/pallas_call | solution.py:353
  11.0 31.2 %conditional.1 = ((f32[512,512]{1,0:T(8,128)S(1)}, bf16[512,512]{1,0:T(8,128)(2,1)S(1)}, f32[8,8,128]{2,1,0:T(8,128)S(1)})) conditional(s32[]{:T(128)} %bitcast.6, (bf16[512,256]{1,0:T(8,128)(2,1)}, s32[4]{0:T(128)S(1)}, bf16[2048,512]{1,0:T(8,128)(2,1)}, bf16[512,512]{1,0:T(8,128)(2,1)}) %tuple.17, (bf16[352,256]{1,0:T(8,128)(2,1)S(1)}, ...), branch_computations={%region_0.0_spmd, %region_1.0_spmd} | conditional | flops 1075052544 | bytes 28614856 | solution.py:433
  11.0 16.2 %all_gather.8.own = bf16[352,1024]{1,0:T(8,128)(2,1)S(1)} all-gather(bf16[352,256]{1,0:T(8,128)(2,1)S(1)} %get-tuple-element.29), channel_id=1, replica_groups=mesh['z'=8,'x'=4,'yh'=2,'yl'=4,'core'=2] {'yl'}, dimensions={1}, use_global_device_ids=true | all-gather | bytes 901120 | tf_op jit(solution)/shard_map/cond/branch_1_fun/all_gather | solution.py:395
  27.2 9.8 %collective-permute-start = (bf16[352,1024]{1,0:T(8,128)(2,1)S(1)}, bf16[352,1024]{1,0:T(8,128)(2,1)S(1)}, u32[]{:S(2)}, u32[]{:S(2)}) collective-permute-start(bf16[352,1024]{1,0:T(8,128)(2,1)S(1)} %all_gather.8.own), channel_id=1, source_target_pairs={{0,1},{1,0},{2,3},{3,2},{4,5},{5,4},{6,7},{7,6},{8,9},{9,8},{10,11... | collective-permute-start | bytes 2162696 | tf_op jit(solution)/shard_map/cond/branch_1_fun/ppermute | solution.py:396
  37.0 1.8 %collective-permute-done.other = bf16[352,1024]{1,0:T(8,128)(2,1)S(1)} collective-permute-done((bf16[352,1024]{1,0:T(8,128)(2,1)S(1)}, bf16[352,1024]{1,0:T(8,128)(2,1)S(1)}, u32[]{:S(2)}, u32[]{:S(2)}) %collective-permute-start) | collective-permute-done | bytes 720928 | tf_op jit(solution)/shard_map/cond/branch_1_fun/ppermute | solution.py:396
  38.8 3.4 %hidden.1 = (f32[512,512]{1,0:T(8,128)S(1)}, bf16[512,512]{1,0:T(8,128)(2,1)S(1)}, f32[8,8,128]{2,1,0:T(8,128)S(1)}) custom-call(s32[4]{0:T(128)S(1)} %get-tuple-element.28.ids, bf16[352,1024]{1,0:T(8,128)(2,1)S(1)} %all_gather.8.own, bf16[352,1024]{1,0:T(8,128)(2,1)S(1)} %collective-permute-done.other, bf16[2048,512]{1,0:T(8,128)(2,1)} %get-tuple-element.30.weight, ...), custom_call_target="tpu_custom_call" | custom-call | flops 738197504 | bytes 5685264 | tf_op jit(solution)/shard_map/cond/branch_1_fun/hidden/pallas_call | solution.py:353
  42.2 7.7 %all_to_all.40.squares = f32[8,8,128]{2,1,0:T(8,128)S(1)} all-to-all(f32[8,8,128]{2,1,0:T(8,128)S(1)} %get-tuple-element.66), channel_id=1, replica_groups=mesh['z'=8,'x'=4,'yh'=2,'yl'=4,'core'=2] {'yl','core'}, dimensions={0} | all-to-all | bytes 65536 | tf_op jit(solution)/shard_map/all_to_all | solution.py:364
  49.9 1.5 pool.1
  51.4 6.9 %all_to_all.41.q_all = bf16[4,16,640]{2,1,0:T(8,128)(2,1)S(1)} all-to-all(bf16[4,16,640]{2,1,0:T(8,128)(2,1)S(1)} %get-tuple-element.68), channel_id=1, replica_groups=mesh['z'=8,'x'=4,'yh'=2,'yl'=4,'core'=2] {'x'}, dimensions={0} | all-to-all | bytes 163840 | tf_op jit(solution)/shard_map/all_to_all | solution.py:364
  58.3 12.2 %all-to-all-start.2 = ((bf16[16,16,512]{2,1,0:T(8,128)(2,1)}), bf16[16,16,512]{2,1,0:T(8,128)(2,1)S(1)}, u32[]{:S(2)}, u32[]{:S(2)}) async-start(bf16[16,16,512]{2,1,0:T(8,128)(2,1)} %get-tuple-element.69), calls=%async_computation.2 | async-start | bytes 524288 | tf_op jit(solution)/shard_map/all_to_all | solution.py:364
  70.6 4.9 %lift.1 = bf16[544,2048]{1,0:T(8,128)(2,1)} custom-call(bf16[512,512]{1,0:T(8,128)(2,1)S(1)} %get-tuple-element.72.low, bf16[32,512]{1,0:T(8,128)(2,1)S(1)} %get-tuple-element.71.lift.pooled, bf16[2048,512]{1,0:T(8,128)(2,1)} %weight.3), custom_call_target="tpu_custom_call" | custom-call | flops 1073741824 | bytes 4882432 | tf_op jit(solution)/shard_map/lift/pallas_call | solution.py:353
  75.5 7.5 %all-to-all-done.2.p_all = bf16[16,16,512]{2,1,0:T(8,128)(2,1)S(1)} async-done(((bf16[16,16,512]{2,1,0:T(8,128)(2,1)}), bf16[16,16,512]{2,1,0:T(8,128)(2,1)S(1)}, u32[]{:S(2)}, u32[]{:S(2)}) %all-to-all-start.2) | async-done | bytes 262176 | tf_op jit(solution)/shard_map/all_to_all | solution.py:364
  83.4 12.3 %all_to_all.42.parts = f32[8,8,384]{2,1,0:T(8,128)S(1)} all-to-all(f32[8,8,384]{2,1,0:T(8,128)S(1)} %get-tuple-element.74), channel_id=1, replica_groups=mesh['z'=8,'x'=4,'yh'=2,'yl'=4,'core'=2] {'yl','core'}, dimensions={0} | all-to-all | bytes 196608 | tf_op jit(solution)/shard_map/all_to_all | solution.py:364
  95.7 0.8 softmax.1
  96.5 9.5 %all_to_all.43.parts = bf16[8,16,256]{2,1,0:T(8,128)(2,1)S(1)} all-to-all(bf16[8,16,256]{2,1,0:T(8,128)(2,1)S(1)} %get-tuple-element.76), channel_id=1, replica_groups=mesh['z'=8,'x'=4,'yh'=2,'yl'=4,'core'=2] {'yl','core'}, dimensions={0} | all-to-all | bytes 131072 | tf_op jit(solution)/shard_map/all_to_all | solution.py:364
  106.1 0.9 query.1
  107.0 7.8 %all_to_all.44.parts = bf16[4,48,512]{2,1,0:T(8,128)(2,1)S(1)} all-to-all(bf16[4,48,512]{2,1,0:T(8,128)(2,1)S(1)} %get-tuple-element.77), channel_id=1, replica_groups=mesh['z'=8,'x'=4,'yh'=2,'yl'=4,'core'=2] {'x'}, dimensions={0} | all-to-all | bytes 393216 | tf_op jit(solution)/shard_map/all_to_all | solution.py:364
  114.8 0.9 passage.1
  115.7 15.5 %all_to_all.45.p_parts = bf16[16,16,512]{2,1,0:T(8,128)(2,1)S(1)} all-to-all(bf16[16,16,512]{2,1,0:T(8,128)(2,1)S(1)} %get-tuple-element.81), channel_id=1, replica_groups=mesh['z'=8,'x'=4,'yh'=2,'yl'=4,'core'=2] {'z','yh'}, dimensions={0} | all-to-all | bytes 524288 | tf_op jit(solution)/shard_map/all_to_all | solution.py:364
  131.2 1.6 up.1
  132.8 6.6 %all-to-all-start.7 = ((bf16[8,48,256]{2,1,0:T(8,128)(2,1)}), bf16[8,48,256]{2,1,0:T(8,128)(2,1)S(1)}, u32[]{:S(2)}, u32[]{:S(2)}) async-start(bf16[8,48,256]{2,1,0:T(8,128)(2,1)} %get-tuple-element.84), calls=%async_computation.8 | async-start | bytes 393216 | tf_op jit(solution)/shard_map/all_to_all | solution.py:364
  139.9 6.0 %all-to-all-done.7.parts = bf16[8,48,256]{2,1,0:T(8,128)(2,1)S(1)} async-done(((bf16[8,48,256]{2,1,0:T(8,128)(2,1)}), bf16[8,48,256]{2,1,0:T(8,128)(2,1)S(1)}, u32[]{:S(2)}, u32[]{:S(2)}) %all-to-all-start.7) | async-done | bytes 196640 | tf_op jit(solution)/shard_map/all_to_all | solution.py:364
  145.9 1.0 copy-done
  146.8 3.6 %final.1 = (bf16[512,512]{1,0:T(8,128)(2,1)}, bf16[512,256]{1,0:T(8,128)(2,1)}) custom-call(bf16[8,48,256]{2,1,0:T(8,128)(2,1)S(1)} %all-to-all-done.7.parts, f32[8,128]{1,0:T(8,128)S(1)} %get-tuple-element.85.side, f32[72,512]{1,0:T(8,128)S(1)} %get-tuple-element.70.state, f32[32,512]{1,0:T(8,128)S(1)} %get-tuple-element.86.back_gain, ...), custom_call_target="tpu_custom_call" | custom-call | flops 1048576 | bytes 2527232 | tf_op jit(solution)/shard_map/final/pallas_call | solution.py:353
  (25 shorter events, 2.4 us)
Async XLA Ops:
  7.2 0.7 copy-start.3
  7.8 0.7 copy-start.5
  11.0 38.9 %copy-start.2 = (f32[512]{0:T(512)S(1)}, f32[512]{0:T(512)}, u32[]{:S(2)}) copy-start(f32[512]{0:T(512)} %param.13) | copy-start | bytes 6148
  11.0 38.9 %copy-start.4 = (s32[16]{0:T(128)S(1)}, s32[16]{0:T(128)}, u32[]{:S(2)}) copy-start(s32[16]{0:T(128)} %param.14) | copy-start | bytes 196
  11.0 38.9 %copy-start.6 = (s32[16]{0:T(128)S(1)}, s32[16]{0:T(128)}, u32[]{:S(2)}) copy-start(s32[16]{0:T(128)} %param.15) | copy-start | bytes 196
  11.0 38.9 %copy-start.7 = (s32[16]{0:T(128)S(1)}, s32[16]{0:T(128)}, u32[]{:S(2)}) copy-start(s32[16]{0:T(128)} %param.16) | copy-start | bytes 196
  27.2 11.6 %collective-permute-start = (bf16[352,1024]{1,0:T(8,128)(2,1)S(1)}, bf16[352,1024]{1,0:T(8,128)(2,1)S(1)}, u32[]{:S(2)}, u32[]{:S(2)}) collective-permute-start(bf16[352,1024]{1,0:T(8,128)(2,1)S(1)} %all_gather.8.own), channel_id=1, source_target_pairs={{0,1},{1,0},{2,3},{3,2},{4,5},{5,4},{6,7},{7,6},{8,9},{9,8},{10,11... | collective-permute-start | bytes 2162696 | tf_op jit(solution)/shard_map/cond/branch_1_fun/ppermute | solution.py:396
  42.2 33.3 %copy-start.10 = (f32[512,512]{1,0:T(8,128)}, f32[512,512]{1,0:T(8,128)S(1)}, u32[]{:S(2)}) copy-start(f32[512,512]{1,0:T(8,128)S(1)} %get-tuple-element.67.hidden) | copy-start | bytes 3145732
  58.3 24.6 %all-to-all-start.2 = ((bf16[16,16,512]{2,1,0:T(8,128)(2,1)}), bf16[16,16,512]{2,1,0:T(8,128)(2,1)S(1)}, u32[]{:S(2)}, u32[]{:S(2)}) async-start(bf16[16,16,512]{2,1,0:T(8,128)(2,1)} %get-tuple-element.69), calls=%async_computation.2 | async-start | bytes 524288 | tf_op jit(solution)/shard_map/all_to_all | solution.py:364
  70.5 62.2 %reduce-scatter.2.cloned.1.call-start = ((), (), s32[]{:S(2)}) async-start(), calls=%async_computation.9 | async-start | bytes 2506752 | tf_op jit(solution)/shard_map/reduce_scatter | solution.py:482
  75.5 20.2 %copy-start.1 = (s32[8,8]{1,0:T(8,128)S(1)}, s32[8,8]{1,0:T(8,128)}, u32[]{:S(2)}) copy-start(s32[8,8]{1,0:T(8,128)} %tile_mask.1) | copy-start | bytes 772
  83.4 47.8 %copy-start.8 = (bf16[2048,512]{1,0:T(8,128)(2,1)S(1)}, bf16[2048,512]{1,0:T(8,128)(2,1)}, u32[]{:S(2)}) copy-start(bf16[2048,512]{1,0:T(8,128)(2,1)} %weight.3) | copy-start | bytes 6291460
  132.8 13.1 %all-to-all-start.7 = ((bf16[8,48,256]{2,1,0:T(8,128)(2,1)}), bf16[8,48,256]{2,1,0:T(8,128)(2,1)S(1)}, u32[]{:S(2)}, u32[]{:S(2)}) async-start(bf16[8,48,256]{2,1,0:T(8,128)(2,1)} %get-tuple-element.84), calls=%async_computation.8 | async-start | bytes 393216 | tf_op jit(solution)/shard_map/all_to_all | solution.py:364
  145.9 1.0 copy-start
Sparse Core Ops, SparseCore 0:
  83.6 37.7 reduce-scatter.1

commit v6 on v5

--- a/solution.py
+++ b/solution.py
@@ -104,9 +104,19 @@
         payload[...] = jnp.concatenate(rows + [jnp.zeros((6, 128), f32)], axis=0)
 
 
-def compact_kernel(q_len, p_len, context, out, dest, fits):
+def compact_kernel(q_len, p_len, context, out, dest, fits, q_here, p_here, context_here, sems):
+    copies = [
+        pltpu.make_async_copy(source, target, sems.at[i])
+        for i, (source, target) in enumerate(
+            ((q_len, q_here), (p_len, p_here), (context, context_here))
+        )
+    ]
+    for copy in copies:
+        copy.start()
+    copies[0].wait()
+    copies[1].wait()
     lengths = jnp.concatenate(
-        [to_col(q_len[...].astype(f32), Q_DEV), to_col(p_len[...].astype(f32), P_DEV)], axis=0
+        [to_col(q_here[...].astype(f32), Q_DEV), to_col(p_here[...].astype(f32), P_DEV)], axis=0
     )
     by_lane = to_row(lengths, SEQS)
     fits[0, 0] = (jnp.sum(by_lane) <= CAP).astype(i32)
@@ -117,7 +127,8 @@
     row = jnp.sum(row, axis=0, keepdims=True) - 1.0
     dest[...] = jnp.broadcast_to(row, (8, TOKENS))
     chosen = (iota((CAP, TOKENS), 0).astype(f32) == row).astype(f32).astype(bf16)
-    out[...] = dot(chosen, context[...]).astype(bf16)
+    copies[2].wait()
+    out[...] = dot(chosen, context_here[...]).astype(bf16)
 
 
 def few_kernel(ids, own, other, weight, residual, dest, hidden, low, payload):
@@ -155,19 +166,22 @@
     )
     slot = (iota((SEQS, TOKENS), 1) % SEQ_LEN).astype(f32)
     weight = jnp.where(seg_mask() & (slot < lengths), 1.0 / lengths, 0.0) * inverse
-    value = dot(weight, hidden[...], exact=True) * gain[...]
+    high, rest = (piece.astype(bf16) for piece in split(weight))
+    hidden_high, hidden_rest = (piece.astype(bf16) for piece in split(hidden[...]))
+    both = dot(jnp.concatenate([high, rest], axis=0), hidden_high)
+    value = (both[:SEQS] + both[SEQS:] + dot(high, hidden_rest)) * gain[...]
     state[:SEQS, :] = weight
     state[SEQS : 2 * SEQS, :] = value
     state[2 * SEQS :, :] = jnp.concatenate([inverse, gain[...], jnp.zeros((6, WIDTH), f32)], axis=0)
     lift[...] = (value * gain[...]).astype(bf16)
-    low = value.astype(bf16)
+    short = value.astype(bf16)
     where = to_col(position[...].astype(f32), Q_DEV)
     high = jnp.floor(where * (1.0 / 32.0))
     lane = iota((Q_DEV, 128), 1)
     where = jnp.where(lane == 0, high, jnp.where(lane == 1, where - 32.0 * high, 0.0))
-    q_pay[:, :, :WIDTH] = jnp.broadcast_to(low[None, :Q_DEV], (N_ROW, Q_DEV, WIDTH))
+    q_pay[:, :, :WIDTH] = jnp.broadcast_to(short[None, :Q_DEV], (N_ROW, Q_DEV, WIDTH))
     q_pay[:, :, WIDTH:] = jnp.broadcast_to(where.astype(bf16)[None], (N_ROW, Q_DEV, 128))
-    p_pay[...] = jnp.broadcast_to(low[None, Q_DEV:], (N_COL, P_DEV, WIDTH))
+    p_pay[...] = jnp.broadcast_to(short[None, Q_DEV:], (N_COL, P_DEV, WIDTH))
 
 
 def lift_kernel(low, pooled, weight, out):
@@ -308,7 +322,11 @@
         payload[n, SEQS:, :] = side
 
 
-def final_kernel(parts, side, state, back_gain, hidden, lifted, d_res, d_ctx):
+def stage_kernel(far, here):
+    here[...] = far[...]
+
+
+def final_kernel(parts, side, state, back_gain, hidden, lifted, d_res, d_ctx, res, ctx, sems):
     total = jnp.sum(parts[...].astype(f32), axis=0)
     rows = total[SEQS : SEQS + 8] + total[SEQS + 8 :]
     cross_back = jnp.concatenate([rows[0:1], rows[1:2]], axis=1)
@@ -323,17 +341,28 @@
     trail = inverse * inverse * by_token / FULL
     d_pooled = back_gain[...] - ratio * (state[SEQS : 2 * SEQS, :] * gain)
     seq_up = total[:SEQS] - ratio * lifted[TOKENS:, :].astype(f32)
-    both = jnp.concatenate([d_pooled, seq_up], axis=1)
+    lead_high, lead_rest = split(lead)
+    both_high, both_rest = split(jnp.concatenate([d_pooled, seq_up], axis=1))
+    leads = jnp.concatenate([lead_high, lead_rest, lead_high], axis=0).astype(bf16)
+    both = jnp.concatenate([both_high, both_high, both_rest], axis=0).astype(bf16)
+    copies = []
     for b in range(TOKENS // 128):
         part = slice(b * 128, (b + 1) * 128)
-        spread = dot(lead[:, part], both, ((0,), (0,)), exact=True)
+        spread = dot(leads[:, part], both, ((0,), (0,)))
         column = to_col(trail[:, part], 128)
-        d_res[part, :] = (spread[:, :WIDTH] - column * hidden[part, :]).astype(bf16)
-        d_ctx[part, :] = (spread[:, WIDTH:] - column * lifted[part, :].astype(f32)).astype(bf16)
+        res[part, :] = (spread[:, :WIDTH] - column * hidden[part, :]).astype(bf16)
+        ctx[part, :] = (spread[:, WIDTH:] - column * lifted[part, :].astype(f32)).astype(bf16)
+        for i, (here, far) in enumerate(((res, d_res), (ctx, d_ctx))):
+            copies.append(
+                pltpu.make_async_copy(here.at[part, :], far.at[part, :], sems.at[2 * b + i])
+            )
+            copies[-1].start()
+    for copy in copies:
+        copy.wait()
 
 
 VMEM = pl.BlockSpec()
-PINNED = pl.BlockSpec(memory_space=pltpu.VMEM)
+ANY = pl.BlockSpec(memory_space=pl.ANY)
 SMEM = pl.BlockSpec(memory_space=pltpu.SMEM)
 
 
@@ -341,20 +370,33 @@
     return pl.BlockSpec(shape, lambda i: (0,) * len(shape))
 
 
-def call(kernel, name, outs, args, scalars=0, flops=1 << 20, flags=0, pinned=(), **grid):
+def call(
+    kernel,
+    name,
+    outs,
+    args,
+    scalars=0,
+    flops=1 << 20,
+    flags=0,
+    anywhere=(),
+    anywhere_out=False,
+    scratch=(),
+    **grid,
+):
     out = [jax.ShapeDtypeStruct(shape, dtype) for shape, dtype in outs]
     if not grid:
         grid = dict(
             in_specs=[SMEM] * scalars
-            + [PINNED if i in pinned else VMEM for i in range(scalars, len(args))],
-            out_specs=[VMEM] * (len(out) - flags) + [SMEM] * flags,
+            + [ANY if i in anywhere else VMEM for i in range(scalars, len(args))],
+            out_specs=[ANY if anywhere_out else VMEM] * (len(out) - flags) + [SMEM] * flags,
+            scratch_shapes=list(scratch),
         )
     size = sum(a.size * a.dtype.itemsize for a in (*args, *out))
     return pl.pallas_call(
         kernel,
         out_shape=out,
         **grid,
-        compiler_params=pltpu.CompilerParams(vmem_limit_bytes=16 << 20),
+        compiler_params=pltpu.CompilerParams(vmem_limit_bytes=10 << 20),
         cost_estimate=pl.CostEstimate(flops=flops, bytes_accessed=size, transcendentals=0),
         name=name,
     )(*args)
@@ -429,6 +471,13 @@
         (query_lengths.reshape(1, Q_DEV), passage_lengths.reshape(1, P_DEV), context),
         flops=2 * CAP * TOKENS * HW_DEV,
         flags=1,
+        anywhere=(0, 1, 2),
+        scratch=[
+            pltpu.VMEM((1, Q_DEV), i32),
+            pltpu.VMEM((1, P_DEV), i32),
+            pltpu.VMEM((TOKENS, HW_DEV), bf16),
+            pltpu.SemaphoreType.DMA((3,)),
+        ],
     )
     hidden, low, squares = lax.cond(
         fits[0, 0] == 1,
@@ -509,11 +558,18 @@
         (back_q, exchange(payload, COL), state, low, out_weight),
     )
     payload, lifted = lax.optimization_barrier((payload, lifted))
+    (lifted,) = call(stage_kernel, "stage", [(lifted.shape, bf16)], (lifted,))
     residual_gradient, d_context = call(
         final_kernel,
         "final",
         [((TOKENS, WIDTH), bf16), ((TOKENS, HW_DEV), bf16)],
         (exchange(payload, T), side, state, back_gain, hidden, lifted),
+        anywhere_out=True,
+        scratch=[
+            pltpu.VMEM((TOKENS, WIDTH), bf16),
+            pltpu.VMEM((TOKENS, HW_DEV), bf16),
+            pltpu.SemaphoreType.DMA((2 * (TOKENS // 128),)),
+        ],
     )
     return (query_loss, residual_gradient, d_context)
 

time: 158 us -> 156 us (0.987)
  Pallas kernels: 19.8 us -> 18.1 us
    pallas_call x10 -> x11, Pallas kernels: 19.8 us -> 18.1 us  [call(): pl.pallas_call(kernel, out_shape=out, **grid, compiler_params=pltpu.Compi...]
where the time goes in v6:
time: 156 us; the launch traced here: 155 us
  blocking collectives  75.9 us (49%)
  starting transfers between devices  28.8 us (18%)
  Pallas kernels  18.1 us (12%)
  between operations  14.8 us (9%)
  waiting for transfers between devices  14.2 us (9%)
  local copies, waits for them, and re-layouts  2.8 us (2%)
    all_to_all x6, blocking collectives, exchange(): return lax.all_to_all(parts, axes, 0, 0)  59.7 us
    all_to_all x2, starting transfers between devices, exchange(): return lax.all_to_all(parts, axes, 0, 0)  18.9 us
    pallas_call x11, Pallas kernels, call(): pl.pallas_call(kernel, out_shape=out, **grid, compiler_params=pltpu.Compi...  18.1 us
    all_gather x1, blocking collectives, hidden_few(): own = lax.all_gather(compacted, 'yl', axis=1, tiled=True)  16.2 us
    all_to_all x2, waiting for transfers between devices, exchange(): return lax.all_to_all(parts, axes, 0, 0)  12.4 us
    ppermute x1, starting transfers between devices, hidden_few(): other = lax.ppermute(own, 'core', [(0, 1), (1, 0)])  9.8 us
  transfers between devices with their start and end apart: 4, of which 3 were waited for; matrix products, arithmetic and copies ran while one was open for 0% of the time, Pallas kernels for 6%

profile of v6, /device:TPU:1, one launch (start us, length us, event | category | flops | bytes accessed | tf_op | source)
XLA Modules:
  0.0 154.7 jit_solution(12606015973383864624)
XLA Ops:
  8.5 1.5 compact.1
  10.7 31.2 %conditional.1 = ((f32[512,512]{1,0:T(8,128)S(1)}, bf16[512,512]{1,0:T(8,128)(2,1)S(1)}, f32[8,8,128]{2,1,0:T(8,128)S(1)})) conditional(s32[]{:T(128)} %bitcast.6, (bf16[512,256]{1,0:T(8,128)(2,1)}, s32[4]{0:T(128)S(1)}, bf16[2048,512]{1,0:T(8,128)(2,1)}, bf16[512,512]{1,0:T(8,128)(2,1)}) %tuple.17, (bf16[352,256]{1,0:T(8,128)(2,1)S(1)}, ...), branch_computations={%region_0.0_spmd, %region_1.0_spmd} | conditional | flops 1075052544 | bytes 28614856 | solution.py:482
  10.7 16.2 %all_gather.8.own = bf16[352,1024]{1,0:T(8,128)(2,1)S(1)} all-gather(bf16[352,256]{1,0:T(8,128)(2,1)S(1)} %get-tuple-element.29), channel_id=1, replica_groups=mesh['z'=8,'x'=4,'yh'=2,'yl'=4,'core'=2] {'yl'}, dimensions={1}, use_global_device_ids=true | all-gather | bytes 901120 | tf_op jit(solution)/shard_map/cond/branch_1_fun/all_gather | solution.py:437
  26.9 9.8 %collective-permute-start = (bf16[352,1024]{1,0:T(8,128)(2,1)S(1)}, bf16[352,1024]{1,0:T(8,128)(2,1)S(1)}, u32[]{:S(2)}, u32[]{:S(2)}) collective-permute-start(bf16[352,1024]{1,0:T(8,128)(2,1)S(1)} %all_gather.8.own), channel_id=1, source_target_pairs={{0,1},{1,0},{2,3},{3,2},{4,5},{5,4},{6,7},{7,6},{8,9},{9,8},{10,11... | collective-permute-start | bytes 2162696 | tf_op jit(solution)/shard_map/cond/branch_1_fun/ppermute | solution.py:438
  36.7 1.8 %collective-permute-done.other = bf16[352,1024]{1,0:T(8,128)(2,1)S(1)} collective-permute-done((bf16[352,1024]{1,0:T(8,128)(2,1)S(1)}, bf16[352,1024]{1,0:T(8,128)(2,1)S(1)}, u32[]{:S(2)}, u32[]{:S(2)}) %collective-permute-start) | collective-permute-done | bytes 720928 | tf_op jit(solution)/shard_map/cond/branch_1_fun/ppermute | solution.py:438
  38.5 3.4 %hidden.1 = (f32[512,512]{1,0:T(8,128)S(1)}, bf16[512,512]{1,0:T(8,128)(2,1)S(1)}, f32[8,8,128]{2,1,0:T(8,128)S(1)}) custom-call(s32[4]{0:T(128)S(1)} %get-tuple-element.28.ids, bf16[352,1024]{1,0:T(8,128)(2,1)S(1)} %all_gather.8.own, bf16[352,1024]{1,0:T(8,128)(2,1)S(1)} %collective-permute-done.other, bf16[2048,512]{1,0:T(8,128)(2,1)} %get-tuple-element.30.weight, ...), custom_call_target="tpu_custom_call" | custom-call | flops 738197504 | bytes 5685264 | tf_op jit(solution)/shard_map/cond/branch_1_fun/hidden/pallas_call | solution.py:395
  41.9 7.7 %all_to_all.40.squares = f32[8,8,128]{2,1,0:T(8,128)S(1)} all-to-all(f32[8,8,128]{2,1,0:T(8,128)S(1)} %get-tuple-element.66), channel_id=1, replica_groups=mesh['z'=8,'x'=4,'yh'=2,'yl'=4,'core'=2] {'yl','core'}, dimensions={0} | all-to-all | bytes 65536 | tf_op jit(solution)/shard_map/all_to_all | solution.py:406
  49.6 1.2 pool.1
  50.8 6.9 %all_to_all.41.q_all = bf16[4,16,640]{2,1,0:T(8,128)(2,1)S(1)} all-to-all(bf16[4,16,640]{2,1,0:T(8,128)(2,1)S(1)} %get-tuple-element.68), channel_id=1, replica_groups=mesh['z'=8,'x'=4,'yh'=2,'yl'=4,'core'=2] {'x'}, dimensions={0} | all-to-all | bytes 163840 | tf_op jit(solution)/shard_map/all_to_all | solution.py:406
  57.7 12.2 %all-to-all-start.2 = ((bf16[16,16,512]{2,1,0:T(8,128)(2,1)}), bf16[16,16,512]{2,1,0:T(8,128)(2,1)S(1)}, u32[]{:S(2)}, u32[]{:S(2)}) async-start(bf16[16,16,512]{2,1,0:T(8,128)(2,1)} %get-tuple-element.69), calls=%async_computation.2 | async-start | bytes 524288 | tf_op jit(solution)/shard_map/all_to_all | solution.py:406
  70.0 4.9 %lift.1 = bf16[544,2048]{1,0:T(8,128)(2,1)} custom-call(bf16[512,512]{1,0:T(8,128)(2,1)S(1)} %get-tuple-element.72.low, bf16[32,512]{1,0:T(8,128)(2,1)S(1)} %get-tuple-element.71.lift.pooled, bf16[2048,512]{1,0:T(8,128)(2,1)} %weight.3), custom_call_target="tpu_custom_call" | custom-call | flops 1073741824 | bytes 4882432 | tf_op jit(solution)/shard_map/lift/pallas_call | solution.py:395
  74.9 7.5 %all-to-all-done.2.p_all = bf16[16,16,512]{2,1,0:T(8,128)(2,1)S(1)} async-done(((bf16[16,16,512]{2,1,0:T(8,128)(2,1)}), bf16[16,16,512]{2,1,0:T(8,128)(2,1)S(1)}, u32[]{:S(2)}, u32[]{:S(2)}) %all-to-all-start.2) | async-done | bytes 262176 | tf_op jit(solution)/shard_map/all_to_all | solution.py:406
  82.8 12.3 %all_to_all.42.parts = f32[8,8,384]{2,1,0:T(8,128)S(1)} all-to-all(f32[8,8,384]{2,1,0:T(8,128)S(1)} %get-tuple-element.74), channel_id=1, replica_groups=mesh['z'=8,'x'=4,'yh'=2,'yl'=4,'core'=2] {'yl','core'}, dimensions={0} | all-to-all | bytes 196608 | tf_op jit(solution)/shard_map/all_to_all | solution.py:406
  95.1 0.8 softmax.1
  95.9 9.5 %all_to_all.43.parts = bf16[8,16,256]{2,1,0:T(8,128)(2,1)S(1)} all-to-all(bf16[8,16,256]{2,1,0:T(8,128)(2,1)S(1)} %get-tuple-element.76), channel_id=1, replica_groups=mesh['z'=8,'x'=4,'yh'=2,'yl'=4,'core'=2] {'yl','core'}, dimensions={0} | all-to-all | bytes 131072 | tf_op jit(solution)/shard_map/all_to_all | solution.py:406
  105.5 0.9 query.1
  106.4 7.8 %all_to_all.44.parts = bf16[4,48,512]{2,1,0:T(8,128)(2,1)S(1)} all-to-all(bf16[4,48,512]{2,1,0:T(8,128)(2,1)S(1)} %get-tuple-element.77), channel_id=1, replica_groups=mesh['z'=8,'x'=4,'yh'=2,'yl'=4,'core'=2] {'x'}, dimensions={0} | all-to-all | bytes 393216 | tf_op jit(solution)/shard_map/all_to_all | solution.py:406
  114.2 0.9 passage.1
  115.1 15.5 %all_to_all.45.p_parts = bf16[16,16,512]{2,1,0:T(8,128)(2,1)S(1)} all-to-all(bf16[16,16,512]{2,1,0:T(8,128)(2,1)S(1)} %get-tuple-element.81), channel_id=1, replica_groups=mesh['z'=8,'x'=4,'yh'=2,'yl'=4,'core'=2] {'z','yh'}, dimensions={0} | all-to-all | bytes 524288 | tf_op jit(solution)/shard_map/all_to_all | solution.py:406
  130.6 1.6 %up.1 = (f32[32,512]{1,0:T(8,128)S(1)}, bf16[8,48,256]{2,1,0:T(8,128)(2,1)}) custom-call(f32[16,512]{1,0:T(8,128)S(1)} %get-tuple-element.80.back_q, bf16[16,16,512]{2,1,0:T(8,128)(2,1)S(1)} %all_to_all.45.p_parts, f32[72,512]{1,0:T(8,128)S(1)} %get-tuple-element.70.state, bf16[512,512]{1,0:T(8,128)(2,1)S(1)} %get-tuple-element.72.low, ...), custom_call_target="tpu_custom_call" | custom-call | flops 1048576 | bytes 3325952 | tf_op jit(solution)/shard_map/up/pallas_call | solution.py:395
  132.2 6.7 %all-to-all-start.7 = ((bf16[8,48,256]{2,1,0:T(8,128)(2,1)}), bf16[8,48,256]{2,1,0:T(8,128)(2,1)S(1)}, u32[]{:S(2)}, u32[]{:S(2)}) async-start(bf16[8,48,256]{2,1,0:T(8,128)(2,1)} %get-tuple-element.84), calls=%async_computation.8 | async-start | bytes 393216 | tf_op jit(solution)/shard_map/all_to_all | solution.py:406
  139.4 1.0 copy-done
  140.4 5.0 %all-to-all-done.7.parts = bf16[8,48,256]{2,1,0:T(8,128)(2,1)S(1)} async-done(((bf16[8,48,256]{2,1,0:T(8,128)(2,1)}), bf16[8,48,256]{2,1,0:T(8,128)(2,1)S(1)}, u32[]{:S(2)}, u32[]{:S(2)}) %all-to-all-start.7) | async-done | bytes 196640 | tf_op jit(solution)/shard_map/all_to_all | solution.py:406
  145.4 2.4 %final.1 = (bf16[512,512]{1,0:T(8,128)(2,1)}, bf16[512,256]{1,0:T(8,128)(2,1)}) custom-call(bf16[8,48,256]{2,1,0:T(8,128)(2,1)S(1)} %all-to-all-done.7.parts, f32[8,128]{1,0:T(8,128)S(1)} %get-tuple-element.85.side, f32[72,512]{1,0:T(8,128)S(1)} %get-tuple-element.70.state, f32[32,512]{1,0:T(8,128)S(1)} %get-tuple-element.86.back_gain, ...), custom_call_target="tpu_custom_call" | custom-call | flops 1048576 | bytes 2527232 | tf_op jit(solution)/shard_map/final/pallas_call | solution.py:395
  (26 shorter events, 2.4 us)
Async XLA Ops:
  7.2 0.7 copy-start.3
  7.8 0.7 copy-start.5
  10.7 38.9 %copy-start.2 = (f32[512]{0:T(512)S(1)}, f32[512]{0:T(512)}, u32[]{:S(2)}) copy-start(f32[512]{0:T(512)} %param.13) | copy-start | bytes 6148
  10.7 38.9 %copy-start.4 = (s32[16]{0:T(128)S(1)}, s32[16]{0:T(128)}, u32[]{:S(2)}) copy-start(s32[16]{0:T(128)} %param.14) | copy-start | bytes 196
  10.7 38.9 %copy-start.6 = (s32[16]{0:T(128)S(1)}, s32[16]{0:T(128)}, u32[]{:S(2)}) copy-start(s32[16]{0:T(128)} %param.15) | copy-start | bytes 196
  10.7 38.9 %copy-start.7 = (s32[16]{0:T(128)S(1)}, s32[16]{0:T(128)}, u32[]{:S(2)}) copy-start(s32[16]{0:T(128)} %param.16) | copy-start | bytes 196
  26.9 11.6 %collective-permute-start = (bf16[352,1024]{1,0:T(8,128)(2,1)S(1)}, bf16[352,1024]{1,0:T(8,128)(2,1)S(1)}, u32[]{:S(2)}, u32[]{:S(2)}) collective-permute-start(bf16[352,1024]{1,0:T(8,128)(2,1)S(1)} %all_gather.8.own), channel_id=1, source_target_pairs={{0,1},{1,0},{2,3},{3,2},{4,5},{5,4},{6,7},{7,6},{8,9},{9,8},{10,11... | collective-permute-start | bytes 2162696 | tf_op jit(solution)/shard_map/cond/branch_1_fun/ppermute | solution.py:438
  41.9 33.0 %copy-start.10 = (f32[512,512]{1,0:T(8,128)}, f32[512,512]{1,0:T(8,128)S(1)}, u32[]{:S(2)}) copy-start(f32[512,512]{1,0:T(8,128)S(1)} %get-tuple-element.67.hidden) | copy-start | bytes 3145732
  57.7 24.6 %all-to-all-start.2 = ((bf16[16,16,512]{2,1,0:T(8,128)(2,1)}), bf16[16,16,512]{2,1,0:T(8,128)(2,1)S(1)}, u32[]{:S(2)}, u32[]{:S(2)}) async-start(bf16[16,16,512]{2,1,0:T(8,128)(2,1)} %get-tuple-element.69), calls=%async_computation.2 | async-start | bytes 524288 | tf_op jit(solution)/shard_map/all_to_all | solution.py:406
  69.9 62.3 %reduce-scatter.2.cloned.1.call-start = ((), (), s32[]{:S(2)}) async-start(), calls=%async_computation.9 | async-start | bytes 2506752 | tf_op jit(solution)/shard_map/reduce_scatter | solution.py:531
  74.9 20.2 %copy-start.1 = (s32[8,8]{1,0:T(8,128)S(1)}, s32[8,8]{1,0:T(8,128)}, u32[]{:S(2)}) copy-start(s32[8,8]{1,0:T(8,128)} %tile_mask.1) | copy-start | bytes 772
  82.8 47.8 %copy-start.8 = (bf16[2048,512]{1,0:T(8,128)(2,1)S(1)}, bf16[2048,512]{1,0:T(8,128)(2,1)}, u32[]{:S(2)}) copy-start(bf16[2048,512]{1,0:T(8,128)(2,1)} %weight.3) | copy-start | bytes 6291460
  132.2 13.2 %all-to-all-start.7 = ((bf16[8,48,256]{2,1,0:T(8,128)(2,1)}), bf16[8,48,256]{2,1,0:T(8,128)(2,1)S(1)}, u32[]{:S(2)}, u32[]{:S(2)}) async-start(bf16[8,48,256]{2,1,0:T(8,128)(2,1)} %get-tuple-element.84), calls=%async_computation.8 | async-start | bytes 393216 | tf_op jit(solution)/shard_map/all_to_all | solution.py:406
  139.4 1.0 copy-start
Sparse Core Ops, SparseCore 0:
  82.9 37.6 reduce-scatter.1

commit v7 on v6

--- a/solution.py
+++ b/solution.py
@@ -104,21 +104,11 @@
         payload[...] = jnp.concatenate(rows + [jnp.zeros((6, 128), f32)], axis=0)
 
 
-def compact_kernel(q_len, p_len, context, out, dest, fits, q_here, p_here, context_here, sems):
-    copies = [
-        pltpu.make_async_copy(source, target, sems.at[i])
-        for i, (source, target) in enumerate(
-            ((q_len, q_here), (p_len, p_here), (context, context_here))
-        )
-    ]
-    for copy in copies:
-        copy.start()
-    copies[0].wait()
-    copies[1].wait()
-    lengths = jnp.concatenate(
-        [to_col(q_here[...].astype(f32), Q_DEV), to_col(p_here[...].astype(f32), P_DEV)], axis=0
-    )
-    by_lane = to_row(lengths, SEQS)
+def compact_kernel(lens, context, out, dest, fits, context_here, sems):
+    fetch = pltpu.make_async_copy(context, context_here, sems.at[0])
+    fetch.start()
+    by_lane = lens[...].astype(f32)
+    lengths = to_col(by_lane, SEQS)
     fits[0, 0] = (jnp.sum(by_lane) <= CAP).astype(i32)
     before = iota((SEQS, SEQS), 1) < iota((SEQS, SEQS), 0)
     first = jnp.sum(jnp.where(before, by_lane, 0.0), axis=1, keepdims=True)
@@ -127,7 +117,7 @@
     row = jnp.sum(row, axis=0, keepdims=True) - 1.0
     dest[...] = jnp.broadcast_to(row, (8, TOKENS))
     chosen = (iota((CAP, TOKENS), 0).astype(f32) == row).astype(f32).astype(bf16)
-    copies[2].wait()
+    fetch.wait()
     out[...] = dot(chosen, context_here[...]).astype(bf16)
 
 
@@ -156,14 +146,12 @@
 
 
 def pool_kernel(
-    squares, q_len, p_len, position, gain, hidden, state, lift, q_pay, p_pay
+    squares, lens, position, gain, hidden, state, lift, q_pay, p_pay
 ):
     total = jnp.sum(squares[...], axis=0)
     total = jnp.concatenate([total[b : b + 1] for b in range(TOKENS // 128)], axis=1)
     inverse = lax.rsqrt(total / FULL + EPS)
-    lengths = jnp.concatenate(
-        [to_col(q_len[...].astype(f32), Q_DEV), to_col(p_len[...].astype(f32), P_DEV)], axis=0
-    )
+    lengths = to_col(lens[...].astype(f32), SEQS)
     slot = (iota((SEQS, TOKENS), 1) % SEQ_LEN).astype(f32)
     weight = jnp.where(seg_mask() & (slot < lengths), 1.0 / lengths, 0.0) * inverse
     high, rest = (piece.astype(bf16) for piece in split(weight))
@@ -316,9 +304,11 @@
     inner = jnp.concatenate([inner, jnp.zeros((1, HW_DEV - SEQS), f32)], axis=1)
     rows = [cross[:, :HW_DEV], cross[:, HW_DEV:], inner, jnp.zeros((5, HW_DEV), f32)]
     side = jnp.concatenate(split(jnp.concatenate(rows, axis=0)), axis=0).astype(bf16)
+    wide = jnp.concatenate([scaled, jnp.zeros((128 - SEQS, WIDTH), bf16)], axis=0)
     for n in range(NT):
         w = weight[n * HW_DEV : (n + 1) * HW_DEV, :]
-        payload[n, :SEQS, :] = dot(scaled, w, ((1,), (1,))).astype(bf16)
+        block = jnp.transpose(dot(w, wide, ((1,), (1,))))
+        payload[n, :SEQS, :] = block[:SEQS].astype(bf16)
         payload[n, SEQS:, :] = side
 
 
@@ -463,20 +453,19 @@
         [lax.axis_index("core"), me, lax.axis_index("z"), lax.axis_index("x")]
     ).astype(i32)
     gain = final_norm_weight.reshape(1, WIDTH)
+    lengths = jnp.concatenate([query_lengths, passage_lengths]).reshape(1, SEQS)
 
     compacted, dest, fits = call(
         compact_kernel,
         "compact",
         [((CAP, HW_DEV), bf16), ((8, TOKENS), f32), ((1, 1), i32)],
-        (query_lengths.reshape(1, Q_DEV), passage_lengths.reshape(1, P_DEV), context),
+        (lengths, context),
         flops=2 * CAP * TOKENS * HW_DEV,
         flags=1,
-        anywhere=(0, 1, 2),
+        anywhere=(1,),
         scratch=[
-            pltpu.VMEM((1, Q_DEV), i32),
-            pltpu.VMEM((1, P_DEV), i32),
             pltpu.VMEM((TOKENS, HW_DEV), bf16),
-            pltpu.SemaphoreType.DMA((3,)),
+            pltpu.SemaphoreType.DMA((1,)),
         ],
     )
     hidden, low, squares = lax.cond(
@@ -497,8 +486,7 @@
         ],
         (
             squares,
-            query_lengths.reshape(1, Q_DEV),
-            passage_lengths.reshape(1, P_DEV),
+            lengths,
             positive_index.reshape(1, Q_DEV),
             gain,
             hidden,

time: 156 us -> 155 us (level)
  no operation moved by 1% of the time
where the time goes in v7:
time: 155 us; the launch traced here: 154 us
  blocking collectives  75.9 us (49%)
  starting transfers between devices  28.7 us (19%)
  Pallas kernels  18 us (12%)
  between operations  14.8 us (10%)
  waiting for transfers between devices  14.2 us (9%)
    all_to_all x6, blocking collectives, exchange(): return lax.all_to_all(parts, axes, 0, 0)  59.7 us
    all_to_all x2, starting transfers between devices, exchange(): return lax.all_to_all(parts, axes, 0, 0)  18.9 us
    pallas_call x11, Pallas kernels, call(): pl.pallas_call(kernel, out_shape=out, **grid, compiler_params=pltpu.Compi...  18 us
    all_gather x1, blocking collectives, hidden_few(): own = lax.all_gather(compacted, 'yl', axis=1, tiled=True)  16.2 us
    all_to_all x2, waiting for transfers between devices, exchange(): return lax.all_to_all(parts, axes, 0, 0)  12.4 us
    ppermute x1, starting transfers between devices, hidden_few(): other = lax.ppermute(own, 'core', [(0, 1), (1, 0)])  9.8 us
  transfers between devices with their start and end apart: 4, of which 3 were waited for; matrix products, arithmetic and copies ran while one was open for 0% of the time, Pallas kernels for 6%

profile of v7, /device:TPU:1, one launch (start us, length us, event | category | flops | bytes accessed | tf_op | source)
XLA Modules:
  0.0 153.9 jit_solution(9454994611392316905)
XLA Ops:
  7.9 1.5 compact.1
  10.1 31.2 %conditional.1 = ((f32[512,512]{1,0:T(8,128)S(1)}, bf16[512,512]{1,0:T(8,128)(2,1)S(1)}, f32[8,8,128]{2,1,0:T(8,128)S(1)})) conditional(s32[]{:T(128)} %bitcast.5, (bf16[512,256]{1,0:T(8,128)(2,1)}, s32[4]{0:T(128)S(1)}, bf16[2048,512]{1,0:T(8,128)(2,1)}, bf16[512,512]{1,0:T(8,128)(2,1)}) %tuple.17, (bf16[352,256]{1,0:T(8,128)(2,1)S(1)}, ...), branch_computations={%region_0.0_spmd, %region_1.0_spmd} | conditional | flops 1075052544 | bytes 28614856 | solution.py:471
  10.1 16.2 %all_gather.8.own = bf16[352,1024]{1,0:T(8,128)(2,1)S(1)} all-gather(bf16[352,256]{1,0:T(8,128)(2,1)S(1)} %get-tuple-element.29), channel_id=1, replica_groups=mesh['z'=8,'x'=4,'yh'=2,'yl'=4,'core'=2] {'yl'}, dimensions={1}, use_global_device_ids=true | all-gather | bytes 901120 | tf_op jit(solution)/shard_map/cond/branch_1_fun/all_gather | solution.py:427
  26.3 9.8 %collective-permute-start = (bf16[352,1024]{1,0:T(8,128)(2,1)S(1)}, bf16[352,1024]{1,0:T(8,128)(2,1)S(1)}, u32[]{:S(2)}, u32[]{:S(2)}) collective-permute-start(bf16[352,1024]{1,0:T(8,128)(2,1)S(1)} %all_gather.8.own), channel_id=1, source_target_pairs={{0,1},{1,0},{2,3},{3,2},{4,5},{5,4},{6,7},{7,6},{8,9},{9,8},{10,11... | collective-permute-start | bytes 2162696 | tf_op jit(solution)/shard_map/cond/branch_1_fun/ppermute | solution.py:428
  36.1 1.8 %collective-permute-done.other = bf16[352,1024]{1,0:T(8,128)(2,1)S(1)} collective-permute-done((bf16[352,1024]{1,0:T(8,128)(2,1)S(1)}, bf16[352,1024]{1,0:T(8,128)(2,1)S(1)}, u32[]{:S(2)}, u32[]{:S(2)}) %collective-permute-start) | collective-permute-done | bytes 720928 | tf_op jit(solution)/shard_map/cond/branch_1_fun/ppermute | solution.py:428
  37.9 3.4 %hidden.1 = (f32[512,512]{1,0:T(8,128)S(1)}, bf16[512,512]{1,0:T(8,128)(2,1)S(1)}, f32[8,8,128]{2,1,0:T(8,128)S(1)}) custom-call(s32[4]{0:T(128)S(1)} %get-tuple-element.28.ids, bf16[352,1024]{1,0:T(8,128)(2,1)S(1)} %all_gather.8.own, bf16[352,1024]{1,0:T(8,128)(2,1)S(1)} %collective-permute-done.other, bf16[2048,512]{1,0:T(8,128)(2,1)} %get-tuple-element.30.weight, ...), custom_call_target="tpu_custom_call" | custom-call | flops 738197504 | bytes 5685264 | tf_op jit(solution)/shard_map/cond/branch_1_fun/hidden/pallas_call | solution.py:385
  41.3 7.7 %all_to_all.40.squares = f32[8,8,128]{2,1,0:T(8,128)S(1)} all-to-all(f32[8,8,128]{2,1,0:T(8,128)S(1)} %get-tuple-element.66), channel_id=1, replica_groups=mesh['z'=8,'x'=4,'yh'=2,'yl'=4,'core'=2] {'yl','core'}, dimensions={0} | all-to-all | bytes 65536 | tf_op jit(solution)/shard_map/all_to_all | solution.py:396
  49.0 1.1 pool.1
  50.1 6.9 %all_to_all.41.q_all = bf16[4,16,640]{2,1,0:T(8,128)(2,1)S(1)} all-to-all(bf16[4,16,640]{2,1,0:T(8,128)(2,1)S(1)} %get-tuple-element.68), channel_id=1, replica_groups=mesh['z'=8,'x'=4,'yh'=2,'yl'=4,'core'=2] {'x'}, dimensions={0} | all-to-all | bytes 163840 | tf_op jit(solution)/shard_map/all_to_all | solution.py:396
  57.0 12.2 %all-to-all-start.2 = ((bf16[16,16,512]{2,1,0:T(8,128)(2,1)}), bf16[16,16,512]{2,1,0:T(8,128)(2,1)S(1)}, u32[]{:S(2)}, u32[]{:S(2)}) async-start(bf16[16,16,512]{2,1,0:T(8,128)(2,1)} %get-tuple-element.69), calls=%async_computation.2 | async-start | bytes 524288 | tf_op jit(solution)/shard_map/all_to_all | solution.py:396
  69.3 4.9 %lift.1 = bf16[544,2048]{1,0:T(8,128)(2,1)} custom-call(bf16[512,512]{1,0:T(8,128)(2,1)S(1)} %get-tuple-element.72.low, bf16[32,512]{1,0:T(8,128)(2,1)S(1)} %get-tuple-element.71.lift.pooled, bf16[2048,512]{1,0:T(8,128)(2,1)} %weight.3), custom_call_target="tpu_custom_call" | custom-call | flops 1073741824 | bytes 4882432 | tf_op jit(solution)/shard_map/lift/pallas_call | solution.py:385
  74.2 7.4 %all-to-all-done.2.p_all = bf16[16,16,512]{2,1,0:T(8,128)(2,1)S(1)} async-done(((bf16[16,16,512]{2,1,0:T(8,128)(2,1)}), bf16[16,16,512]{2,1,0:T(8,128)(2,1)S(1)}, u32[]{:S(2)}, u32[]{:S(2)}) %all-to-all-start.2) | async-done | bytes 262176 | tf_op jit(solution)/shard_map/all_to_all | solution.py:396
  82.1 12.3 %all_to_all.42.parts = f32[8,8,384]{2,1,0:T(8,128)S(1)} all-to-all(f32[8,8,384]{2,1,0:T(8,128)S(1)} %get-tuple-element.74), channel_id=1, replica_groups=mesh['z'=8,'x'=4,'yh'=2,'yl'=4,'core'=2] {'yl','core'}, dimensions={0} | all-to-all | bytes 196608 | tf_op jit(solution)/shard_map/all_to_all | solution.py:396
  94.4 0.8 softmax.1
  95.2 9.5 %all_to_all.43.parts = bf16[8,16,256]{2,1,0:T(8,128)(2,1)S(1)} all-to-all(bf16[8,16,256]{2,1,0:T(8,128)(2,1)S(1)} %get-tuple-element.76), channel_id=1, replica_groups=mesh['z'=8,'x'=4,'yh'=2,'yl'=4,'core'=2] {'yl','core'}, dimensions={0} | all-to-all | bytes 131072 | tf_op jit(solution)/shard_map/all_to_all | solution.py:396
  104.8 0.9 query.1
  105.7 7.8 %all_to_all.44.parts = bf16[4,48,512]{2,1,0:T(8,128)(2,1)S(1)} all-to-all(bf16[4,48,512]{2,1,0:T(8,128)(2,1)S(1)} %get-tuple-element.77), channel_id=1, replica_groups=mesh['z'=8,'x'=4,'yh'=2,'yl'=4,'core'=2] {'x'}, dimensions={0} | all-to-all | bytes 393216 | tf_op jit(solution)/shard_map/all_to_all | solution.py:396
  113.5 0.9 passage.1
  114.4 15.5 %all_to_all.45.p_parts = bf16[16,16,512]{2,1,0:T(8,128)(2,1)S(1)} all-to-all(bf16[16,16,512]{2,1,0:T(8,128)(2,1)S(1)} %get-tuple-element.81), channel_id=1, replica_groups=mesh['z'=8,'x'=4,'yh'=2,'yl'=4,'core'=2] {'z','yh'}, dimensions={0} | all-to-all | bytes 524288 | tf_op jit(solution)/shard_map/all_to_all | solution.py:396
  129.9 1.6 %up.1 = (f32[32,512]{1,0:T(8,128)S(1)}, bf16[8,48,256]{2,1,0:T(8,128)(2,1)}) custom-call(f32[16,512]{1,0:T(8,128)S(1)} %get-tuple-element.80.back_q, bf16[16,16,512]{2,1,0:T(8,128)(2,1)S(1)} %all_to_all.45.p_parts, f32[72,512]{1,0:T(8,128)S(1)} %get-tuple-element.70.state, bf16[512,512]{1,0:T(8,128)(2,1)S(1)} %get-tuple-element.72.low, ...), custom_call_target="tpu_custom_call" | custom-call | flops 1048576 | bytes 3325952 | tf_op jit(solution)/shard_map/up/pallas_call | solution.py:385
  131.5 6.7 %all-to-all-start.7 = ((bf16[8,48,256]{2,1,0:T(8,128)(2,1)}), bf16[8,48,256]{2,1,0:T(8,128)(2,1)S(1)}, u32[]{:S(2)}, u32[]{:S(2)}) async-start(bf16[8,48,256]{2,1,0:T(8,128)(2,1)} %get-tuple-element.84), calls=%async_computation.8 | async-start | bytes 393216 | tf_op jit(solution)/shard_map/all_to_all | solution.py:396
  138.7 1.0 copy-done
  139.6 5.0 %all-to-all-done.7.parts = bf16[8,48,256]{2,1,0:T(8,128)(2,1)S(1)} async-done(((bf16[8,48,256]{2,1,0:T(8,128)(2,1)}), bf16[8,48,256]{2,1,0:T(8,128)(2,1)S(1)}, u32[]{:S(2)}, u32[]{:S(2)}) %all-to-all-start.7) | async-done | bytes 196640 | tf_op jit(solution)/shard_map/all_to_all | solution.py:396
  144.6 2.5 %final.1 = (bf16[512,512]{1,0:T(8,128)(2,1)}, bf16[512,256]{1,0:T(8,128)(2,1)}) custom-call(bf16[8,48,256]{2,1,0:T(8,128)(2,1)S(1)} %all-to-all-done.7.parts, f32[8,128]{1,0:T(8,128)S(1)} %get-tuple-element.85.side, f32[72,512]{1,0:T(8,128)S(1)} %get-tuple-element.70.state, f32[32,512]{1,0:T(8,128)S(1)} %get-tuple-element.86.back_gain, ...), custom_call_target="tpu_custom_call" | custom-call | flops 1048576 | bytes 2527232 | tf_op jit(solution)/shard_map/final/pallas_call | solution.py:385
  (19 shorter events, 1.9 us)
Async XLA Ops:
  10.1 38.9 %copy-start.2 = (f32[512]{0:T(512)S(1)}, f32[512]{0:T(512)}, u32[]{:S(2)}) copy-start(f32[512]{0:T(512)} %param.13) | copy-start | bytes 6148
  10.1 38.9 %copy-start.3 = (s32[16]{0:T(128)S(1)}, s32[16]{0:T(128)}, u32[]{:S(2)}) copy-start(s32[16]{0:T(128)} %param.16) | copy-start | bytes 196
  26.3 11.6 %collective-permute-start = (bf16[352,1024]{1,0:T(8,128)(2,1)S(1)}, bf16[352,1024]{1,0:T(8,128)(2,1)S(1)}, u32[]{:S(2)}, u32[]{:S(2)}) collective-permute-start(bf16[352,1024]{1,0:T(8,128)(2,1)S(1)} %all_gather.8.own), channel_id=1, source_target_pairs={{0,1},{1,0},{2,3},{3,2},{4,5},{5,4},{6,7},{7,6},{8,9},{9,8},{10,11... | collective-permute-start | bytes 2162696 | tf_op jit(solution)/shard_map/cond/branch_1_fun/ppermute | solution.py:428
  41.3 32.9 %copy-start.6 = (f32[512,512]{1,0:T(8,128)}, f32[512,512]{1,0:T(8,128)S(1)}, u32[]{:S(2)}) copy-start(f32[512,512]{1,0:T(8,128)S(1)} %get-tuple-element.67.hidden) | copy-start | bytes 3145732
  57.0 24.6 %all-to-all-start.2 = ((bf16[16,16,512]{2,1,0:T(8,128)(2,1)}), bf16[16,16,512]{2,1,0:T(8,128)(2,1)S(1)}, u32[]{:S(2)}, u32[]{:S(2)}) async-start(bf16[16,16,512]{2,1,0:T(8,128)(2,1)} %get-tuple-element.69), calls=%async_computation.2 | async-start | bytes 524288 | tf_op jit(solution)/shard_map/all_to_all | solution.py:396
  69.2 62.2 %reduce-scatter.2.cloned.1.call-start = ((), (), s32[]{:S(2)}) async-start(), calls=%async_computation.9 | async-start | bytes 2506752 | tf_op jit(solution)/shard_map/reduce_scatter | solution.py:519
  74.2 20.2 %copy-start.1 = (s32[8,8]{1,0:T(8,128)S(1)}, s32[8,8]{1,0:T(8,128)}, u32[]{:S(2)}) copy-start(s32[8,8]{1,0:T(8,128)} %tile_mask.1) | copy-start | bytes 772
  82.1 47.8 %copy-start.4 = (bf16[2048,512]{1,0:T(8,128)(2,1)S(1)}, bf16[2048,512]{1,0:T(8,128)(2,1)}, u32[]{:S(2)}) copy-start(bf16[2048,512]{1,0:T(8,128)(2,1)} %weight.3) | copy-start | bytes 6291460
  131.5 13.2 %all-to-all-start.7 = ((bf16[8,48,256]{2,1,0:T(8,128)(2,1)}), bf16[8,48,256]{2,1,0:T(8,128)(2,1)S(1)}, u32[]{:S(2)}, u32[]{:S(2)}) async-start(bf16[8,48,256]{2,1,0:T(8,128)(2,1)} %get-tuple-element.84), calls=%async_computation.8 | async-start | bytes 393216 | tf_op jit(solution)/shard_map/all_to_all | solution.py:396
  138.7 1.0 copy-start
Sparse Core Ops, SparseCore 0:
  82.2 37.7 reduce-scatter.1

commit v8 on v7

--- a/solution.py
+++ b/solution.py
@@ -167,17 +167,39 @@
     high = jnp.floor(where * (1.0 / 32.0))
     lane = iota((Q_DEV, 128), 1)
     where = jnp.where(lane == 0, high, jnp.where(lane == 1, where - 32.0 * high, 0.0))
-    q_pay[:, :, :WIDTH] = jnp.broadcast_to(short[None, :Q_DEV], (N_ROW, Q_DEV, WIDTH))
-    q_pay[:, :, WIDTH:] = jnp.broadcast_to(where.astype(bf16)[None], (N_ROW, Q_DEV, 128))
+    q_pay[:, :WIDTH] = short[:Q_DEV]
+    q_pay[:, WIDTH:] = where.astype(bf16)
     p_pay[...] = jnp.broadcast_to(short[None, Q_DEV:], (N_COL, P_DEV, WIDTH))
 
 
-def lift_kernel(low, pooled, weight, out):
-    out[:TOKENS, :] = dot(low[...], weight[...], ((1,), (1,))).astype(bf16)
-    out[TOKENS:, :] = dot(pooled[...], weight[...], ((1,), (1,))).astype(bf16)
-
-
-def score_kernel(q_all, p_all, state, lift, low, payload, position):
+def lift_kernel(low, pooled, weight, out, weight_here, out_here, sems):
+    blocks = [slice(n * 2 * HW_DEV, (n + 1) * 2 * HW_DEV) for n in range(NT // 2)]
+    reads = [
+        pltpu.make_async_copy(weight.at[part, :], weight_here.at[part, :], sems.at[0, n])
+        for n, part in enumerate(blocks)
+    ]
+    writes = [
+        pltpu.make_async_copy(out_here.at[:, part], out.at[:, part], sems.at[1, n])
+        for n, part in enumerate(blocks)
+    ]
+    for read in reads:
+        read.start()
+    for read, write, part in zip(reads, writes, blocks):
+        read.wait()
+        block = weight_here[part, :]
+        out_here[:TOKENS, part] = dot(low[...], block, ((1,), (1,))).astype(bf16)
+        out_here[TOKENS:, part] = dot(pooled[...], block, ((1,), (1,))).astype(bf16)
+        write.start()
+    for write in writes:
+        write.wait()
+
+
+def score_kernel(ids, *refs):
+    q_parts, (p_all, state, lift, low, payload, position, q_all, by_distance) = refs[:NX], refs[NX:]
+    for r in range(NX):
+        by_distance[r] = q_parts[r][...]
+    for x in range(NX):
+        q_all[x] = by_distance[(ids[3] - x + NX) % NX]
     order = row_order()
     q_rows = dot(order, q_all[...].reshape(ROWS, WIDTH + 128))
     position[...] = q_rows[:, WIDTH:]
@@ -481,7 +503,7 @@
         [
             ((2 * SEQS + 8, WIDTH), f32),
             ((SEQS, WIDTH), bf16),
-            ((N_ROW, Q_DEV, WIDTH + 128), bf16),
+            ((Q_DEV, WIDTH + 128), bf16),
             ((N_COL, P_DEV, WIDTH), bf16),
         ],
         (
@@ -492,28 +514,36 @@
             hidden,
         ),
     )
-    q_all = exchange(q_pay, ROW)
+    q_parts = [q_pay] + [
+        lax.ppermute(q_pay, "x", [(x, (x + r) % NX) for x in range(NX)]) for r in range(1, NX)
+    ]
     (lifted,) = call(
         lift_kernel,
         "lift",
         [((TOKENS + SEQS, NT * HW_DEV), bf16)],
         (low, lift, out_weight),
         flops=2 * TOKENS * 2048 * WIDTH,
-        grid=(NT // 2,),
-        in_specs=[
-            whole(TOKENS, WIDTH),
-            whole(SEQS, WIDTH),
-            pl.BlockSpec((2 * HW_DEV, WIDTH), lambda i: (i, 0)),
+        anywhere=(2,),
+        anywhere_out=True,
+        scratch=[
+            pltpu.VMEM((NT * HW_DEV, WIDTH), bf16),
+            pltpu.VMEM((TOKENS + SEQS, NT * HW_DEV), bf16),
+            pltpu.SemaphoreType.DMA((2, NT // 2)),
         ],
-        out_specs=[pl.BlockSpec((TOKENS + SEQS, 2 * HW_DEV), lambda i: (0, i))],
     )
     p_all = exchange(p_pay, COL)
 
-    payload, position = call(
+    payload, position, q_all = call(
         score_kernel,
         "score",
-        [((NT, SHARE, COLS + 128), f32), ((ROWS, 128), f32)],
-        (q_all, p_all, state, lift, low),
+        [
+            ((NT, SHARE, COLS + 128), f32),
+            ((ROWS, 128), f32),
+            ((N_ROW, Q_DEV, WIDTH + 128), bf16),
+        ],
+        (ids, *q_parts, p_all, state, lift, low),
+        1,
+        scratch=[pltpu.VMEM((N_ROW, Q_DEV, WIDTH + 128), bf16)],
     )
     payload, lifted = lax.optimization_barrier((payload, lifted))
     lifted = lax.psum_scatter(lifted, T, scatter_dimension=1, tiled=True)

time: 155 us -> 155 us (level)
  starting transfers between devices: 28.7 us -> 37.5 us
  waiting for transfers between devices: 14.2 us -> 6.79 us
    ppermute x0 -> x3, starting transfers between devices: none -> 10.5 us  [body(): lax.ppermute(q_pay, 'x', [(x, (x + r) % NX) for x in range(NX)])]
    all_to_all x2, waiting for transfers between devices: 12.4 us -> 4.97 us  [exchange(): return lax.all_to_all(parts, axes, 0, 0)]
    all_to_all x2, starting transfers between devices: 18.9 us -> 17.2 us  [exchange(): return lax.all_to_all(parts, axes, 0, 0)]
    all_to_all x6 -> x5, blocking collectives: 59.7 us -> 58.5 us  [exchange(): return lax.all_to_all(parts, axes, 0, 0)]
  transfers between devices with their start and end apart: 4 -> 7, of which waited for: 3 -> 2; matrix products, arithmetic and copies ran while one was open for 0% -> 0% of each run, Pallas kernels for 6% -> 5%
where the time goes in v8:
time: 155 us; the launch traced here: 154 us
  blocking collectives  74.7 us (48%)
  starting transfers between devices  37.5 us (24%)
  Pallas kernels  17.8 us (11%)
  between operations  14.9 us (10%)
  waiting for transfers between devices  6.79 us (4%)
    all_to_all x5, blocking collectives, exchange(): return lax.all_to_all(parts, axes, 0, 0)  58.5 us
    pallas_call x11, Pallas kernels, call(): pl.pallas_call(kernel, out_shape=out, **grid, compiler_params=pltpu.Compi...  17.8 us
    all_to_all x2, starting transfers between devices, exchange(): return lax.all_to_all(parts, axes, 0, 0)  17.2 us
    all_gather x1, blocking collectives, hidden_few(): own = lax.all_gather(compacted, 'yl', axis=1, tiled=True)  16.2 us
    ppermute x3, starting transfers between devices, body(): lax.ppermute(q_pay, 'x', [(x, (x + r) % NX) for x in range(NX)])  10.5 us
    ppermute x1, starting transfers between devices, hidden_few(): other = lax.ppermute(own, 'core', [(0, 1), (1, 0)])  9.8 us
    all_to_all x2, waiting for transfers between devices, exchange(): return lax.all_to_all(parts, axes, 0, 0)  4.97 us
  transfers between devices with their start and end apart: 7, of which 2 were waited for; matrix products, arithmetic and copies ran while one was open for 0% of the time, Pallas kernels for 5%

profile of v8, /device:TPU:1, one launch (start us, length us, event | category | flops | bytes accessed | tf_op | source)
XLA Modules:
  0.0 154.0 jit_solution(6117374075122328317)
XLA Ops:
  7.9 1.5 compact.1
  10.1 31.2 %conditional.1 = ((f32[512,512]{1,0:T(8,128)S(1)}, bf16[512,512]{1,0:T(8,128)(2,1)S(1)}, f32[8,8,128]{2,1,0:T(8,128)S(1)})) conditional(s32[]{:T(128)} %bitcast.5, (bf16[512,256]{1,0:T(8,128)(2,1)}, s32[4]{0:T(128)S(1)}, bf16[2048,512]{1,0:T(8,128)(2,1)}, bf16[512,512]{1,0:T(8,128)(2,1)}) %tuple.17, (bf16[352,256]{1,0:T(8,128)(2,1)S(1)}, ...), branch_computations={%region_0.0_spmd, %region_1.0_spmd} | conditional | flops 1075052544 | bytes 28614856 | solution.py:493
  10.1 16.2 %all_gather.8.own = bf16[352,1024]{1,0:T(8,128)(2,1)S(1)} all-gather(bf16[352,256]{1,0:T(8,128)(2,1)S(1)} %get-tuple-element.29), channel_id=1, replica_groups=mesh['z'=8,'x'=4,'yh'=2,'yl'=4,'core'=2] {'yl'}, dimensions={1}, use_global_device_ids=true | all-gather | bytes 901120 | tf_op jit(solution)/shard_map/cond/branch_1_fun/all_gather | solution.py:449
  26.3 9.8 %collective-permute-start = (bf16[352,1024]{1,0:T(8,128)(2,1)S(1)}, bf16[352,1024]{1,0:T(8,128)(2,1)S(1)}, u32[]{:S(2)}, u32[]{:S(2)}) collective-permute-start(bf16[352,1024]{1,0:T(8,128)(2,1)S(1)} %all_gather.8.own), channel_id=1, source_target_pairs={{0,1},{1,0},{2,3},{3,2},{4,5},{5,4},{6,7},{7,6},{8,9},{9,8},{10,11... | collective-permute-start | bytes 2162696 | tf_op jit(solution)/shard_map/cond/branch_1_fun/ppermute | solution.py:450
  36.1 1.8 %collective-permute-done.other = bf16[352,1024]{1,0:T(8,128)(2,1)S(1)} collective-permute-done((bf16[352,1024]{1,0:T(8,128)(2,1)S(1)}, bf16[352,1024]{1,0:T(8,128)(2,1)S(1)}, u32[]{:S(2)}, u32[]{:S(2)}) %collective-permute-start) | collective-permute-done | bytes 720928 | tf_op jit(solution)/shard_map/cond/branch_1_fun/ppermute | solution.py:450
  37.9 3.4 %hidden.1 = (f32[512,512]{1,0:T(8,128)S(1)}, bf16[512,512]{1,0:T(8,128)(2,1)S(1)}, f32[8,8,128]{2,1,0:T(8,128)S(1)}) custom-call(s32[4]{0:T(128)S(1)} %get-tuple-element.28.ids, bf16[352,1024]{1,0:T(8,128)(2,1)S(1)} %all_gather.8.own, bf16[352,1024]{1,0:T(8,128)(2,1)S(1)} %collective-permute-done.other, bf16[2048,512]{1,0:T(8,128)(2,1)} %get-tuple-element.30.weight, ...), custom_call_target="tpu_custom_call" | custom-call | flops 738197504 | bytes 5685264 | tf_op jit(solution)/shard_map/cond/branch_1_fun/hidden/pallas_call | solution.py:407
  41.3 7.7 %all_to_all.35.squares = f32[8,8,128]{2,1,0:T(8,128)S(1)} all-to-all(f32[8,8,128]{2,1,0:T(8,128)S(1)} %get-tuple-element.67), channel_id=1, replica_groups=mesh['z'=8,'x'=4,'yh'=2,'yl'=4,'core'=2] {'yl','core'}, dimensions={0} | all-to-all | bytes 65536 | tf_op jit(solution)/shard_map/all_to_all | solution.py:418
  49.0 1.1 pool.1
  50.1 10.7 %all-to-all-start.1 = ((bf16[16,16,512]{2,1,0:T(8,128)(2,1)}), bf16[16,16,512]{2,1,0:T(8,128)(2,1)S(1)}, u32[]{:S(2)}, u32[]{:S(2)}) async-start(bf16[16,16,512]{2,1,0:T(8,128)(2,1)} %get-tuple-element.70), calls=%async_computation.1 | async-start | bytes 524288 | tf_op jit(solution)/shard_map/all_to_all | solution.py:418
  60.9 3.1 %collective-permute-start.3 = (bf16[16,640]{1,0:T(8,128)(2,1)S(1)}, bf16[16,640]{1,0:T(8,128)(2,1)S(1)}, u32[]{:S(2)}, u32[]{:S(2)}) collective-permute-start(bf16[16,640]{1,0:T(8,128)(2,1)S(1)} %get-tuple-element.69.refs_0_), channel_id=1, source_target_pairs={{0,16},{16,32},{32,48},{48,0},{1,17},{17,33},{33,49},{49,1},{2,18}... | collective-permute-start | bytes 61448 | tf_op jit(solution)/shard_map/ppermute | solution.py:518
  64.1 4.4 %collective-permute-start.4 = (bf16[16,640]{1,0:T(8,128)(2,1)S(1)}, bf16[16,640]{1,0:T(8,128)(2,1)S(1)}, u32[]{:S(2)}, u32[]{:S(2)}) collective-permute-start(bf16[16,640]{1,0:T(8,128)(2,1)S(1)} %get-tuple-element.69.refs_0_), channel_id=1, source_target_pairs={{0,32},{16,48},{32,0},{48,16},{1,33},{17,49},{33,1},{49,17},{2,34}... | collective-permute-start | bytes 61448 | tf_op jit(solution)/shard_map/ppermute | solution.py:518
  68.4 3.1 %collective-permute-start.5 = (bf16[16,640]{1,0:T(8,128)(2,1)S(1)}, bf16[16,640]{1,0:T(8,128)(2,1)S(1)}, u32[]{:S(2)}, u32[]{:S(2)}) collective-permute-start(bf16[16,640]{1,0:T(8,128)(2,1)S(1)} %get-tuple-element.69.refs_0_), channel_id=1, source_target_pairs={{0,48},{16,0},{32,16},{48,32},{1,49},{17,1},{33,17},{49,33},{2,50}... | collective-permute-start | bytes 61448 | tf_op jit(solution)/shard_map/ppermute | solution.py:518
  71.5 4.2 %lift.1 = bf16[544,2048]{1,0:T(8,128)(2,1)} custom-call(bf16[512,512]{1,0:T(8,128)(2,1)S(1)} %get-tuple-element.73.refs_7_.low, bf16[32,512]{1,0:T(8,128)(2,1)S(1)} %get-tuple-element.72.refs_6_.pooled, bf16[2048,512]{1,0:T(8,128)(2,1)} %weight.3), custom_call_target="tpu_custom_call" | custom-call | flops 1073741824 | bytes 4882432 | tf_op jit(solution)/shard_map/lift/pallas_call | solution.py:407
  75.7 1.0 score.1
  76.7 9.9 %all_to_all.36.parts = f32[8,8,384]{2,1,0:T(8,128)S(1)} all-to-all(f32[8,8,384]{2,1,0:T(8,128)S(1)} %get-tuple-element.75), channel_id=1, replica_groups=mesh['z'=8,'x'=4,'yh'=2,'yl'=4,'core'=2] {'yl','core'}, dimensions={0} | all-to-all | bytes 196608 | tf_op jit(solution)/shard_map/all_to_all | solution.py:418
  87.4 8.8 %all_to_all.37.parts = bf16[8,16,256]{2,1,0:T(8,128)(2,1)S(1)} all-to-all(bf16[8,16,256]{2,1,0:T(8,128)(2,1)S(1)} %get-tuple-element.77), channel_id=1, replica_groups=mesh['z'=8,'x'=4,'yh'=2,'yl'=4,'core'=2] {'yl','core'}, dimensions={0} | all-to-all | bytes 131072 | tf_op jit(solution)/shard_map/all_to_all | solution.py:418
  97.1 9.0 %all_to_all.38.parts = bf16[4,48,512]{2,1,0:T(8,128)(2,1)S(1)} all-to-all(bf16[4,48,512]{2,1,0:T(8,128)(2,1)S(1)} %get-tuple-element.79), channel_id=1, replica_groups=mesh['z'=8,'x'=4,'yh'=2,'yl'=4,'core'=2] {'x'}, dimensions={0} | all-to-all | bytes 393216 | tf_op jit(solution)/shard_map/all_to_all | solution.py:418
  106.1 0.9 passage.1
  107.1 23.1 %all_to_all.39.p_parts = bf16[16,16,512]{2,1,0:T(8,128)(2,1)S(1)} all-to-all(bf16[16,16,512]{2,1,0:T(8,128)(2,1)S(1)} %get-tuple-element.83), channel_id=1, replica_groups=mesh['z'=8,'x'=4,'yh'=2,'yl'=4,'core'=2] {'z','yh'}, dimensions={0} | all-to-all | bytes 524288 | tf_op jit(solution)/shard_map/all_to_all | solution.py:418
  130.2 1.6 %up.1 = (f32[32,512]{1,0:T(8,128)S(1)}, bf16[8,48,256]{2,1,0:T(8,128)(2,1)}) custom-call(f32[16,512]{1,0:T(8,128)S(1)} %get-tuple-element.82.back_q, bf16[16,16,512]{2,1,0:T(8,128)(2,1)S(1)} %all_to_all.39.p_parts, f32[72,512]{1,0:T(8,128)S(1)} %get-tuple-element.71.refs_5_.state, bf16[512,512]{1,0:T(8,128)(2,1)S(1)} %get-tuple-element.73.refs_7_.low, ...), custom_call_target="tpu_custom_call" | custom-call | flops 1048576 | bytes 3325952 | tf_op jit(solution)/shard_map/up/pallas_call | solution.py:407
  131.8 6.4 %all-to-all-start.6 = ((bf16[8,48,256]{2,1,0:T(8,128)(2,1)}), bf16[8,48,256]{2,1,0:T(8,128)(2,1)S(1)}, u32[]{:S(2)}, u32[]{:S(2)}) async-start(bf16[8,48,256]{2,1,0:T(8,128)(2,1)} %get-tuple-element.86), calls=%async_computation.7 | async-start | bytes 393216 | tf_op jit(solution)/shard_map/all_to_all | solution.py:418
  138.7 1.0 copy-done
  139.7 5.0 %all-to-all-done.6.parts = bf16[8,48,256]{2,1,0:T(8,128)(2,1)S(1)} async-done(((bf16[8,48,256]{2,1,0:T(8,128)(2,1)}), bf16[8,48,256]{2,1,0:T(8,128)(2,1)S(1)}, u32[]{:S(2)}, u32[]{:S(2)}) %all-to-all-start.6) | async-done | bytes 196640 | tf_op jit(solution)/shard_map/all_to_all | solution.py:418
  144.7 2.5 %final.1 = (bf16[512,512]{1,0:T(8,128)(2,1)}, bf16[512,256]{1,0:T(8,128)(2,1)}) custom-call(bf16[8,48,256]{2,1,0:T(8,128)(2,1)S(1)} %all-to-all-done.6.parts, f32[8,128]{1,0:T(8,128)S(1)} %get-tuple-element.87.side, f32[72,512]{1,0:T(8,128)S(1)} %get-tuple-element.71.refs_5_.state, f32[32,512]{1,0:T(8,128)S(1)} %get-tuple-element.88.back_gain, ...), custom_call_target="tpu_custom_call" | custom-call | flops 1048576 | bytes 2527232 | tf_op jit(solution)/shard_map/final/pallas_call | solution.py:407
  (24 shorter events, 3.2 us)
Async XLA Ops:
  10.1 38.9 %copy-start.2 = (f32[512]{0:T(512)S(1)}, f32[512]{0:T(512)}, u32[]{:S(2)}) copy-start(f32[512]{0:T(512)} %param.13) | copy-start | bytes 6148
  10.1 38.9 %copy-start.3 = (s32[16]{0:T(128)S(1)}, s32[16]{0:T(128)}, u32[]{:S(2)}) copy-start(s32[16]{0:T(128)} %param.16) | copy-start | bytes 196
  26.3 11.6 %collective-permute-start = (bf16[352,1024]{1,0:T(8,128)(2,1)S(1)}, bf16[352,1024]{1,0:T(8,128)(2,1)S(1)}, u32[]{:S(2)}, u32[]{:S(2)}) collective-permute-start(bf16[352,1024]{1,0:T(8,128)(2,1)S(1)} %all_gather.8.own), channel_id=1, source_target_pairs={{0,1},{1,0},{2,3},{3,2},{4,5},{5,4},{6,7},{7,6},{8,9},{9,8},{10,11... | collective-permute-start | bytes 2162696 | tf_op jit(solution)/shard_map/cond/branch_1_fun/ppermute | solution.py:450
  41.3 19.6 %copy-start.6 = (f32[512,512]{1,0:T(8,128)}, f32[512,512]{1,0:T(8,128)S(1)}, u32[]{:S(2)}) copy-start(f32[512,512]{1,0:T(8,128)S(1)} %get-tuple-element.68.hidden) | copy-start | bytes 3145732
  50.1 25.6 %all-to-all-start.1 = ((bf16[16,16,512]{2,1,0:T(8,128)(2,1)}), bf16[16,16,512]{2,1,0:T(8,128)(2,1)S(1)}, u32[]{:S(2)}, u32[]{:S(2)}) async-start(bf16[16,16,512]{2,1,0:T(8,128)(2,1)} %get-tuple-element.70), calls=%async_computation.1 | async-start | bytes 524288 | tf_op jit(solution)/shard_map/all_to_all | solution.py:418
  60.9 70.9 %reduce-scatter.2.cloned.1.call-start = ((), (), s32[]{:S(2)}) async-start(), calls=%async_computation.8 | async-start | bytes 2506752 | tf_op jit(solution)/shard_map/reduce_scatter | solution.py:549
  60.9 14.7 %collective-permute-start.3 = (bf16[16,640]{1,0:T(8,128)(2,1)S(1)}, bf16[16,640]{1,0:T(8,128)(2,1)S(1)}, u32[]{:S(2)}, u32[]{:S(2)}) collective-permute-start(bf16[16,640]{1,0:T(8,128)(2,1)S(1)} %get-tuple-element.69.refs_0_), channel_id=1, source_target_pairs={{0,16},{16,32},{32,48},{48,0},{1,17},{17,33},{33,49},{49,1},{2,18}... | collective-permute-start | bytes 61448 | tf_op jit(solution)/shard_map/ppermute | solution.py:518
  64.1 11.6 %collective-permute-start.4 = (bf16[16,640]{1,0:T(8,128)(2,1)S(1)}, bf16[16,640]{1,0:T(8,128)(2,1)S(1)}, u32[]{:S(2)}, u32[]{:S(2)}) collective-permute-start(bf16[16,640]{1,0:T(8,128)(2,1)S(1)} %get-tuple-element.69.refs_0_), channel_id=1, source_target_pairs={{0,32},{16,48},{32,0},{48,16},{1,33},{17,49},{33,1},{49,17},{2,34}... | collective-permute-start | bytes 61448 | tf_op jit(solution)/shard_map/ppermute | solution.py:518
  68.4 7.3 %collective-permute-start.5 = (bf16[16,640]{1,0:T(8,128)(2,1)S(1)}, bf16[16,640]{1,0:T(8,128)(2,1)S(1)}, u32[]{:S(2)}, u32[]{:S(2)}) collective-permute-start(bf16[16,640]{1,0:T(8,128)(2,1)S(1)} %get-tuple-element.69.refs_0_), channel_id=1, source_target_pairs={{0,48},{16,0},{32,16},{48,32},{1,49},{17,1},{33,17},{49,33},{2,50}... | collective-permute-start | bytes 61448 | tf_op jit(solution)/shard_map/ppermute | solution.py:518
  75.7 11.0 %copy-start.1 = (s32[8,8]{1,0:T(8,128)S(1)}, s32[8,8]{1,0:T(8,128)}, u32[]{:S(2)}) copy-start(s32[8,8]{1,0:T(8,128)} %tile_mask.1) | copy-start | bytes 772
  76.7 53.5 %copy-start.4 = (bf16[2048,512]{1,0:T(8,128)(2,1)S(1)}, bf16[2048,512]{1,0:T(8,128)(2,1)}, u32[]{:S(2)}) copy-start(bf16[2048,512]{1,0:T(8,128)(2,1)} %weight.3) | copy-start | bytes 6291460
  131.8 12.9 %all-to-all-start.6 = ((bf16[8,48,256]{2,1,0:T(8,128)(2,1)}), bf16[8,48,256]{2,1,0:T(8,128)(2,1)S(1)}, u32[]{:S(2)}, u32[]{:S(2)}) async-start(bf16[8,48,256]{2,1,0:T(8,128)(2,1)} %get-tuple-element.86), calls=%async_computation.7 | async-start | bytes 393216 | tf_op jit(solution)/shard_map/all_to_all | solution.py:418
  138.7 1.0 copy-start
Sparse Core Ops, SparseCore 0:
  76.9 42.3 reduce-scatter.1
